TPU v7x, 32 devices: a whole 2x2x4 slice. The times are simulated.
32 devices in a mesh: chan: 4 (over y, x), tm: 8 (over z, core).
Axes of the slice: x: 2, y: 2, z: 4, core: 2. Of those that a mesh axis runs over, the one named last changes fastest.
Arguments:
- records: bfloat16 [8, 1536, 1536], P('tm', 'chan')
- partners: int32 [4, 3], P('chan'), may hold values from 0 to 3, as said below
- counts: int32 [4], P('chan'), may hold values from 1 to 3, as said below
- sources: int32 [4, 2], P('chan'), may hold values from 0 to 383, as said below
Outputs:
- xcorr: float32 [4, 384, 3, 2, 384], P('chan', 'tm')
Inputs may be any that keep to these rules, and one draw needn't show every extreme that they name: `partners`: each row holds 3 different blocks. `counts`: some block has all 3 slots live. `sources`: each row holds 2 different channels.
All inputs are finite; a program needn't handle non-finite values.
Results may differ from a plain program's by a relative error of at most 0.008.
Values may be sent and summed in bfloat16 or wider, within the bound.
No kernel may reach another device: no remote copies, remote signals or barrier semaphores. Data moves between devices by JAX's collectives and lax.ppermute only.
A program may use at most 64 MiB of HBM per device.

v0:
```python
import math

import jax
import jax.numpy as jnp
from jax import lax
from jax.sharding import PartitionSpec as P

L = 1536
F = 320
HL = 192
SMOOTH = 32


def dft_table(length, bins):
    sample_index = jnp.arange(length, dtype=jnp.int32)[:, None]
    bin_index = jnp.arange(bins, dtype=jnp.int32)[None, :] + 1
    phase_index = sample_index * bin_index % length
    angle = phase_index.astype(jnp.float32) * (2.0 * math.pi / length)
    return jnp.concatenate([jnp.cos(angle), -jnp.sin(angle)], axis=1).astype(jnp.bfloat16)


def lag_table(length, bins, half):
    bin_index = jnp.arange(bins, dtype=jnp.int32)[:, None] + 1
    lag_index = jnp.arange(2 * half, dtype=jnp.int32)[None, :] - half
    phase_index = jnp.mod(bin_index * lag_index, length)
    angle = phase_index.astype(jnp.float32) * (2.0 * math.pi / length)
    return jnp.concatenate([jnp.cos(angle), -jnp.sin(angle)], axis=0)


def band_table(bins, half):
    input_bin = jnp.arange(bins, dtype=jnp.int32)[:, None]
    output_bin = jnp.arange(bins, dtype=jnp.int32)[None, :]
    centre = jnp.clip(output_bin, half, bins - 1 - half)
    return (jnp.abs(input_bin - centre) <= half).astype(jnp.float32)


def whiten(block_records):
    windows, channels, length = block_records.shape
    signal = block_records.astype(jnp.float32)
    signal = signal - jnp.mean(signal, axis=-1, keepdims=True)
    demeaned = signal.astype(jnp.bfloat16).reshape(windows * channels, length)
    spectrum = jnp.dot(demeaned, dft_table(L, F), preferred_element_type=jnp.float32)
    real_part = spectrum[:, :F]
    imag_part = spectrum[:, F:]
    amplitude = jnp.sqrt(real_part * real_part + imag_part * imag_part)
    smooth = jnp.dot(amplitude, band_table(F, SMOOTH), precision=lax.Precision.HIGHEST) / (
        2 * SMOOTH + 1
    )
    factor = 1.0 / (smooth + 1e-06)
    whitened = jnp.concatenate([real_part * factor, imag_part * factor], axis=1)
    return whitened.astype(jnp.bfloat16).reshape(windows, channels, 2 * F)


def cross_terms(source_spec, partner_white):
    src_real = source_spec[..., :F]
    src_imag = source_spec[..., F:]
    rec_real = partner_white[..., :F]
    rec_imag = partner_white[..., F:]
    cross_real = jnp.einsum(
        "wsf,pwcf->cpsf", src_real, rec_real, preferred_element_type=jnp.float32
    ) + jnp.einsum("wsf,pwcf->cpsf", src_imag, rec_imag, preferred_element_type=jnp.float32)
    cross_imag = jnp.einsum(
        "wsf,pwcf->cpsf", src_real, rec_imag, preferred_element_type=jnp.float32
    ) - jnp.einsum("wsf,pwcf->cpsf", src_imag, rec_real, preferred_element_type=jnp.float32)
    return jnp.concatenate([cross_real, cross_imag], axis=-1)


def local(records, partners, counts, sources):
    windows, channels, length = records.shape
    slots = partners.shape[1]
    white = whiten(records)
    partner_ids = partners[0]
    live = jnp.arange(slots, dtype=jnp.int32) < counts[0]
    piece = lax.all_gather(white, "chan", axis=1, tiled=True)
    blocks_here = piece.shape[1] // channels
    block_ids = jnp.arange(blocks_here, dtype=jnp.int32)
    matches = ((block_ids[None, :] == partner_ids[:, None]) & live[:, None]).astype(jnp.bfloat16)
    shaped = piece.reshape(windows, blocks_here, channels, piece.shape[2])
    partner_white = jnp.einsum(
        "pj,wjcf->pwcf", matches, shaped, preferred_element_type=jnp.float32
    ).astype(jnp.bfloat16)
    picker = (jnp.arange(channels, dtype=jnp.int32)[None, :] == sources[0][:, None]).astype(
        jnp.bfloat16
    )
    source_spec = jnp.einsum(
        "sc,wcf->wsf", picker, white, preferred_element_type=jnp.float32
    ).astype(jnp.bfloat16)
    sources_count = source_spec.shape[1]
    inverse = lag_table(L, F, HL)
    scale = 1.0 / math.sqrt(F * windows * lax.axis_size("tm"))
    share_rows = channels // lax.axis_size("tm")
    stacked = cross_terms(source_spec, partner_white)
    lagged = jnp.dot(
        stacked.reshape(share_rows * lax.axis_size("tm") * slots * sources_count, 2 * F),
        inverse,
        precision=lax.Precision.HIGHEST,
    )
    result = lax.psum_scatter(
        lagged.reshape(share_rows * lax.axis_size("tm"), slots, sources_count, 2 * HL) * scale,
        "tm",
        scatter_dimension=0,
        tiled=True,
    )
    return result[None]


def solution(mesh):
    return jax.shard_map(
        local,
        mesh=mesh,
        in_specs=(P("tm", "chan", None), P("chan", None), P("chan"), P("chan", None)),
        out_specs=P("chan", "tm", None, None, None),
        check_vma=False,
    )
```

profile of v0, /device:TPU:0, one launch (start us, length us, event | category | flops | bytes accessed | tf_op | source)
XLA Modules:
  0.0 128.0 jit_solution(3411525161726095171)
XLA Ops:
  6.5 0.0 all-gather.2.cloned.1.call-start
  6.5 10.0 %cosine_convert_fusion = (bf16[1536,320]{1,0:T(8,128)(2,1)S(1)}, bf16[1536,320]{1,0:T(8,128)(2,1)S(1)}) fusion(s32[320]{0:T(512)S(1)} %iota_add_fusion.1), kind=kLoop, calls=%fused_computation.15 | loop fusion | flops 5898240 | bytes 1967360 | tf_op jit(solution)/shard_map/convert.30
  16.6 0.0 copy-done
  16.6 0.2 convert_reduce_fusion
  16.8 1.2 fusion.10
  18.0 0.0 copy-start.2
  18.0 1.1 multiply_convert_fusion.1
  19.1 0.0 copy-start.1
  19.1 0.9 pad_maximum_fusion
  20.0 0.0 all-gather.2.cloned.1.call-update
  20.0 0.0 reduce-scatter.2.cloned.1.call-start
  20.8 0.3 fusion.26
  21.0 0.1 convert_bitcast_fusion.4
  21.1 2.1 %fusion.42 = (f32[320,384]{1,0:T(8,128)S(1)}, f32[320,384]{1,0:T(8,128)S(1)}) fusion(s32[384]{0:T(512)S(1)} %iota_add_fusion, s32[320]{0:T(512)S(1)} %iota_add_fusion.1), kind=kLoop, calls=%fused_computation.59 | loop fusion | flops 1228800 | bytes 985856 | tf_op jit(solution)/shard_map/cos | solution.py:27
  23.2 33.9 %all-gather.2.cloned.1.call-done = bf16[1,1536,640]{2,1,0:T(8,128)(2,1)} async-done(((bf16[1,384,640]{2,1,0:T(8,128)(2,1)}), bf16[1,1536,640]{2,1,0:T(8,128)(2,1)}) %all-gather.2.cloned.1.call-update) | async-done | bytes 1966096 | tf_op jit(solution)/shard_map/all_gather | solution.py:74
  57.1 3.2 %convert_bitcast_fusion.2 = bf16[3,1,384,640]{3,0,2,1:T(4,128)(2,1)S(1)} fusion(bf16[4,384,640]{2,1,0:T(8,128)(2,1)} %bitcast.57, s32[3]{0:T(128)S(1)} %bitcast.61, pred[3]{0:T(512)(128)(4,1)S(1)} %iota_compare_fusion.1), kind=kOutput, calls=%fused_computation.26 | convolution fusion | flops 6635544 | bytes 3440655 | tf_op jit(solution)/shard_map/pj,wjcf->pwcf/dot_general | solution.py:79
  60.3 1.2 convert_bitcast_fusion.1
  61.5 0.1 copy.7
  61.6 0.1 copy.8
  61.8 0.9 add_bitcast_fusion
  62.7 12.5 %fusion.16 = f32[384,3,2,384]{3,0,2,1:T(8,128)} fusion(f32[384,3,2,320]{3,0,2,1:T(8,128)S(1)} %get-tuple-element.6, f32[384,3,2,320]{3,0,2,1:T(8,128)S(1)} %get-tuple-element.5, f32[320,384]{1,0:T(8,128)S(1)} %get-tuple-element.12, f32[320,384]{1,0:T(8,128)S(1)} %get-tuple-element.11), kind=kOutput, calls=%fused_computation.27 | convolution fusion | flops 6797377536 | bytes 10420224 | tf_op jit(solution)/shard_map/dot_general | solution.py:93
  75.1 0.0 reduce-scatter.2.cloned.1.call-update
  75.1 44.0 %reduce-scatter.2.cloned.1.call-done = f32[48,3,2,384]{3,0,2,1:T(8,128)} async-done(((f32[384,3,2,384]{3,0,2,1:T(8,128)}), f32[48,3,2,384]{3,0,2,1:T(8,128)}) %reduce-scatter.2.cloned.1.call-update) | async-done | bytes 442384 | tf_op jit(solution)/shard_map/reduce_scatter | solution.py:98
  119.1 2.0 %copy.9 = f32[1,48,3,2,384]{4,3,2,1,0:T(2,128)} copy(f32[1,48,3,2,384]{4,1,3,2,0:T(8,128)} %bitcast.58) | data formatting | bytes 884736 | tf_op jit(solution)/shard_map/broadcast_in_dim | solution.py:104
  (8 shorter events, 0.0 us)
Async XLA Ops:
  6.5 10.0 %copy-start = (bf16[1,384,1536]{2,1,0:T(8,128)(2,1)S(1)}, bf16[1,384,1536]{2,1,0:T(8,128)(2,1)}, u32[]{:S(2)}) copy-start(bf16[1,384,1536]{2,1,0:T(8,128)(2,1)} %param.4) | copy-start | bytes 3538948
  6.5 50.6 %all-gather.2.cloned.1.call-start = ((), (), s32[]{:S(2)}) async-start(), calls=%async_computation.1 | async-start | bytes 2457600 | tf_op jit(solution)/shard_map/all_gather | solution.py:74
  18.0 2.8 %copy-start.2 = (s32[1,2]{1,0:T(1,128)S(1)}, s32[1,2]{1,0:T(1,128)}, u32[]{:S(2)}) copy-start(s32[1,2]{1,0:T(1,128)} %param.7) | copy-start | bytes 28
  19.1 38.1 %copy-start.1 = (s32[1,3]{1,0:T(1,128)S(1)}, s32[1,3]{1,0:T(1,128)}, u32[]{:S(2)}) copy-start(s32[1,3]{1,0:T(1,128)} %param.5) | copy-start | bytes 40
  20.0 99.1 %reduce-scatter.2.cloned.1.call-start = ((), (), s32[]{:S(2)}) async-start(), calls=%async_computation.2 | async-start | bytes 3981312 | tf_op jit(solution)/shard_map/reduce_scatter | solution.py:98
Sparse Core Ops, SparseCore 0:
  20.2 36.9 all-gather.1
  75.3 43.8 reduce-scatter.1
where the time goes:
time: 128 us
  waiting for transfers between devices  77.9 us (61%)
  matrix products  18.2 us (14%)
  other arithmetic  15.4 us (12%)
  between operations  14.2 us (11%)
  local copies, waits for them, and re-layouts  2.25 us (2%)
    reduce_scatter x1, waiting for transfers between devices, local(): lax.psum_scatter(lagged.reshape(share_rows * lax.axis_size('tm'), slots,...  44 us
    all_gather x1, waiting for transfers between devices, local(): piece = lax.all_gather(white, 'chan', axis=1, tiled=True)  33.9 us
    dot_general x1, matrix products, local(): jnp.dot(stacked.reshape(share_rows * lax.axis_size('tm') * slots * source...  12.5 us
    another operation x3, other arithmetic  11.2 us
    dot_general x1, matrix products, local(): jnp.einsum('pj,wjcf->pwcf', matches, shaped, preferred_element_type=jnp.f...  3.21 us
  transfers between devices with their start and end apart: 2, of which 2 were waited for; matrix products, arithmetic and copies ran while one was open for 2% of the time, Pallas kernels for 0%

commit v1 on v0

v1 whole, which is shorter than its diff:
```python
import functools
import math

import jax
import jax.numpy as jnp
import ml_dtypes
import numpy as np
from jax import lax
from jax.experimental import pallas as pl
from jax.experimental.pallas import tpu as pltpu
from jax.sharding import PartitionSpec as P

L = 1536
F = 320
HL = 192
SMOOTH = 32
LANES = 128
MAIN = F // LANES * LANES
TAIL = F - MAIN
WIDTH = 2 * F
SRC_ROWS = 8
F32 = jnp.float32
BF16 = jnp.bfloat16


def dft_table():
    n = np.arange(L)[:, None]
    k = np.arange(F)[None, :] + 1
    angle = (n * k % L).astype(np.float32) * np.float32(2.0 * math.pi / L)
    c, s = np.cos(angle), -np.sin(angle)
    table = np.concatenate([c[:, :MAIN], s[:, :MAIN], c[:, MAIN:], s[:, MAIN:]], axis=1)
    return table.astype(ml_dtypes.bfloat16)


def band_table():
    bins = np.concatenate([np.arange(MAIN), np.arange(MAIN, F), np.arange(MAIN, F)])
    centre = np.clip(bins, SMOOTH, F - 1 - SMOOTH)
    band = np.abs(bins[:, None] - centre[None, :]) <= SMOOTH
    band[F:] = False
    return band.astype(ml_dtypes.bfloat16)


def lag_tables(scale):
    k = np.arange(F)[:, None] + 1
    j = np.arange(2 * HL)[None, :] - HL
    angle = np.mod(k * j, L).astype(np.float32) * np.float32(2.0 * math.pi / L)
    c, s = np.cos(angle) * np.float32(scale), -np.sin(angle) * np.float32(scale)
    table = np.concatenate([c[:MAIN], s[:MAIN], c[MAIN:], c[MAIN:], s[MAIN:], -s[MAIN:]], axis=0)
    high = table.astype(ml_dtypes.bfloat16)
    low = (table - high.astype(np.float32)).astype(ml_dtypes.bfloat16)
    return high, low


def whiten_kernel(chunks, shared, zs, src_ref, rec_ref, tab_ref, band_ref, *rest):
    outs, white = rest[:-1], rest[-1]
    rows = rec_ref.shape[0]
    signal = rec_ref[...].astype(F32)
    signal = signal - jnp.sum(signal, axis=1, keepdims=True) * (1.0 / L)
    spec = jnp.dot(signal.astype(BF16), tab_ref[...], preferred_element_type=F32)
    re, im, tail = spec[:, :MAIN], spec[:, MAIN : 2 * MAIN], spec[:, 2 * MAIN :]
    tail_sq = tail * tail
    amp = jnp.sqrt(
        jnp.concatenate([re * re + im * im, tail_sq + pltpu.roll(tail_sq, TAIL, 1)], axis=1)
    )
    high = amp.astype(BF16)
    low = (amp - high.astype(F32)).astype(BF16)
    total = jnp.dot(high, band_ref[...], preferred_element_type=F32) + jnp.dot(
        low, band_ref[...], preferred_element_type=F32
    )
    factor = 1.0 / (total * (1.0 / (2 * SMOOTH + 1)) + 1e-06)
    white[:, :MAIN] = re * factor[:, :MAIN]
    white[:, MAIN : 2 * MAIN] = im * factor[:, :MAIN]
    white[:, 2 * MAIN :] = tail * factor[:, MAIN:]

    place = lax.axis_index("tm")
    z, core = place // 2, lax.rem(place, 2)
    row_id = lax.broadcasted_iota(jnp.int32, (SRC_ROWS, WIDTH), 0)
    source = jnp.zeros((SRC_ROWS, WIDTH), F32)
    for s in range(src_ref.shape[1]):
        source = jnp.where(row_id == s, white[pl.ds(src_ref[0, s], 1), :], source)

    def share(d, q, start, size):
        owner = jnp.bitwise_xor(z, d) * 2 + jnp.bitwise_xor(core, q)
        return white[pl.ds(pl.multiple_of(owner * shared + start, 8), size), :]

    first, second = chunks
    for d in range(zs):
        block = [share(d, 0, 0, first), share(d, 1, 0, first), source]
        outs[d][...] = jnp.concatenate(block, axis=0).astype(BF16)
        for q in range(2):
            outs[zs + 2 * d + q][...] = share(d, q, first, second).astype(BF16)


def pack_kernel(sources, first, *refs):
    ins, out = refs[:-1], refs[-1]
    parts = [ref[...].astype(F32)[2 * first : 2 * first + sources] for ref in ins]
    out[...] = jnp.concatenate(parts, axis=0).astype(BF16)


def cross_kernel(count, windows, sources, parts, *refs):
    src_refs = refs[:count]
    rec_refs = refs[count : count + windows]
    high_ref, low_ref = refs[count + windows : count + windows + 2]
    outs = refs[count + windows + 2 : 2 * count + windows + 2]
    rec, src, stack = refs[2 * count + windows + 2 :]
    size = parts[0][1]
    for w in range(windows):
        start = parts[w][0]
        rec[pl.ds(w * size, size), :WIDTH] = rec_refs[w][...].astype(F32)[start : start + size]
        part = rec[pl.ds(w * size, size), 2 * MAIN : WIDTH]
        rec[pl.ds(w * size, size), WIDTH:] = pltpu.roll(part, TAIL, 1)
    per = windows * sources
    for b in range(count):
        src[pl.ds(b * per, per), :] = src_refs[b][...].astype(F32)
    step = 16 if size % 16 == 0 else 8
    for b in range(count):
        for s in range(sources):
            for g in range(0, size, step):
                totals = [0.0] * 4
                for w in range(windows):
                    a = src[pl.ds(b * per + w * sources + s, 1), :]
                    r = rec[pl.ds(w * size + g, step), :]
                    a_re, a_im, a_tail = a[:, :MAIN], a[:, MAIN : 2 * MAIN], a[:, 2 * MAIN :]
                    r_re, r_im = r[:, :MAIN], r[:, MAIN : 2 * MAIN]
                    totals[0] += a_re * r_re + a_im * r_im
                    totals[1] += a_re * r_im - a_im * r_re
                    totals[2] += a_tail * r[:, 2 * MAIN : WIDTH]
                    totals[3] += a_tail * r[:, WIDTH:]
                stack[pl.ds((b * sources + s) * size + g, step), :] = jnp.concatenate(totals, axis=1)
    cross = stack[...]
    high = cross.astype(BF16)
    low = (cross - high.astype(F32)).astype(BF16)
    lag_high, lag_low = high_ref[...], low_ref[...]
    lagged = (
        jnp.dot(high, lag_high, preferred_element_type=F32)
        + jnp.dot(low, lag_high, preferred_element_type=F32)
        + jnp.dot(high, lag_low, preferred_element_type=F32)
    )
    for b in range(count):
        outs[b][...] = lagged[b * sources * size : (b + 1) * sources * size].astype(BF16)


def finish_kernel(count, chunks, sources, partner_ref, counts_ref, *refs):
    ins, out = refs[:-1], refs[-1]
    me = lax.axis_index("chan")
    slots = partner_ref.shape[1]
    start = 0
    for i, size in enumerate(chunks):
        for p in range(slots):
            wanted = jnp.bitwise_xor(partner_ref[0, p], me)
            wanted = jnp.where(p < counts_ref[0], wanted, -1)
            value = jnp.zeros((sources * size, 2 * HL), F32)
            for e in range(count):
                value = jnp.where(wanted == e, ins[i * count + e][...].astype(F32), value)
            for s in range(sources):
                out[pl.ds(start, size), p, s, :] = value[s * size : (s + 1) * size]
        start += size


def call(kernel, out_shape, scratch, args, smem=0):
    specs = [pl.BlockSpec(memory_space=pltpu.SMEM)] * smem
    specs += [pl.BlockSpec(memory_space=pltpu.VMEM)] * (len(args) - smem)
    return pl.pallas_call(
        kernel,
        out_shape=out_shape,
        in_specs=specs,
        out_specs=jax.tree.map(lambda _: pl.BlockSpec(memory_space=pltpu.VMEM), out_shape),
        scratch_shapes=scratch,
        compiler_params=pltpu.CompilerParams(vmem_limit_bytes=40 * 1024 * 1024),
    )(*args)


def swap(value, axis, size, distance):
    return lax.ppermute(value, axis, [(i, i ^ distance) for i in range(size)])


def local(chans, tms, records, partners, counts, sources):
    channels = records.shape[1]
    picked = sources.shape[1]
    shared = channels // tms
    zs = tms // 2
    first = max(8, shared // 3 // 8 * 8)
    chunks = (first, shared - first)
    second = chunks[1]
    shape = jax.ShapeDtypeStruct
    high, low = lag_tables(1.0 / math.sqrt(F * tms))

    sent = call(
        functools.partial(whiten_kernel, chunks, shared, zs),
        [shape((2 * first + SRC_ROWS, WIDTH), BF16)] * zs + [shape((second, WIDTH), BF16)] * tms,
        [pltpu.VMEM((channels, WIDTH), F32)],
        (sources, records[0], jnp.asarray(dft_table()), jnp.asarray(band_table())),
        smem=1,
    )
    sent_one, sent_two = sent[:zs], sent[zs:]
    one = [sent_one[0]] + [None] * (zs - 1)
    for d in sorted(range(1, zs), key=lambda d: d == 1):
        one[d] = swap(sent_one[d], "tm", tms, 2 * d)
    two = [sent_two[0]] + [swap(sent_two[d], "tm", tms, d) for d in range(1, tms)]
    other = [swap(value, "tm", tms, 1) for value in one]

    own = call(
        functools.partial(pack_kernel, picked, first),
        shape((tms * picked, WIDTH), BF16),
        [],
        one + other,
    )
    spectra = [own] + [swap(own, "chan", chans, e) for e in range(1, chans)]

    def cross(receivers, parts):
        size = parts[0][1]
        return call(
            functools.partial(cross_kernel, chans, tms, picked, parts),
            [shape((picked * size, 2 * HL), BF16)] * chans,
            [
                pltpu.VMEM((tms * size, WIDTH + LANES), F32),
                pltpu.VMEM((chans * tms * picked, WIDTH), F32),
                pltpu.VMEM((chans * picked * size, WIDTH + LANES), F32),
            ],
            (*spectra, *receivers, jnp.asarray(high), jnp.asarray(low)),
        )

    done_one = cross(one + other, [(0, first)] * zs + [(first, first)] * zs)
    order = list(range(0, tms, 2)) + list(range(1, tms, 2))
    done_two = cross([two[d] for d in order], [(0, second)] * tms)
    arrived = []
    for done in (done_one, done_two):
        arrived += [done[0]] + [swap(done[e], "chan", chans, e) for e in range(1, chans)]
    result = call(
        functools.partial(finish_kernel, chans, chunks, picked),
        shape((shared, partners.shape[1], picked, 2 * HL), F32),
        [],
        (partners, counts, *arrived),
        smem=2,
    )
    return result[None]


def solution(mesh):
    sizes = dict(mesh.shape)
    return jax.shard_map(
        functools.partial(local, sizes["chan"], sizes["tm"]),
        mesh=mesh,
        in_specs=(P("tm", "chan", None), P("chan", None), P("chan"), P("chan", None)),
        out_specs=P("chan", "tm", None, None, None),
        check_vma=False,
    )
```

time: 128 us -> 47 us (0.37)
  waiting for transfers between devices: 77.9 us -> 8.61 us
  starting transfers between devices: 0.04 us -> 26.2 us
  matrix products: 18.2 us -> 0 us
  other arithmetic: 15.4 us -> 0 us
  between operations: 14.2 us -> 0.76 us
  Pallas kernels: 0 us -> 6.69 us
  local copies, waits for them, and re-layouts: 2.25 us -> 4.54 us
    reduce_scatter x1 -> x0, waiting for transfers between devices: 44 us -> none  [local(): lax.psum_scatter(lagged.reshape(share_rows * lax.axis_size('tm'), slots,...]
    all_gather x1 -> x0, waiting for transfers between devices: 33.9 us -> none  [local(): piece = lax.all_gather(white, 'chan', axis=1, tiled=True)]
    ppermute x0 -> x23, starting transfers between devices: none -> 26.2 us  [swap(): return lax.ppermute(value, axis, [(i, i ^ distance) for i in range(size)])]
    dot_general x5 -> x0, matrix products: 18.2 us -> none  [the longest x1 12.5 us: local(): jnp.dot(stacked.reshape(share_rows * lax.axis_size('tm') * slots * source...]
    another operation x3 -> x0, other arithmetic: 11.2 us -> none
    ppermute x0 -> x23, waiting for transfers between devices: none -> 8.61 us  [swap(): return lax.ppermute(value, axis, [(i, i ^ distance) for i in range(size)])]
    pallas_call x0 -> x5, Pallas kernels: none -> 6.69 us  [call(): pl.pallas_call(kernel, out_shape=out_shape, in_specs=specs, out_specs=jax...]
    unnamed x6 -> x14, local copies, waits for them, and re-layouts: 0.02 us -> 4.54 us
  transfers between devices with their start and end apart: 2 -> 23, of which waited for: 2 -> 6; matrix products, arithmetic and copies ran while one was open for 2% -> 0% of each run, Pallas kernels for 0% -> 5%
where the time goes in v1:
time: 47 us; the launch traced here: 46.8 us
  starting transfers between devices  26.2 us (56%)
  waiting for transfers between devices  8.61 us (18%)
  Pallas kernels  6.69 us (14%)
  local copies, waits for them, and re-layouts  4.54 us (10%)
  between operations  0.76 us (2%)
    ppermute x23, starting transfers between devices, swap(): return lax.ppermute(value, axis, [(i, i ^ distance) for i in range(size)])  26.2 us
    ppermute x23, waiting for transfers between devices, swap(): return lax.ppermute(value, axis, [(i, i ^ distance) for i in range(size)])  8.61 us
    pallas_call x5, Pallas kernels, call(): pl.pallas_call(kernel, out_shape=out_shape, in_specs=specs, out_specs=jax...  6.69 us
    unnamed x14, local copies, waits for them, and re-layouts  4.54 us
  transfers between devices with their start and end apart: 23, of which 6 were waited for; matrix products, arithmetic and copies ran while one was open for 0% of the time, Pallas kernels for 5%

profile of v1, /device:TPU:0, one launch (start us, length us, event | category | flops | bytes accessed | tf_op | source)
XLA Modules:
  0.0 46.8 jit_solution(5075824807279232638)
XLA Ops:
  0.0 1.6 %copy-done.2 = bf16[1536,640]{1,0:T(8,128)(2,1)S(1)} copy-done((bf16[1536,640]{1,0:T(8,128)(2,1)S(1)}, bf16[1536,640]{1,0:T(8,128)(2,1)}, u32[]{:S(2)}) %copy-start.2) | copy-done | bytes 1966104
  1.6 1.3 %copy-done.3 = bf16[1,384,1536]{2,1,0:T(8,128)(2,1)S(1)} copy-done((bf16[1,384,1536]{2,1,0:T(8,128)(2,1)S(1)}, bf16[1,384,1536]{2,1,0:T(8,128)(2,1)}, u32[]{:S(2)}) %copy-start.3) | copy-done | bytes 1179672
  2.9 1.0 %copy-done.4 = bf16[384,384]{1,0:T(8,128)(2,1)S(1)} copy-done((bf16[384,384]{1,0:T(8,128)(2,1)S(1)}, bf16[384,384]{1,0:T(8,128)(2,1)}, u32[]{:S(2)}) %copy-start.4) | copy-done | bytes 294936
  3.9 0.7 %copy-done.5 = s32[1,2]{1,0:T(1,128)S(1)} copy-done((s32[1,2]{1,0:T(1,128)S(1)}, s32[1,2]{1,0:T(1,128)}, u32[]{:S(2)}) %copy-start.5) | copy-done | bytes 32
  4.5 2.8 %shard_map.82 = (bf16[40,640]{1,0:T(8,128)(2,1)S(1)}, bf16[40,640]{1,0:T(8,128)(2,1)S(1)}, bf16[40,640]{1,0:T(8,128)(2,1)S(1)}, bf16[40,640]{1,0:T(8,128)(2,1)S(...) custom-call(s32[1,2]{1,0:T(1,128)S(1)} %copy-done.5, ...), custom_call_target="tpu_custom_call" | custom-call | tf_op jit(solution)/shard_map/pallas_call | solution.py:163
  7.4 3.1 %collective-permute-start = (bf16[40,640]{1,0:T(8,128)(2,1)S(1)}, bf16[40,640]{1,0:T(8,128)(2,1)S(1)}, u32[]{:S(2)}, u32[]{:S(2)}) collective-permute-start(bf16[40,640]{1,0:T(8,128)(2,1)S(1)} %get-tuple-element.26), channel_id=1, source_target_pairs={{0,2},{1,3},{2,0},{3,1},{4,6},{5,7},{6,4},{7,5},{8,10},{9,11},{10,... | collective-permute-start | bytes 153608 | tf_op jit(solution)/shard_map/ppermute | solution.py:174
  10.5 2.6 %collective-permute-start.1 = (bf16[40,640]{1,0:T(8,128)(2,1)S(1)}, bf16[40,640]{1,0:T(8,128)(2,1)S(1)}, u32[]{:S(2)}, u32[]{:S(2)}) collective-permute-start(bf16[40,640]{1,0:T(8,128)(2,1)S(1)} %get-tuple-element.27), channel_id=1, source_target_pairs={{0,4},{1,5},{2,6},{3,7},{4,0},{5,1},{6,2},{7,3},{8,12},{9,13},{10,... | collective-permute-start | bytes 153608 | tf_op jit(solution)/shard_map/ppermute | solution.py:174
  13.6 2.9 %collective-permute-done.1.refs_2_.refs_6_ = bf16[40,640]{1,0:T(8,128)(2,1)S(1)} collective-permute-done((bf16[40,640]{1,0:T(8,128)(2,1)S(1)}, bf16[40,640]{1,0:T(8,128)(2,1)S(1)}, u32[]{:S(2)}, u32[]{:S(2)}) %collective-permute-start.1) | collective-permute-done | bytes 51232 | tf_op jit(solution)/shard_map/ppermute | solution.py:174
  16.5 2.5 %collective-permute-done.2.refs_3_.refs_7_ = bf16[40,640]{1,0:T(8,128)(2,1)S(1)} collective-permute-done((bf16[40,640]{1,0:T(8,128)(2,1)S(1)}, bf16[40,640]{1,0:T(8,128)(2,1)S(1)}, u32[]{:S(2)}, u32[]{:S(2)}) %collective-permute-start.2) | collective-permute-done | bytes 51232 | tf_op jit(solution)/shard_map/ppermute | solution.py:174
  19.0 1.9 %collective-permute-start.14 = (bf16[32,640]{1,0:T(8,128)(2,1)S(1)}, bf16[32,640]{1,0:T(8,128)(2,1)S(1)}, u32[]{:S(2)}, u32[]{:S(2)}) collective-permute-start(bf16[32,640]{1,0:T(8,128)(2,1)S(1)} %get-tuple-element.35), channel_id=1, source_target_pairs={{0,4},{1,5},{2,6},{3,7},{4,0},{5,1},{6,2},{7,3},{8,12},{9,13},{10,... | collective-permute-start | bytes 122888 | tf_op jit(solution)/shard_map/ppermute | solution.py:174
  20.9 2.5 %collective-permute-start.9 = (bf16[16,640]{1,0:T(8,128)(2,1)S(1)}, bf16[16,640]{1,0:T(8,128)(2,1)S(1)}, u32[]{:S(2)}, u32[]{:S(2)}) collective-permute-start(bf16[16,640]{1,0:T(8,128)(2,1)S(1)} %shard_map.83.refs_0_), channel_id=1, source_target_pairs={{0,24},{8,16},{16,8},{24,0},{1,25},{9,17},{17,9},{25,1},{2,26},{10... | collective-permute-start | bytes 61448 | tf_op jit(solution)/shard_map/ppermute | solution.py:174
  24.0 0.5 %collective-permute-start.7 = (bf16[16,640]{1,0:T(8,128)(2,1)S(1)}, bf16[16,640]{1,0:T(8,128)(2,1)S(1)}, u32[]{:S(2)}, u32[]{:S(2)}) collective-permute-start(bf16[16,640]{1,0:T(8,128)(2,1)S(1)} %shard_map.83.refs_0_), channel_id=1, source_target_pairs={{0,8},{8,0},{16,24},{24,16},{1,9},{9,1},{17,25},{25,17},{2,10},{10... | collective-permute-start | bytes 61448 | tf_op jit(solution)/shard_map/ppermute | solution.py:174
  24.5 2.4 %collective-permute-start.15 = (bf16[32,640]{1,0:T(8,128)(2,1)S(1)}, bf16[32,640]{1,0:T(8,128)(2,1)S(1)}, u32[]{:S(2)}, u32[]{:S(2)}) collective-permute-start(bf16[32,640]{1,0:T(8,128)(2,1)S(1)} %get-tuple-element.36), channel_id=1, source_target_pairs={{0,6},{1,7},{2,4},{3,5},{4,2},{5,3},{6,0},{7,1},{8,14},{9,15},{10,... | collective-permute-start | bytes 122888 | tf_op jit(solution)/shard_map/ppermute | solution.py:174
  27.2 1.5 %collective-permute-start.18 = (bf16[32,640]{1,0:T(8,128)(2,1)S(1)}, bf16[32,640]{1,0:T(8,128)(2,1)S(1)}, u32[]{:S(2)}, u32[]{:S(2)}) collective-permute-start(bf16[32,640]{1,0:T(8,128)(2,1)S(1)} %get-tuple-element.39), channel_id=1, source_target_pairs={{0,5},{1,4},{2,7},{3,6},{4,1},{5,0},{6,3},{7,2},{8,13},{9,12},{10,... | collective-permute-start | bytes 122888 | tf_op jit(solution)/shard_map/ppermute | solution.py:174
  28.7 2.5 %collective-permute-start.19 = (bf16[32,640]{1,0:T(8,128)(2,1)S(1)}, bf16[32,640]{1,0:T(8,128)(2,1)S(1)}, u32[]{:S(2)}, u32[]{:S(2)}) collective-permute-start(bf16[32,640]{1,0:T(8,128)(2,1)S(1)} %get-tuple-element.40), channel_id=1, source_target_pairs={{0,7},{1,6},{2,5},{3,4},{4,3},{5,2},{6,1},{7,0},{8,15},{9,14},{10,... | collective-permute-start | bytes 122888 | tf_op jit(solution)/shard_map/ppermute | solution.py:174
  31.2 0.8 %shard_map.84 = (bf16[32,384]{1,0:T(8,128)(2,1)S(1)}, bf16[32,384]{1,0:T(8,128)(2,1)S(1)}, bf16[32,384]{1,0:T(8,128)(2,1)S(1)}, bf16[32,384]{1,0:T(8,128)(2,1)S(1)}) custom-call(bf16[16,640]{1,0:T(8,128)(2,1)S(1)} %shard_map.83.refs_0_, bf16[16,640]{1,0:T(8,128)(2,1)S(1)} %collective-permute-done.7.refs_1_, ...), custom_call_target="tpu_custom_call" | custom-call | tf_op jit(solution)/shard_map/pallas_call | solution.py:163
  32.1 1.6 %collective-permute-start.10 = (bf16[32,384]{1,0:T(8,128)(2,1)S(1)}, bf16[32,384]{1,0:T(8,128)(2,1)S(1)}, u32[]{:S(2)}, u32[]{:S(2)}) collective-permute-start(bf16[32,384]{1,0:T(8,128)(2,1)S(1)} %get-tuple-element.30), channel_id=1, source_target_pairs={{0,8},{8,0},{16,24},{24,16},{1,9},{9,1},{17,25},{25,17},{2,10},{10... | collective-permute-start | bytes 73736 | tf_op jit(solution)/shard_map/ppermute | solution.py:174
  34.0 1.5 %shard_map.85 = (bf16[64,384]{1,0:T(8,128)(2,1)S(1)}, bf16[64,384]{1,0:T(8,128)(2,1)S(1)}, bf16[64,384]{1,0:T(8,128)(2,1)S(1)}, bf16[64,384]{1,0:T(8,128)(2,1)S(1)}) custom-call(bf16[16,640]{1,0:T(8,128)(2,1)S(1)} %shard_map.83.refs_0_, bf16[16,640]{1,0:T(8,128)(2,1)S(1)} %collective-permute-done.7.refs_1_, ...), custom_call_target="tpu_custom_call" | custom-call | tf_op jit(solution)/shard_map/pallas_call | solution.py:163
  35.4 1.6 %collective-permute-start.20 = (bf16[64,384]{1,0:T(8,128)(2,1)S(1)}, bf16[64,384]{1,0:T(8,128)(2,1)S(1)}, u32[]{:S(2)}, u32[]{:S(2)}) collective-permute-start(bf16[64,384]{1,0:T(8,128)(2,1)S(1)} %get-tuple-element.42), channel_id=1, source_target_pairs={{0,8},{8,0},{16,24},{24,16},{1,9},{9,1},{17,25},{25,17},{2,10},{10... | collective-permute-start | bytes 147464 | tf_op jit(solution)/shard_map/ppermute | solution.py:174
  37.0 1.5 %collective-permute-start.21 = (bf16[64,384]{1,0:T(8,128)(2,1)S(1)}, bf16[64,384]{1,0:T(8,128)(2,1)S(1)}, u32[]{:S(2)}, u32[]{:S(2)}) collective-permute-start(bf16[64,384]{1,0:T(8,128)(2,1)S(1)} %get-tuple-element.43), channel_id=1, source_target_pairs={{0,16},{8,24},{16,0},{24,8},{1,17},{9,25},{17,1},{25,9},{2,18},{10... | collective-permute-start | bytes 147464 | tf_op jit(solution)/shard_map/ppermute | solution.py:174
  39.0 1.5 %collective-permute-start.11 = (bf16[32,384]{1,0:T(8,128)(2,1)S(1)}, bf16[32,384]{1,0:T(8,128)(2,1)S(1)}, u32[]{:S(2)}, u32[]{:S(2)}) collective-permute-start(bf16[32,384]{1,0:T(8,128)(2,1)S(1)} %get-tuple-element.31), channel_id=1, source_target_pairs={{0,16},{8,24},{16,0},{24,8},{1,17},{9,25},{17,1},{25,9},{2,18},{10... | collective-permute-start | bytes 73736 | tf_op jit(solution)/shard_map/ppermute | solution.py:174
  40.5 1.4 %collective-permute-start.12 = (bf16[32,384]{1,0:T(8,128)(2,1)S(1)}, bf16[32,384]{1,0:T(8,128)(2,1)S(1)}, u32[]{:S(2)}, u32[]{:S(2)}) collective-permute-start(bf16[32,384]{1,0:T(8,128)(2,1)S(1)} %get-tuple-element.32), channel_id=1, source_target_pairs={{0,24},{8,16},{16,8},{24,0},{1,25},{9,17},{17,9},{25,1},{2,26},{10... | collective-permute-start | bytes 73736 | tf_op jit(solution)/shard_map/ppermute | solution.py:174
  42.8 2.4 %collective-permute-done.12.refs_3_ = bf16[32,384]{1,0:T(8,128)(2,1)S(1)} collective-permute-done((bf16[32,384]{1,0:T(8,128)(2,1)S(1)}, bf16[32,384]{1,0:T(8,128)(2,1)S(1)}, u32[]{:S(2)}, u32[]{:S(2)}) %collective-permute-start.12) | collective-permute-done | bytes 24608 | tf_op jit(solution)/shard_map/ppermute | solution.py:174
  45.3 1.5 %shard_map.86 = f32[48,3,2,384]{3,2,1,0:T(2,128)} custom-call(s32[1,3]{1,0:T(1,128)S(1)} %copy-done.6, s32[1]{0:T(128)S(6)} %copy.9.counts_ref, bf16[32,384]{1,0:T(8,128)(2,1)S(1)} %get-tuple-element.29.refs_0_, bf16[32,384]{1,0:T(8,128)(2,1)S(1)} %collective-permute-done.10.refs_1_, bf16[32,384]{1,0:T(8,128)(2,1)S(1)} %collective-permute-done.11.refs_2_, ...), custom_call_target="tpu_custom_call" | custom-call | tf_op jit(solution)/shard_map/pallas_call | solution.py:163
  (41 shorter events, 2.4 us)
Async XLA Ops:
  7.4 37.9 %copy-start.6 = (s32[1,3]{1,0:T(1,128)S(1)}, s32[1,3]{1,0:T(1,128)}, u32[]{:S(2)}) copy-start(s32[1,3]{1,0:T(1,128)} %partner_ref.1) | copy-start | bytes 40
  7.4 5.7 %collective-permute-start = (bf16[40,640]{1,0:T(8,128)(2,1)S(1)}, bf16[40,640]{1,0:T(8,128)(2,1)S(1)}, u32[]{:S(2)}, u32[]{:S(2)}) collective-permute-start(bf16[40,640]{1,0:T(8,128)(2,1)S(1)} %get-tuple-element.26), channel_id=1, source_target_pairs={{0,2},{1,3},{2,0},{3,1},{4,6},{5,7},{6,4},{7,5},{8,10},{9,11},{10,... | collective-permute-start | bytes 153608 | tf_op jit(solution)/shard_map/ppermute | solution.py:174
  10.5 6.0 %collective-permute-start.1 = (bf16[40,640]{1,0:T(8,128)(2,1)S(1)}, bf16[40,640]{1,0:T(8,128)(2,1)S(1)}, u32[]{:S(2)}, u32[]{:S(2)}) collective-permute-start(bf16[40,640]{1,0:T(8,128)(2,1)S(1)} %get-tuple-element.27), channel_id=1, source_target_pairs={{0,4},{1,5},{2,6},{3,7},{4,0},{5,1},{6,2},{7,3},{8,12},{9,13},{10,... | collective-permute-start | bytes 153608 | tf_op jit(solution)/shard_map/ppermute | solution.py:174
  13.0 5.9 %collective-permute-start.2 = (bf16[40,640]{1,0:T(8,128)(2,1)S(1)}, bf16[40,640]{1,0:T(8,128)(2,1)S(1)}, u32[]{:S(2)}, u32[]{:S(2)}) collective-permute-start(bf16[40,640]{1,0:T(8,128)(2,1)S(1)} %get-tuple-element.28), channel_id=1, source_target_pairs={{0,6},{1,7},{2,4},{3,5},{4,2},{5,3},{6,0},{7,1},{8,14},{9,15},{10,... | collective-permute-start | bytes 153608 | tf_op jit(solution)/shard_map/ppermute | solution.py:174
  13.1 5.9 %collective-permute-start.3 = (bf16[40,640]{1,0:T(8,128)(2,1)S(1)}, bf16[40,640]{1,0:T(8,128)(2,1)S(1)}, u32[]{:S(2)}, u32[]{:S(2)}) collective-permute-start(bf16[40,640]{1,0:T(8,128)(2,1)S(1)} %get-tuple-element.25.refs_0_.refs_4_), channel_id=1, source_target_pairs={{0,1},{1,0},{2,3},{3,2},{4,5},{5,4},{6,7},{7,6},{8,9},{9,8},{10,11... | collective-permute-start | bytes 153608 | tf_op jit(solution)/shard_map/ppermute | solution.py:174
  13.1 7.8 %collective-permute-start.4 = (bf16[40,640]{1,0:T(8,128)(2,1)S(1)}, bf16[40,640]{1,0:T(8,128)(2,1)S(1)}, u32[]{:S(2)}, u32[]{:S(2)}) collective-permute-start(bf16[40,640]{1,0:T(8,128)(2,1)S(1)} %collective-permute-done.refs_1_.refs_5_), channel_id=1, source_target_pairs={{0,1},{1,0},{2,3},{3,2},{4,5},{5,4},{6,7},{7,6},{8,9},{9,8},{10,11... | collective-permute-start | bytes 153608 | tf_op jit(solution)/shard_map/ppermute | solution.py:174
  16.5 4.5 %collective-permute-start.5 = (bf16[40,640]{1,0:T(8,128)(2,1)S(1)}, bf16[40,640]{1,0:T(8,128)(2,1)S(1)}, u32[]{:S(2)}, u32[]{:S(2)}) collective-permute-start(bf16[40,640]{1,0:T(8,128)(2,1)S(1)} %collective-permute-done.1.refs_2_.refs_6_), channel_id=1, source_target_pairs={{0,1},{1,0},{2,3},{3,2},{4,5},{5,4},{6,7},{7,6},{8,9},{9,8},{10,11... | collective-permute-start | bytes 153608 | tf_op jit(solution)/shard_map/ppermute | solution.py:174
  19.0 2.0 %collective-permute-start.6 = (bf16[40,640]{1,0:T(8,128)(2,1)S(1)}, bf16[40,640]{1,0:T(8,128)(2,1)S(1)}, u32[]{:S(2)}, u32[]{:S(2)}) collective-permute-start(bf16[40,640]{1,0:T(8,128)(2,1)S(1)} %collective-permute-done.2.refs_3_.refs_7_), channel_id=1, source_target_pairs={{0,1},{1,0},{2,3},{3,2},{4,5},{5,4},{6,7},{7,6},{8,9},{9,8},{10,11... | collective-permute-start | bytes 153608 | tf_op jit(solution)/shard_map/ppermute | solution.py:174
  19.0 5.5 %collective-permute-start.13 = (bf16[32,640]{1,0:T(8,128)(2,1)S(1)}, bf16[32,640]{1,0:T(8,128)(2,1)S(1)}, u32[]{:S(2)}, u32[]{:S(2)}) collective-permute-start(bf16[32,640]{1,0:T(8,128)(2,1)S(1)} %get-tuple-element.34), channel_id=1, source_target_pairs={{0,2},{1,3},{2,0},{3,1},{4,6},{5,7},{6,4},{7,5},{8,10},{9,11},{10,... | collective-permute-start | bytes 122888 | tf_op jit(solution)/shard_map/ppermute | solution.py:174
  19.0 8.0 %collective-permute-start.14 = (bf16[32,640]{1,0:T(8,128)(2,1)S(1)}, bf16[32,640]{1,0:T(8,128)(2,1)S(1)}, u32[]{:S(2)}, u32[]{:S(2)}) collective-permute-start(bf16[32,640]{1,0:T(8,128)(2,1)S(1)} %get-tuple-element.35), channel_id=1, source_target_pairs={{0,4},{1,5},{2,6},{3,7},{4,0},{5,1},{6,2},{7,3},{8,12},{9,13},{10,... | collective-permute-start | bytes 122888 | tf_op jit(solution)/shard_map/ppermute | solution.py:174
  20.9 6.0 %collective-permute-start.9 = (bf16[16,640]{1,0:T(8,128)(2,1)S(1)}, bf16[16,640]{1,0:T(8,128)(2,1)S(1)}, u32[]{:S(2)}, u32[]{:S(2)}) collective-permute-start(bf16[16,640]{1,0:T(8,128)(2,1)S(1)} %shard_map.83.refs_0_), channel_id=1, source_target_pairs={{0,24},{8,16},{16,8},{24,0},{1,25},{9,17},{17,9},{25,1},{2,26},{10... | collective-permute-start | bytes 61448 | tf_op jit(solution)/shard_map/ppermute | solution.py:174
  23.5 3.8 %collective-permute-start.8 = (bf16[16,640]{1,0:T(8,128)(2,1)S(1)}, bf16[16,640]{1,0:T(8,128)(2,1)S(1)}, u32[]{:S(2)}, u32[]{:S(2)}) collective-permute-start(bf16[16,640]{1,0:T(8,128)(2,1)S(1)} %shard_map.83.refs_0_), channel_id=1, source_target_pairs={{0,16},{8,24},{16,0},{24,8},{1,17},{9,25},{17,1},{25,9},{2,18},{10... | collective-permute-start | bytes 61448 | tf_op jit(solution)/shard_map/ppermute | solution.py:174
  24.0 4.7 %collective-permute-start.7 = (bf16[16,640]{1,0:T(8,128)(2,1)S(1)}, bf16[16,640]{1,0:T(8,128)(2,1)S(1)}, u32[]{:S(2)}, u32[]{:S(2)}) collective-permute-start(bf16[16,640]{1,0:T(8,128)(2,1)S(1)} %shard_map.83.refs_0_), channel_id=1, source_target_pairs={{0,8},{8,0},{16,24},{24,16},{1,9},{9,1},{17,25},{25,17},{2,10},{10... | collective-permute-start | bytes 61448 | tf_op jit(solution)/shard_map/ppermute | solution.py:174
  24.5 7.5 %collective-permute-start.15 = (bf16[32,640]{1,0:T(8,128)(2,1)S(1)}, bf16[32,640]{1,0:T(8,128)(2,1)S(1)}, u32[]{:S(2)}, u32[]{:S(2)}) collective-permute-start(bf16[32,640]{1,0:T(8,128)(2,1)S(1)} %get-tuple-element.36), channel_id=1, source_target_pairs={{0,6},{1,7},{2,4},{3,5},{4,2},{5,3},{6,0},{7,1},{8,14},{9,15},{10,... | collective-permute-start | bytes 122888 | tf_op jit(solution)/shard_map/ppermute | solution.py:174
  27.0 6.7 %collective-permute-start.16 = (bf16[32,640]{1,0:T(8,128)(2,1)S(1)}, bf16[32,640]{1,0:T(8,128)(2,1)S(1)}, u32[]{:S(2)}, u32[]{:S(2)}) collective-permute-start(bf16[32,640]{1,0:T(8,128)(2,1)S(1)} %get-tuple-element.37), channel_id=1, source_target_pairs={{0,1},{1,0},{2,3},{3,2},{4,5},{5,4},{6,7},{7,6},{8,9},{9,8},{10,11... | collective-permute-start | bytes 122888 | tf_op jit(solution)/shard_map/ppermute | solution.py:174
  27.0 6.7 %collective-permute-start.17 = (bf16[32,640]{1,0:T(8,128)(2,1)S(1)}, bf16[32,640]{1,0:T(8,128)(2,1)S(1)}, u32[]{:S(2)}, u32[]{:S(2)}) collective-permute-start(bf16[32,640]{1,0:T(8,128)(2,1)S(1)} %get-tuple-element.38), channel_id=1, source_target_pairs={{0,3},{1,2},{2,1},{3,0},{4,7},{5,6},{6,5},{7,4},{8,11},{9,10},{10,... | collective-permute-start | bytes 122888 | tf_op jit(solution)/shard_map/ppermute | solution.py:174
  27.2 6.4 %collective-permute-start.18 = (bf16[32,640]{1,0:T(8,128)(2,1)S(1)}, bf16[32,640]{1,0:T(8,128)(2,1)S(1)}, u32[]{:S(2)}, u32[]{:S(2)}) collective-permute-start(bf16[32,640]{1,0:T(8,128)(2,1)S(1)} %get-tuple-element.39), channel_id=1, source_target_pairs={{0,5},{1,4},{2,7},{3,6},{4,1},{5,0},{6,3},{7,2},{8,13},{9,12},{10,... | collective-permute-start | bytes 122888 | tf_op jit(solution)/shard_map/ppermute | solution.py:174
  28.7 5.3 %collective-permute-start.19 = (bf16[32,640]{1,0:T(8,128)(2,1)S(1)}, bf16[32,640]{1,0:T(8,128)(2,1)S(1)}, u32[]{:S(2)}, u32[]{:S(2)}) collective-permute-start(bf16[32,640]{1,0:T(8,128)(2,1)S(1)} %get-tuple-element.40), channel_id=1, source_target_pairs={{0,7},{1,6},{2,5},{3,4},{4,3},{5,2},{6,1},{7,0},{8,15},{9,14},{10,... | collective-permute-start | bytes 122888 | tf_op jit(solution)/shard_map/ppermute | solution.py:174
  32.1 8.5 %collective-permute-start.10 = (bf16[32,384]{1,0:T(8,128)(2,1)S(1)}, bf16[32,384]{1,0:T(8,128)(2,1)S(1)}, u32[]{:S(2)}, u32[]{:S(2)}) collective-permute-start(bf16[32,384]{1,0:T(8,128)(2,1)S(1)} %get-tuple-element.30), channel_id=1, source_target_pairs={{0,8},{8,0},{16,24},{24,16},{1,9},{9,1},{17,25},{25,17},{2,10},{10... | collective-permute-start | bytes 73736 | tf_op jit(solution)/shard_map/ppermute | solution.py:174
  35.4 9.8 %collective-permute-start.20 = (bf16[64,384]{1,0:T(8,128)(2,1)S(1)}, bf16[64,384]{1,0:T(8,128)(2,1)S(1)}, u32[]{:S(2)}, u32[]{:S(2)}) collective-permute-start(bf16[64,384]{1,0:T(8,128)(2,1)S(1)} %get-tuple-element.42), channel_id=1, source_target_pairs={{0,8},{8,0},{16,24},{24,16},{1,9},{9,1},{17,25},{25,17},{2,10},{10... | collective-permute-start | bytes 147464 | tf_op jit(solution)/shard_map/ppermute | solution.py:174
  37.0 8.3 %collective-permute-start.21 = (bf16[64,384]{1,0:T(8,128)(2,1)S(1)}, bf16[64,384]{1,0:T(8,128)(2,1)S(1)}, u32[]{:S(2)}, u32[]{:S(2)}) collective-permute-start(bf16[64,384]{1,0:T(8,128)(2,1)S(1)} %get-tuple-element.43), channel_id=1, source_target_pairs={{0,16},{8,24},{16,0},{24,8},{1,17},{9,25},{17,1},{25,9},{2,18},{10... | collective-permute-start | bytes 147464 | tf_op jit(solution)/shard_map/ppermute | solution.py:174
  38.5 6.7 %collective-permute-start.22 = (bf16[64,384]{1,0:T(8,128)(2,1)S(1)}, bf16[64,384]{1,0:T(8,128)(2,1)S(1)}, u32[]{:S(2)}, u32[]{:S(2)}) collective-permute-start(bf16[64,384]{1,0:T(8,128)(2,1)S(1)} %get-tuple-element.44), channel_id=1, source_target_pairs={{0,24},{8,16},{16,8},{24,0},{1,25},{9,17},{17,9},{25,1},{2,26},{10... | collective-permute-start | bytes 147464 | tf_op jit(solution)/shard_map/ppermute | solution.py:174
  39.0 3.8 %collective-permute-start.11 = (bf16[32,384]{1,0:T(8,128)(2,1)S(1)}, bf16[32,384]{1,0:T(8,128)(2,1)S(1)}, u32[]{:S(2)}, u32[]{:S(2)}) collective-permute-start(bf16[32,384]{1,0:T(8,128)(2,1)S(1)} %get-tuple-element.31), channel_id=1, source_target_pairs={{0,16},{8,24},{16,0},{24,8},{1,17},{9,25},{17,1},{25,9},{2,18},{10... | collective-permute-start | bytes 73736 | tf_op jit(solution)/shard_map/ppermute | solution.py:174
  40.5 4.7 %collective-permute-start.12 = (bf16[32,384]{1,0:T(8,128)(2,1)S(1)}, bf16[32,384]{1,0:T(8,128)(2,1)S(1)}, u32[]{:S(2)}, u32[]{:S(2)}) collective-permute-start(bf16[32,384]{1,0:T(8,128)(2,1)S(1)} %get-tuple-element.32), channel_id=1, source_target_pairs={{0,24},{8,16},{16,8},{24,0},{1,25},{9,17},{17,9},{25,1},{2,26},{10... | collective-permute-start | bytes 73736 | tf_op jit(solution)/shard_map/ppermute | solution.py:174
  (6 other events, 66.9 us)

commit v2 on v1

v2 whole, which is shorter than its diff:
```python
import functools
import math

import jax
import jax.numpy as jnp
import ml_dtypes
import numpy as np
from jax import lax
from jax.experimental import pallas as pl
from jax.experimental.pallas import tpu as pltpu
from jax.sharding import PartitionSpec as P

L = 1536
F = 320
HL = 192
SMOOTH = 32
LANES = 128
TAIL = F % LANES
MAIN = F - TAIL
WIDTH = 2 * F
HALF = L // 2
SRC_ROWS = 8
F32 = jnp.float32
BF16 = jnp.bfloat16


def dft_half():
    n = np.arange(HALF)[:, None]
    k = np.arange(F)[None, :] + 1
    angle = (n * k % L).astype(np.float32) * np.float32(2.0 * math.pi / L)
    c, s = np.cos(angle), -np.sin(angle)
    table = np.concatenate([c[:, :MAIN], s[:, :MAIN], c[:, MAIN:], s[:, MAIN:]], axis=1)
    return table.astype(ml_dtypes.bfloat16)


def band_table():
    bins = np.concatenate([np.arange(F), np.arange(MAIN, F)])
    centre = np.clip(bins, SMOOTH, F - 1 - SMOOTH)
    band = np.abs(bins[:, None] - centre[None, :]) <= SMOOTH
    band[F:] = False
    return band.astype(ml_dtypes.bfloat16)


def lag_tables(scale):
    k = np.arange(F)[:, None] + 1
    j = np.arange(2 * HL)[None, :] - HL
    angle = np.mod(k * j, L).astype(np.float32) * np.float32(2.0 * math.pi / L)
    c, s = np.cos(angle) * np.float32(scale), -np.sin(angle) * np.float32(scale)
    table = np.concatenate([c[:MAIN], s[:MAIN], c[MAIN:], c[MAIN:], s[MAIN:], -s[MAIN:]], axis=0)
    high = table.astype(ml_dtypes.bfloat16)
    low = (table - high.astype(np.float32)).astype(ml_dtypes.bfloat16)
    return np.concatenate([high, low], axis=0)


def whiten(signal, tab, band):
    rows = signal.shape[0]
    signal = (signal - jnp.sum(signal, axis=1, keepdims=True) * (1.0 / L)).astype(BF16)
    halves = jnp.concatenate([signal[:, :HALF], signal[:, HALF:]], axis=0)
    spec = jnp.dot(halves, tab[...], preferred_element_type=F32)
    lane = lax.broadcasted_iota(jnp.int32, (1, WIDTH), 1)
    spec = spec[:rows] + jnp.where(lane % 2 == 1, 1.0, -1.0).astype(F32) * spec[rows:]
    re, im, tail = spec[:, :MAIN], spec[:, MAIN : 2 * MAIN], spec[:, 2 * MAIN :]
    tail_sq = tail * tail
    amp = jnp.sqrt(
        jnp.concatenate([re * re + im * im, tail_sq + pltpu.roll(tail_sq, TAIL, 1)], axis=1)
    )
    high = amp.astype(BF16)
    low = (amp - high.astype(F32)).astype(BF16)
    total = jnp.dot(high, band[...], preferred_element_type=F32) + jnp.dot(
        low, band[...], preferred_element_type=F32
    )
    factor = 1.0 / (total * (1.0 / (2 * SMOOTH + 1)) + 1e-06)
    return re * factor[:, :MAIN], im * factor[:, :MAIN], tail * factor[:, MAIN:]


def keep(ref, here, parts):
    ref[here, :MAIN], ref[here, MAIN : 2 * MAIN], ref[here, 2 * MAIN :] = parts


def whiten_kernel(layout, shared, src_hbm, rec_hbm, tab_hbm, band_hbm, *rest):
    outs = rest[: len(layout)]
    rec, tab, band, white, picked, sem = rest[len(layout) :]
    loads = [
        pltpu.make_async_copy(*pair, sem.at[i])
        for i, pair in enumerate(
            [(rec_hbm.at[0], rec), (tab_hbm, tab), (src_hbm, picked), (band_hbm, band)]
        )
    ]
    for load in loads:
        load.start()
    loads[0].wait()
    signal = rec[...].astype(F32)
    for load in loads[1:]:
        load.wait()
    keep(white, slice(None), whiten(signal, tab, band))
    place = lax.axis_index("tm")
    chip, core = place // 2, lax.rem(place, 2)
    row_id = lax.broadcasted_iota(jnp.int32, (SRC_ROWS, WIDTH), 0)
    source = jnp.zeros((SRC_ROWS, WIDTH), F32)
    for s in range(picked.shape[1]):
        source = jnp.where(row_id == s, white[pl.ds(picked[0, s], 1), :], source)
    for out, (d, first, size, with_source) in zip(outs, layout):
        rows = []
        for q in range(2):
            owner = jnp.bitwise_xor(chip, d) * 2 + jnp.bitwise_xor(core, q)
            if size:
                rows.append(white[pl.ds(pl.multiple_of(owner * shared + first, 8), size), :])
        if with_source:
            rows.append(source)
        out[...] = jnp.concatenate(rows, axis=0).astype(BF16)


def gather_kernel(size, *refs):
    ins, out = refs[:-1], refs[-1]
    parts = [ref[...].astype(F32)[2 * size :] for ref in ins]
    out[...] = jnp.concatenate(parts, axis=0).astype(BF16)


def hold_kernel(first, rest, count, *refs):
    out = refs[-1]
    parts = [ref[...].astype(F32)[first : 2 * first] for ref in refs[:count] if first]
    parts += [ref[...].astype(F32)[rest:] for ref in refs[count : 2 * count]]
    out[...] = jnp.concatenate(parts, axis=0).astype(BF16)


def pack_kernel(start, sources, here, there, out):
    parts = []
    for ref in (here, there):
        value = ref[...].astype(F32)[start:]
        parts += [value[i : i + sources] for i in range(0, value.shape[0], SRC_ROWS)]
    out[...] = jnp.concatenate(parts, axis=0).astype(BF16)


def cross_kernel(count, windows, sources, size, parts, *refs):
    src_refs = refs[:count]
    rec_refs = refs[count : count + len(parts)]
    lag_hbm = refs[count + len(parts)]
    outs = refs[count + len(parts) + 1 : 2 * count + len(parts) + 1]
    rec, src, stack, lag, sem = refs[2 * count + len(parts) + 1 :]
    lag_load = pltpu.make_async_copy(lag_hbm, lag, sem)
    lag_load.start()
    for ref, places in zip(rec_refs, parts):
        rows = ref[...].astype(F32)
        for w, start, place, length in places:
            value = rows[start : start + length]
            here = pl.ds(w * size + place, length)
            rec[here, :WIDTH] = value
            rec[here, WIDTH:] = pltpu.roll(value[:, 2 * MAIN :], TAIL, 1)
    per = windows * sources
    for b in range(count):
        src[pl.ds(b * per, per), :] = src_refs[b][...].astype(F32)
    step = 16 if size % 16 == 0 else 8
    for b in range(count):
        for s in range(sources):
            for g in range(0, size, step):
                totals = [0.0] * 4
                for w in range(windows):
                    a = src[pl.ds(b * per + w * sources + s, 1), :]
                    r = rec[pl.ds(w * size + g, step), :]
                    a_re, a_im, a_tail = a[:, :MAIN], a[:, MAIN : 2 * MAIN], a[:, 2 * MAIN :]
                    r_re, r_im = r[:, :MAIN], r[:, MAIN : 2 * MAIN]
                    totals[0] += a_re * r_re + a_im * r_im
                    totals[1] += a_re * r_im - a_im * r_re
                    totals[2] += a_tail * r[:, 2 * MAIN : WIDTH]
                    totals[3] += a_tail * r[:, WIDTH:]
                stack[pl.ds((b * sources + s) * size + g, step), :] = jnp.concatenate(totals, axis=1)
    cross = stack[...]
    high = cross.astype(BF16)
    low = (cross - high.astype(F32)).astype(BF16)
    lag_load.wait()
    lag_high, lag_low = lag[: WIDTH + LANES], lag[WIDTH + LANES :]
    lagged = (
        jnp.dot(high, lag_high, preferred_element_type=F32)
        + jnp.dot(low, lag_high, preferred_element_type=F32)
        + jnp.dot(high, lag_low, preferred_element_type=F32)
    )
    for b in range(count):
        outs[b][...] = lagged[b * sources * size : (b + 1) * sources * size].astype(BF16)


def finish_kernel(count, sources, partner_ref, counts_ref, *refs):
    ins, out = refs[:-1], refs[-1]
    me = lax.axis_index("chan")
    slots = partner_ref.shape[1]
    size = out.shape[0]
    for p in range(slots):
        wanted = jnp.bitwise_xor(partner_ref[0, p], me)
        wanted = jnp.where(p < counts_ref[0], wanted, -1)
        value = jnp.zeros((sources * size, 2 * HL), F32)
        for e in range(count):
            value = jnp.where(wanted == e, ins[e][...].astype(F32), value)
        for s in range(sources):
            out[:, p, s, :] = value[s * size : (s + 1) * size]


def in_hbm(value):
    return pltpu.with_memory_space_constraint(value, pltpu.HBM)


def call(kernel, out_shape, scratch, spaces, args):
    return pl.pallas_call(
        kernel,
        out_shape=out_shape,
        in_specs=[pl.BlockSpec(memory_space=space) for space in spaces],
        out_specs=jax.tree.map(lambda _: pl.BlockSpec(memory_space=pltpu.VMEM), out_shape),
        scratch_shapes=scratch,
        compiler_params=pltpu.CompilerParams(vmem_limit_bytes=40 * 1024 * 1024),
    )(*args)


def swap(value, axis, size, distance):
    return lax.ppermute(value, axis, [(i, i ^ distance) for i in range(size)])


def local(chans, tms, records, partners, counts, sources):
    channels = records.shape[1]
    picked = sources.shape[1]
    shared = channels // tms
    zs = tms // 2
    size = 2 * shared
    shape = jax.ShapeDtypeStruct
    vmem, smem, hbm = pltpu.VMEM, pltpu.SMEM, pltpu.HBM

    table, band = dft_half(), band_table()
    first = 16
    rest = shared - first
    layout = [(d, 0, first, True) for d in range(zs)]
    layout += [(d, first, rest, False) for d in range(zs)]
    rows = [2 * n + (SRC_ROWS if src else 0) for _, _, n, src in layout]
    sent = call(
        functools.partial(whiten_kernel, layout, shared),
        [shape((n, WIDTH), BF16) for n in rows],
        [
            pltpu.VMEM((channels, L), BF16),
            pltpu.VMEM(table.shape, BF16),
            pltpu.VMEM(band.shape, BF16),
            pltpu.VMEM((channels, WIDTH), F32),
            pltpu.SMEM(sources.shape, jnp.int32),
            pltpu.SemaphoreType.DMA((4,)),
        ],
        [hbm] * 4,
        tuple(in_hbm(v) for v in (sources, records, jnp.asarray(table), jnp.asarray(band))),
    )

    def across(values):
        return [v if d == 0 else swap(v, "tm", tms, 2 * d) for d, v in enumerate(values)]

    one, two = across(sent[:zs]), across(sent[zs:])
    gathered = call(
        functools.partial(gather_kernel, first),
        shape((zs * SRC_ROWS, WIDTH), BF16),
        [],
        [vmem] * zs,
        one,
    )
    other_one = swap(gathered, "tm", tms, 1)
    own = call(
        functools.partial(pack_kernel, 0, picked),
        shape((tms * picked, WIDTH), BF16),
        [],
        [vmem] * 2,
        [gathered, other_one],
    )
    spectra = [own] + [swap(own, "chan", chans, e) for e in range(1, chans)]
    deps = spectra[1:]
    gathered = call(
        functools.partial(hold_kernel, first, rest, zs),
        shape((zs * shared, WIDTH), BF16),
        [],
        [vmem] * (2 * zs + len(deps)),
        one + two + deps,
    )
    other_two = swap(gathered, "tm", tms, 1)
    receivers, parts = [], []
    for values, start, size in ((one, 0, first), (two, first, rest)):
        if size:
            receivers += values
            parts += [[(d, 0, start, size)] for d in range(zs)]
    receivers.append(other_two)
    places = [(zs + d, d * first, 0, first) for d in range(zs) if first]
    places += [(zs + d, zs * first + d * rest, first, rest) for d in range(zs)]
    parts.append(places)

    lags = lag_tables(1.0 / math.sqrt(F * tms))
    done = call(
        functools.partial(cross_kernel, chans, tms, picked, shared, parts),
        [shape((picked * shared, 2 * HL), BF16)] * chans,
        [
            pltpu.VMEM((tms * shared, WIDTH + LANES), F32),
            pltpu.VMEM((chans * tms * picked, WIDTH), F32),
            pltpu.VMEM((chans * picked * shared, WIDTH + LANES), F32),
            pltpu.VMEM(lags.shape, BF16),
            pltpu.SemaphoreType.DMA,
        ],
        [vmem] * (chans + len(receivers)) + [hbm],
        (*spectra, *receivers, in_hbm(jnp.asarray(lags))),
    )
    arrived = [done[0]] + [swap(done[e], "chan", chans, e) for e in range(1, chans)]
    result = call(
        functools.partial(finish_kernel, chans, picked),
        shape((shared, partners.shape[1], picked, 2 * HL), F32),
        [],
        [smem] * 2 + [vmem] * chans,
        (partners, counts, *arrived),
    )
    return result[None]


def solution(mesh):
    sizes = dict(mesh.shape)
    return jax.shard_map(
        functools.partial(local, sizes["chan"], sizes["tm"]),
        mesh=mesh,
        in_specs=(P("tm", "chan", None), P("chan", None), P("chan"), P("chan", None)),
        out_specs=P("chan", "tm", None, None, None),
        check_vma=False,
    )
```

time: 47 us -> 37.5 us (0.80)
  starting transfers between devices: 26.2 us -> 17.2 us
  local copies, waits for them, and re-layouts: 4.54 us -> 0.01 us
  waiting for transfers between devices: 8.61 us -> 11.5 us
  Pallas kernels: 6.69 us -> 7.92 us
    ppermute x23 -> x14, starting transfers between devices: 26.2 us -> 17.2 us  [swap(): return lax.ppermute(value, axis, [(i, i ^ distance) for i in range(size)])]
    unnamed x14 -> x2, local copies, waits for them, and re-layouts: 4.54 us -> 0.01 us
    ppermute x23 -> x14, waiting for transfers between devices: 8.61 us -> 11.5 us  [swap(): return lax.ppermute(value, axis, [(i, i ^ distance) for i in range(size)])]
    pallas_call x5 -> x6, Pallas kernels: 6.69 us -> 7.92 us  [call(): pl.pallas_call(kernel, out_shape=out_shape, in_specs=[pl.BlockSpec(memory...]
  transfers between devices with their start and end apart: 23 -> 14, of which waited for: 6 -> 8; matrix products, arithmetic and copies ran while one was open for 0% -> 0% of each run, Pallas kernels for 5% -> 0%
where the time goes in v2:
time: 37.5 us; the launch traced here: 37.4 us
  starting transfers between devices  17.2 us (46%)
  waiting for transfers between devices  11.5 us (31%)
  Pallas kernels  7.92 us (21%)
  between operations  0.71 us (2%)
    ppermute x14, starting transfers between devices, swap(): return lax.ppermute(value, axis, [(i, i ^ distance) for i in range(size)])  17.2 us
    ppermute x14, waiting for transfers between devices, swap(): return lax.ppermute(value, axis, [(i, i ^ distance) for i in range(size)])  11.5 us
    pallas_call x6, Pallas kernels, call(): pl.pallas_call(kernel, out_shape=out_shape, in_specs=[pl.BlockSpec(memory...  7.92 us
  transfers between devices with their start and end apart: 14, of which 8 were waited for; matrix products, arithmetic and copies ran while one was open for 0% of the time, Pallas kernels for 0%

profile of v2, /device:TPU:0, one launch (start us, length us, event | category | flops | bytes accessed | tf_op | source)
XLA Modules:
  0.0 37.4 jit_solution(16493117466300087461)
XLA Ops:
  0.0 3.9 %shard_map.73 = (bf16[40,640]{1,0:T(8,128)(2,1)S(1)}, bf16[40,640]{1,0:T(8,128)(2,1)S(1)}, bf16[40,640]{1,0:T(8,128)(2,1)S(1)}, bf16[40,640]{1,0:T(8,128)(2,1)S(...) custom-call(s32[1,2]{1,0:T(1,128)} %src_hbm.1, ...), custom_call_target="tpu_custom_call" | custom-call | tf_op jit(solution)/shard_map/pallas_call | solution.py:201
  3.9 3.1 %collective-permute-start = (bf16[40,640]{1,0:T(8,128)(2,1)S(1)}, bf16[40,640]{1,0:T(8,128)(2,1)S(1)}, u32[]{:S(2)}, u32[]{:S(2)}) collective-permute-start(bf16[40,640]{1,0:T(8,128)(2,1)S(1)} %get-tuple-element.18), channel_id=1, source_target_pairs={{0,2},{1,3},{2,0},{3,1},{4,6},{5,7},{6,4},{7,5},{8,10},{9,11},{10,... | collective-permute-start | bytes 153608 | tf_op jit(solution)/shard_map/ppermute | solution.py:212
  7.0 2.6 %collective-permute-start.1 = (bf16[40,640]{1,0:T(8,128)(2,1)S(1)}, bf16[40,640]{1,0:T(8,128)(2,1)S(1)}, u32[]{:S(2)}, u32[]{:S(2)}) collective-permute-start(bf16[40,640]{1,0:T(8,128)(2,1)S(1)} %get-tuple-element.19), channel_id=1, source_target_pairs={{0,4},{1,5},{2,6},{3,7},{4,0},{5,1},{6,2},{7,3},{8,12},{9,13},{10,... | collective-permute-start | bytes 153608 | tf_op jit(solution)/shard_map/ppermute | solution.py:212
  9.6 0.9 %collective-permute-start.7 = (bf16[64,640]{1,0:T(8,128)(2,1)S(1)}, bf16[64,640]{1,0:T(8,128)(2,1)S(1)}, u32[]{:S(2)}, u32[]{:S(2)}) collective-permute-start(bf16[64,640]{1,0:T(8,128)(2,1)S(1)} %get-tuple-element.22), channel_id=1, source_target_pairs={{0,2},{1,3},{2,0},{3,1},{4,6},{5,7},{6,4},{7,5},{8,10},{9,11},{10,... | collective-permute-start | bytes 245768 | tf_op jit(solution)/shard_map/ppermute | solution.py:212
  10.5 3.5 %collective-permute-start.8 = (bf16[64,640]{1,0:T(8,128)(2,1)S(1)}, bf16[64,640]{1,0:T(8,128)(2,1)S(1)}, u32[]{:S(2)}, u32[]{:S(2)}) collective-permute-start(bf16[64,640]{1,0:T(8,128)(2,1)S(1)} %get-tuple-element.23), channel_id=1, source_target_pairs={{0,4},{1,5},{2,6},{3,7},{4,0},{5,1},{6,2},{7,3},{8,12},{9,13},{10,... | collective-permute-start | bytes 245768 | tf_op jit(solution)/shard_map/ppermute | solution.py:212
  14.0 0.0 collective-permute-done.refs_1_.refs_5_
  14.0 2.2 %collective-permute-done.2.refs_3_.refs_7_ = bf16[40,640]{1,0:T(8,128)(2,1)S(1)} collective-permute-done((bf16[40,640]{1,0:T(8,128)(2,1)S(1)}, bf16[40,640]{1,0:T(8,128)(2,1)S(1)}, u32[]{:S(2)}, u32[]{:S(2)}) %collective-permute-start.2) | collective-permute-done | bytes 51232 | tf_op jit(solution)/shard_map/ppermute | solution.py:212
  16.2 1.2 %collective-permute-done.3.there = bf16[32,640]{1,0:T(8,128)(2,1)S(1)} collective-permute-done((bf16[32,640]{1,0:T(8,128)(2,1)S(1)}, bf16[32,640]{1,0:T(8,128)(2,1)S(1)}, u32[]{:S(2)}, u32[]{:S(2)}) %collective-permute-start.3) | collective-permute-done | bytes 40992 | tf_op jit(solution)/shard_map/ppermute | solution.py:212
  17.4 1.6 %collective-permute-start.4 = (bf16[16,640]{1,0:T(8,128)(2,1)S(1)}, bf16[16,640]{1,0:T(8,128)(2,1)S(1)}, u32[]{:S(2)}, u32[]{:S(2)}) collective-permute-start(bf16[16,640]{1,0:T(8,128)(2,1)S(1)} %shard_map.75.refs_0_), channel_id=1, source_target_pairs={{0,8},{8,0},{16,24},{24,16},{1,9},{9,1},{17,25},{25,17},{2,10},{10... | collective-permute-start | bytes 61448 | tf_op jit(solution)/shard_map/ppermute | solution.py:212
  19.0 1.5 %collective-permute-start.5 = (bf16[16,640]{1,0:T(8,128)(2,1)S(1)}, bf16[16,640]{1,0:T(8,128)(2,1)S(1)}, u32[]{:S(2)}, u32[]{:S(2)}) collective-permute-start(bf16[16,640]{1,0:T(8,128)(2,1)S(1)} %shard_map.75.refs_0_), channel_id=1, source_target_pairs={{0,16},{8,24},{16,0},{24,8},{1,17},{9,25},{17,1},{25,9},{2,18},{10... | collective-permute-start | bytes 61448 | tf_op jit(solution)/shard_map/ppermute | solution.py:212
  20.5 0.5 %collective-permute-start.6 = (bf16[16,640]{1,0:T(8,128)(2,1)S(1)}, bf16[16,640]{1,0:T(8,128)(2,1)S(1)}, u32[]{:S(2)}, u32[]{:S(2)}) collective-permute-start(bf16[16,640]{1,0:T(8,128)(2,1)S(1)} %shard_map.75.refs_0_), channel_id=1, source_target_pairs={{0,24},{8,16},{16,8},{24,0},{1,25},{9,17},{17,9},{25,1},{2,26},{10... | collective-permute-start | bytes 61448 | tf_op jit(solution)/shard_map/ppermute | solution.py:212
  21.0 0.3 collective-permute-done.4.refs_8_.refs_1_
  21.3 1.5 %collective-permute-done.5.refs_9_.refs_2_ = bf16[16,640]{1,0:T(8,128)(2,1)S(1)} collective-permute-done((bf16[16,640]{1,0:T(8,128)(2,1)S(1)}, bf16[16,640]{1,0:T(8,128)(2,1)S(1)}, u32[]{:S(2)}, u32[]{:S(2)}) %collective-permute-start.5) | collective-permute-done | bytes 20512 | tf_op jit(solution)/shard_map/ppermute | solution.py:212
  22.8 2.4 %collective-permute-done.6.refs_10_.refs_3_ = bf16[16,640]{1,0:T(8,128)(2,1)S(1)} collective-permute-done((bf16[16,640]{1,0:T(8,128)(2,1)S(1)}, bf16[16,640]{1,0:T(8,128)(2,1)S(1)}, u32[]{:S(2)}, u32[]{:S(2)}) %collective-permute-start.6) | collective-permute-done | bytes 20512 | tf_op jit(solution)/shard_map/ppermute | solution.py:212
  25.2 0.0 copy-start
  25.2 0.1 collective-permute-start.10
  25.3 1.5 %collective-permute-done.10.refs_12_ = bf16[192,640]{1,0:T(8,128)(2,1)S(1)} collective-permute-done((bf16[192,640]{1,0:T(8,128)(2,1)S(1)}, bf16[192,640]{1,0:T(8,128)(2,1)S(1)}, u32[]{:S(2)}, u32[]{:S(2)}) %collective-permute-start.10) | collective-permute-done | bytes 245792 | tf_op jit(solution)/shard_map/ppermute | solution.py:212
  26.8 2.5 %shard_map.77 = (bf16[96,384]{1,0:T(8,128)(2,1)S(1)}, bf16[96,384]{1,0:T(8,128)(2,1)S(1)}, bf16[96,384]{1,0:T(8,128)(2,1)S(1)}, bf16[96,384]{1,0:T(8,128)(2,1)S(1)}) custom-call(bf16[16,640]{1,0:T(8,128)(2,1)S(1)} %shard_map.75.refs_0_, bf16[16,640]{1,0:T(8,128)(2,1)S(1)} %collective-permute-done.4.refs_8_.refs_1_, ...), custom_call_target="tpu_custom_call" | custom-call | tf_op jit(solution)/shard_map/pallas_call | solution.py:201
  29.3 0.6 %collective-permute-start.11 = (bf16[96,384]{1,0:T(8,128)(2,1)S(1)}, bf16[96,384]{1,0:T(8,128)(2,1)S(1)}, u32[]{:S(2)}, u32[]{:S(2)}) collective-permute-start(bf16[96,384]{1,0:T(8,128)(2,1)S(1)} %get-tuple-element.26), channel_id=1, source_target_pairs={{0,8},{8,0},{16,24},{24,16},{1,9},{9,1},{17,25},{25,17},{2,10},{10... | collective-permute-start | bytes 221192 | tf_op jit(solution)/shard_map/ppermute | solution.py:212
  29.9 0.5 %collective-permute-start.12 = (bf16[96,384]{1,0:T(8,128)(2,1)S(1)}, bf16[96,384]{1,0:T(8,128)(2,1)S(1)}, u32[]{:S(2)}, u32[]{:S(2)}) collective-permute-start(bf16[96,384]{1,0:T(8,128)(2,1)S(1)} %get-tuple-element.27), channel_id=1, source_target_pairs={{0,16},{8,24},{16,0},{24,8},{1,17},{9,25},{17,1},{25,9},{2,18},{10... | collective-permute-start | bytes 221192 | tf_op jit(solution)/shard_map/ppermute | solution.py:212
  30.4 2.4 %collective-permute-start.13 = (bf16[96,384]{1,0:T(8,128)(2,1)S(1)}, bf16[96,384]{1,0:T(8,128)(2,1)S(1)}, u32[]{:S(2)}, u32[]{:S(2)}) collective-permute-start(bf16[96,384]{1,0:T(8,128)(2,1)S(1)} %get-tuple-element.28), channel_id=1, source_target_pairs={{0,24},{8,16},{16,8},{24,0},{1,25},{9,17},{17,9},{25,1},{2,26},{10... | collective-permute-start | bytes 221192 | tf_op jit(solution)/shard_map/ppermute | solution.py:212
  33.5 0.5 %collective-permute-done.11.refs_1_ = bf16[96,384]{1,0:T(8,128)(2,1)S(1)} collective-permute-done((bf16[96,384]{1,0:T(8,128)(2,1)S(1)}, bf16[96,384]{1,0:T(8,128)(2,1)S(1)}, u32[]{:S(2)}, u32[]{:S(2)}) %collective-permute-start.11) | collective-permute-done | bytes 73760 | tf_op jit(solution)/shard_map/ppermute | solution.py:212
  33.9 1.9 %collective-permute-done.12.refs_2_ = bf16[96,384]{1,0:T(8,128)(2,1)S(1)} collective-permute-done((bf16[96,384]{1,0:T(8,128)(2,1)S(1)}, bf16[96,384]{1,0:T(8,128)(2,1)S(1)}, u32[]{:S(2)}, u32[]{:S(2)}) %collective-permute-start.12) | collective-permute-done | bytes 73760 | tf_op jit(solution)/shard_map/ppermute | solution.py:212
  35.8 1.5 %shard_map.78 = f32[48,3,2,384]{3,2,1,0:T(2,128)} custom-call(s32[1,3]{1,0:T(1,128)S(1)} %copy-done, s32[1]{0:T(128)S(6)} %copy.8.counts_ref, bf16[96,384]{1,0:T(8,128)(2,1)S(1)} %get-tuple-element.25.refs_0_, bf16[96,384]{1,0:T(8,128)(2,1)S(1)} %collective-permute-done.11.refs_1_, bf16[96,384]{1,0:T(8,128)(2,1)S(1)} %collective-permute-done.12.refs_2_, ...), custom_call_target="tpu_custom_call" | custom-call | tf_op jit(solution)/shard_map/pallas_call | solution.py:201
  (12 shorter events, 0.1 us)
Async XLA Ops:
  3.9 10.1 %collective-permute-start = (bf16[40,640]{1,0:T(8,128)(2,1)S(1)}, bf16[40,640]{1,0:T(8,128)(2,1)S(1)}, u32[]{:S(2)}, u32[]{:S(2)}) collective-permute-start(bf16[40,640]{1,0:T(8,128)(2,1)S(1)} %get-tuple-element.18), channel_id=1, source_target_pairs={{0,2},{1,3},{2,0},{3,1},{4,6},{5,7},{6,4},{7,5},{8,10},{9,11},{10,... | collective-permute-start | bytes 153608 | tf_op jit(solution)/shard_map/ppermute | solution.py:212
  7.0 7.0 %collective-permute-start.1 = (bf16[40,640]{1,0:T(8,128)(2,1)S(1)}, bf16[40,640]{1,0:T(8,128)(2,1)S(1)}, u32[]{:S(2)}, u32[]{:S(2)}) collective-permute-start(bf16[40,640]{1,0:T(8,128)(2,1)S(1)} %get-tuple-element.19), channel_id=1, source_target_pairs={{0,4},{1,5},{2,6},{3,7},{4,0},{5,1},{6,2},{7,3},{8,12},{9,13},{10,... | collective-permute-start | bytes 153608 | tf_op jit(solution)/shard_map/ppermute | solution.py:212
  9.6 6.6 %collective-permute-start.2 = (bf16[40,640]{1,0:T(8,128)(2,1)S(1)}, bf16[40,640]{1,0:T(8,128)(2,1)S(1)}, u32[]{:S(2)}, u32[]{:S(2)}) collective-permute-start(bf16[40,640]{1,0:T(8,128)(2,1)S(1)} %get-tuple-element.20), channel_id=1, source_target_pairs={{0,6},{1,7},{2,4},{3,5},{4,2},{5,3},{6,0},{7,1},{8,14},{9,15},{10,... | collective-permute-start | bytes 153608 | tf_op jit(solution)/shard_map/ppermute | solution.py:212
  9.6 10.9 %collective-permute-start.7 = (bf16[64,640]{1,0:T(8,128)(2,1)S(1)}, bf16[64,640]{1,0:T(8,128)(2,1)S(1)}, u32[]{:S(2)}, u32[]{:S(2)}) collective-permute-start(bf16[64,640]{1,0:T(8,128)(2,1)S(1)} %get-tuple-element.22), channel_id=1, source_target_pairs={{0,2},{1,3},{2,0},{3,1},{4,6},{5,7},{6,4},{7,5},{8,10},{9,11},{10,... | collective-permute-start | bytes 245768 | tf_op jit(solution)/shard_map/ppermute | solution.py:212
  10.5 10.5 %collective-permute-start.8 = (bf16[64,640]{1,0:T(8,128)(2,1)S(1)}, bf16[64,640]{1,0:T(8,128)(2,1)S(1)}, u32[]{:S(2)}, u32[]{:S(2)}) collective-permute-start(bf16[64,640]{1,0:T(8,128)(2,1)S(1)} %get-tuple-element.23), channel_id=1, source_target_pairs={{0,4},{1,5},{2,6},{3,7},{4,0},{5,1},{6,2},{7,3},{8,12},{9,13},{10,... | collective-permute-start | bytes 245768 | tf_op jit(solution)/shard_map/ppermute | solution.py:212
  14.0 7.0 %collective-permute-start.9 = (bf16[64,640]{1,0:T(8,128)(2,1)S(1)}, bf16[64,640]{1,0:T(8,128)(2,1)S(1)}, u32[]{:S(2)}, u32[]{:S(2)}) collective-permute-start(bf16[64,640]{1,0:T(8,128)(2,1)S(1)} %get-tuple-element.24), channel_id=1, source_target_pairs={{0,6},{1,7},{2,4},{3,5},{4,2},{5,3},{6,0},{7,1},{8,14},{9,15},{10,... | collective-permute-start | bytes 245768 | tf_op jit(solution)/shard_map/ppermute | solution.py:212
  16.2 1.2 %collective-permute-start.3 = (bf16[32,640]{1,0:T(8,128)(2,1)S(1)}, bf16[32,640]{1,0:T(8,128)(2,1)S(1)}, u32[]{:S(2)}, u32[]{:S(2)}) collective-permute-start(bf16[32,640]{1,0:T(8,128)(2,1)S(1)} %shard_map.74.here), channel_id=1, source_target_pairs={{0,1},{1,0},{2,3},{3,2},{4,5},{5,4},{6,7},{7,6},{8,9},{9,8},{10,11... | collective-permute-start | bytes 122888 | tf_op jit(solution)/shard_map/ppermute | solution.py:212
  17.4 3.8 %collective-permute-start.4 = (bf16[16,640]{1,0:T(8,128)(2,1)S(1)}, bf16[16,640]{1,0:T(8,128)(2,1)S(1)}, u32[]{:S(2)}, u32[]{:S(2)}) collective-permute-start(bf16[16,640]{1,0:T(8,128)(2,1)S(1)} %shard_map.75.refs_0_), channel_id=1, source_target_pairs={{0,8},{8,0},{16,24},{24,16},{1,9},{9,1},{17,25},{25,17},{2,10},{10... | collective-permute-start | bytes 61448 | tf_op jit(solution)/shard_map/ppermute | solution.py:212
  19.0 3.8 %collective-permute-start.5 = (bf16[16,640]{1,0:T(8,128)(2,1)S(1)}, bf16[16,640]{1,0:T(8,128)(2,1)S(1)}, u32[]{:S(2)}, u32[]{:S(2)}) collective-permute-start(bf16[16,640]{1,0:T(8,128)(2,1)S(1)} %shard_map.75.refs_0_), channel_id=1, source_target_pairs={{0,16},{8,24},{16,0},{24,8},{1,17},{9,25},{17,1},{25,9},{2,18},{10... | collective-permute-start | bytes 61448 | tf_op jit(solution)/shard_map/ppermute | solution.py:212
  20.5 4.7 %collective-permute-start.6 = (bf16[16,640]{1,0:T(8,128)(2,1)S(1)}, bf16[16,640]{1,0:T(8,128)(2,1)S(1)}, u32[]{:S(2)}, u32[]{:S(2)}) collective-permute-start(bf16[16,640]{1,0:T(8,128)(2,1)S(1)} %shard_map.75.refs_0_), channel_id=1, source_target_pairs={{0,24},{8,16},{16,8},{24,0},{1,25},{9,17},{17,9},{25,1},{2,26},{10... | collective-permute-start | bytes 61448 | tf_op jit(solution)/shard_map/ppermute | solution.py:212
  25.2 10.6 %copy-start = (s32[1,3]{1,0:T(1,128)S(1)}, s32[1,3]{1,0:T(1,128)}, u32[]{:S(2)}) copy-start(s32[1,3]{1,0:T(1,128)} %partner_ref.1) | copy-start | bytes 40
  25.2 1.6 %collective-permute-start.10 = (bf16[192,640]{1,0:T(8,128)(2,1)S(1)}, bf16[192,640]{1,0:T(8,128)(2,1)S(1)}, u32[]{:S(2)}, u32[]{:S(2)}) collective-permute-start(bf16[192,640]{1,0:T(8,128)(2,1)S(1)} %shard_map.76), channel_id=1, source_target_pairs={{0,1},{1,0},{2,3},{3,2},{4,5},{5,4},{6,7},{7,6},{8,9},{9,8},{10,11... | collective-permute-start | bytes 737288 | tf_op jit(solution)/shard_map/ppermute | solution.py:212
  29.3 4.7 %collective-permute-start.11 = (bf16[96,384]{1,0:T(8,128)(2,1)S(1)}, bf16[96,384]{1,0:T(8,128)(2,1)S(1)}, u32[]{:S(2)}, u32[]{:S(2)}) collective-permute-start(bf16[96,384]{1,0:T(8,128)(2,1)S(1)} %get-tuple-element.26), channel_id=1, source_target_pairs={{0,8},{8,0},{16,24},{24,16},{1,9},{9,1},{17,25},{25,17},{2,10},{10... | collective-permute-start | bytes 221192 | tf_op jit(solution)/shard_map/ppermute | solution.py:212
  29.9 5.9 %collective-permute-start.12 = (bf16[96,384]{1,0:T(8,128)(2,1)S(1)}, bf16[96,384]{1,0:T(8,128)(2,1)S(1)}, u32[]{:S(2)}, u32[]{:S(2)}) collective-permute-start(bf16[96,384]{1,0:T(8,128)(2,1)S(1)} %get-tuple-element.27), channel_id=1, source_target_pairs={{0,16},{8,24},{16,0},{24,8},{1,17},{9,25},{17,1},{25,9},{2,18},{10... | collective-permute-start | bytes 221192 | tf_op jit(solution)/shard_map/ppermute | solution.py:212
  30.4 5.4 %collective-permute-start.13 = (bf16[96,384]{1,0:T(8,128)(2,1)S(1)}, bf16[96,384]{1,0:T(8,128)(2,1)S(1)}, u32[]{:S(2)}, u32[]{:S(2)}) collective-permute-start(bf16[96,384]{1,0:T(8,128)(2,1)S(1)} %get-tuple-element.28), channel_id=1, source_target_pairs={{0,24},{8,16},{16,8},{24,0},{1,25},{9,17},{17,9},{25,1},{2,26},{10... | collective-permute-start | bytes 221192 | tf_op jit(solution)/shard_map/ppermute | solution.py:212

commit v3 on v2

--- a/solution.py
+++ b/solution.py
@@ -77,20 +77,26 @@
     ref[here, :MAIN], ref[here, MAIN : 2 * MAIN], ref[here, 2 * MAIN :] = parts
 
 
-def whiten_kernel(layout, shared, src_hbm, rec_hbm, tab_hbm, band_hbm, *rest):
+def whiten_kernel(layout, shared, src_hbm, rec_hbm, tab_hbm, band_hbm, lag_hbm, *rest):
     outs = rest[: len(layout)]
-    rec, tab, band, white, picked, sem = rest[len(layout) :]
+    lag, rec, tab, band, white, picked, sem = rest[len(layout) :]
     loads = [
         pltpu.make_async_copy(*pair, sem.at[i])
         for i, pair in enumerate(
-            [(rec_hbm.at[0], rec), (tab_hbm, tab), (src_hbm, picked), (band_hbm, band)]
+            [
+                (rec_hbm.at[0], rec),
+                (tab_hbm, tab),
+                (src_hbm, picked),
+                (band_hbm, band),
+                (lag_hbm, lag),
+            ]
         )
     ]
     for load in loads:
         load.start()
     loads[0].wait()
     signal = rec[...].astype(F32)
-    for load in loads[1:]:
+    for load in loads[1:-1]:
         load.wait()
     keep(white, slice(None), whiten(signal, tab, band))
     place = lax.axis_index("tm")
@@ -108,6 +114,7 @@
         if with_source:
             rows.append(source)
         out[...] = jnp.concatenate(rows, axis=0).astype(BF16)
+    loads[-1].wait()
 
 
 def gather_kernel(size, *refs):
@@ -131,14 +138,29 @@
     out[...] = jnp.concatenate(parts, axis=0).astype(BF16)
 
 
-def cross_kernel(count, windows, sources, size, parts, *refs):
-    src_refs = refs[:count]
-    rec_refs = refs[count : count + len(parts)]
-    lag_hbm = refs[count + len(parts)]
-    outs = refs[count + len(parts) + 1 : 2 * count + len(parts) + 1]
-    rec, src, stack, lag, sem = refs[2 * count + len(parts) + 1 :]
-    lag_load = pltpu.make_async_copy(lag_hbm, lag, sem)
-    lag_load.start()
+def cross_sums(count, windows, sources, size, src, rec, put):
+    step = 16 if size % 16 == 0 else 8
+    for b in range(count):
+        for s in range(sources):
+            for g in range(0, size, step):
+                totals = [0.0] * 4
+                for i, w in enumerate(windows):
+                    a = src[pl.ds((b * tms_of(src, count, sources) + w) * sources + s, 1), :]
+                    r = rec[pl.ds(i * size + g, step), :]
+                    a_re, a_im, a_tail = a[:, :MAIN], a[:, MAIN : 2 * MAIN], a[:, 2 * MAIN :]
+                    r_re, r_im = r[:, :MAIN], r[:, MAIN : 2 * MAIN]
+                    totals[0] += a_re * r_re + a_im * r_im
+                    totals[1] += a_re * r_im - a_im * r_re
+                    totals[2] += a_tail * r[:, 2 * MAIN : WIDTH]
+                    totals[3] += a_tail * r[:, WIDTH:]
+                put(pl.ds((b * sources + s) * size + g, step), jnp.concatenate(totals, axis=1))
+
+
+def tms_of(src, count, sources):
+    return src.shape[0] // (count * sources)
+
+
+def unpack_receivers(rec, rec_refs, parts, size):
     for ref, places in zip(rec_refs, parts):
         rows = ref[...].astype(F32)
         for w, start, place, length in places:
@@ -146,28 +168,37 @@
             here = pl.ds(w * size + place, length)
             rec[here, :WIDTH] = value
             rec[here, WIDTH:] = pltpu.roll(value[:, 2 * MAIN :], TAIL, 1)
-    per = windows * sources
-    for b in range(count):
-        src[pl.ds(b * per, per), :] = src_refs[b][...].astype(F32)
-    step = 16 if size % 16 == 0 else 8
-    for b in range(count):
-        for s in range(sources):
-            for g in range(0, size, step):
-                totals = [0.0] * 4
-                for w in range(windows):
-                    a = src[pl.ds(b * per + w * sources + s, 1), :]
-                    r = rec[pl.ds(w * size + g, step), :]
-                    a_re, a_im, a_tail = a[:, :MAIN], a[:, MAIN : 2 * MAIN], a[:, 2 * MAIN :]
-                    r_re, r_im = r[:, :MAIN], r[:, MAIN : 2 * MAIN]
-                    totals[0] += a_re * r_re + a_im * r_im
-                    totals[1] += a_re * r_im - a_im * r_re
-                    totals[2] += a_tail * r[:, 2 * MAIN : WIDTH]
-                    totals[3] += a_tail * r[:, WIDTH:]
-                stack[pl.ds((b * sources + s) * size + g, step), :] = jnp.concatenate(totals, axis=1)
+
+
+def here_kernel(count, windows, sources, size, parts, arrays, *refs):
+    src_refs, rec_refs = refs[:arrays], refs[arrays : arrays + len(parts)]
+    stack, src, rec = refs[arrays + len(parts) :]
+    start = 0
+    for ref in src_refs:
+        src[pl.ds(start, ref.shape[0]), :] = ref[...].astype(F32)
+        start += ref.shape[0]
+    unpack_receivers(rec, rec_refs, parts, size)
+
+    def put(here, value):
+        stack[here, :] = value
+
+    cross_sums(count, windows, sources, size, src, rec, put)
+
+
+def there_kernel(count, windows, sources, size, parts, half, src, *refs):
+    rec_refs = refs[: len(parts)]
+    lag = refs[len(parts)]
+    outs = refs[len(parts) + 1 : len(parts) + 1 + count]
+    rec, stack = refs[len(parts) + 1 + count :]
+    unpack_receivers(rec, rec_refs, parts, size)
+
+    def put(here, value):
+        stack[here, :] = half[here, :] + value
+
+    cross_sums(count, windows, sources, size, src, rec, put)
     cross = stack[...]
     high = cross.astype(BF16)
     low = (cross - high.astype(F32)).astype(BF16)
-    lag_load.wait()
     lag_high, lag_low = lag[: WIDTH + LANES], lag[WIDTH + LANES :]
     lagged = (
         jnp.dot(high, lag_high, preferred_element_type=F32)
@@ -178,17 +209,24 @@
         outs[b][...] = lagged[b * sources * size : (b + 1) * sources * size].astype(BF16)
 
 
-def finish_kernel(count, sources, partner_ref, counts_ref, *refs):
+def wanted_kernel(partner, live, _, wanted):
+    me = lax.axis_index("chan")
+    row_id = lax.broadcasted_iota(jnp.int32, wanted.shape, 0)
+    distance = jnp.full(wanted.shape, -1, jnp.int32)
+    for p in range(partner.shape[1]):
+        value = jnp.where(p < live[0], jnp.bitwise_xor(partner[0, p], me), -1)
+        distance = jnp.where(row_id == p, value, distance)
+    wanted[...] = distance
+
+
+def finish_kernel(order, slots, sources, wanted_ref, *refs):
     ins, out = refs[:-1], refs[-1]
-    me = lax.axis_index("chan")
-    slots = partner_ref.shape[1]
     size = out.shape[0]
     for p in range(slots):
-        wanted = jnp.bitwise_xor(partner_ref[0, p], me)
-        wanted = jnp.where(p < counts_ref[0], wanted, -1)
+        wanted = jnp.broadcast_to(wanted_ref[p : p + 1, :1], (1, 2 * HL))
         value = jnp.zeros((sources * size, 2 * HL), F32)
-        for e in range(count):
-            value = jnp.where(wanted == e, ins[e][...].astype(F32), value)
+        for e, ref in zip(order, ins):
+            value = jnp.where(wanted == e, ref[...].astype(F32), value)
         for s in range(sources):
             out[:, p, s, :] = value[s * size : (s + 1) * size]
 
@@ -224,26 +262,31 @@
     table, band = dft_half(), band_table()
     first = 16
     rest = shared - first
-    layout = [(d, 0, first, True) for d in range(zs)]
-    layout += [(d, first, rest, False) for d in range(zs)]
+    order = sorted(range(zs), key=lambda d: (d == 1, d))
+    layout = [(d, 0, first, True) for d in order]
+    layout += [(d, first, rest, False) for d in order]
     rows = [2 * n + (SRC_ROWS if src else 0) for _, _, n, src in layout]
-    sent = call(
+    lags = lag_tables(1.0 / math.sqrt(F * tms))
+    *sent, lags = call(
         functools.partial(whiten_kernel, layout, shared),
-        [shape((n, WIDTH), BF16) for n in rows],
+        [shape((n, WIDTH), BF16) for n in rows] + [shape(lags.shape, BF16)],
         [
             pltpu.VMEM((channels, L), BF16),
             pltpu.VMEM(table.shape, BF16),
             pltpu.VMEM(band.shape, BF16),
             pltpu.VMEM((channels, WIDTH), F32),
             pltpu.SMEM(sources.shape, jnp.int32),
-            pltpu.SemaphoreType.DMA((4,)),
+            pltpu.SemaphoreType.DMA((5,)),
         ],
-        [hbm] * 4,
-        tuple(in_hbm(v) for v in (sources, records, jnp.asarray(table), jnp.asarray(band))),
+        [hbm] * 5,
+        (
+            *(in_hbm(value) for value in (sources, records)),
+            *(in_hbm(jnp.asarray(constant)) for constant in (table, band, lags)),
+        ),
     )
 
     def across(values):
-        return [v if d == 0 else swap(v, "tm", tms, 2 * d) for d, v in enumerate(values)]
+        return [v if d == 0 else swap(v, "tm", tms, 2 * d) for d, v in zip(order, values)]
 
     one, two = across(sent[:zs]), across(sent[zs:])
     gathered = call(
@@ -261,8 +304,9 @@
         [vmem] * 2,
         [gathered, other_one],
     )
-    spectra = [own] + [swap(own, "chan", chans, e) for e in range(1, chans)]
-    deps = spectra[1:]
+    blocks = list(reversed(range(chans)))
+    spectra = [own if e == 0 else swap(own, "chan", chans, e) for e in blocks]
+    deps = spectra[:-1]
     gathered = call(
         functools.partial(hold_kernel, first, rest, zs),
         shape((zs * shared, WIDTH), BF16),
@@ -276,32 +320,45 @@
         if size:
             receivers += values
             parts += [[(d, 0, start, size)] for d in range(zs)]
-    receivers.append(other_two)
-    places = [(zs + d, d * first, 0, first) for d in range(zs) if first]
-    places += [(zs + d, zs * first + d * rest, first, rest) for d in range(zs)]
-    parts.append(places)
-
-    lags = lag_tables(1.0 / math.sqrt(F * tms))
+    pairs = chans * picked * shared
+    half, src = call(
+        functools.partial(
+            here_kernel, chans, range(zs), picked, shared, parts, len(spectra)
+        ),
+        [shape((pairs, WIDTH + LANES), F32), shape((chans * tms * picked, WIDTH), F32)],
+        [pltpu.VMEM((zs * shared, WIDTH + LANES), F32)],
+        [vmem] * (len(spectra) + len(receivers)),
+        (*spectra, *receivers),
+    )
+    places = [(d, d * first, 0, first) for d in range(zs) if first]
+    places += [(d, zs * first + d * rest, first, rest) for d in range(zs)]
     done = call(
-        functools.partial(cross_kernel, chans, tms, picked, shared, parts),
+        functools.partial(there_kernel, chans, range(zs, tms), picked, shared, [places]),
         [shape((picked * shared, 2 * HL), BF16)] * chans,
         [
-            pltpu.VMEM((tms * shared, WIDTH + LANES), F32),
-            pltpu.VMEM((chans * tms * picked, WIDTH), F32),
-            pltpu.VMEM((chans * picked * shared, WIDTH + LANES), F32),
-            pltpu.VMEM(lags.shape, BF16),
-            pltpu.SemaphoreType.DMA,
+            pltpu.VMEM((zs * shared, WIDTH + LANES), F32),
+            pltpu.VMEM((pairs, WIDTH + LANES), F32),
         ],
-        [vmem] * (chans + len(receivers)) + [hbm],
-        (*spectra, *receivers, in_hbm(jnp.asarray(lags))),
-    )
-    arrived = [done[0]] + [swap(done[e], "chan", chans, e) for e in range(1, chans)]
+        [vmem] * 4,
+        (half, src, other_two, lags),
+    )
+    done = dict(zip(blocks, done))
+    ways = list(range(2, chans)) + [1, 0] if chans > 1 else [0]
+    arrived = [done[e] if e == 0 else swap(done[e], "chan", chans, e) for e in ways]
+    slots = partners.shape[1]
+    wanted = call(
+        wanted_kernel,
+        shape((-(-slots // 8) * 8, LANES), jnp.int32),
+        [],
+        [smem, smem, vmem],
+        (partners, counts, done[0]),
+    )
     result = call(
-        functools.partial(finish_kernel, chans, picked),
-        shape((shared, partners.shape[1], picked, 2 * HL), F32),
-        [],
-        [smem] * 2 + [vmem] * chans,
-        (partners, counts, *arrived),
+        functools.partial(finish_kernel, ways, slots, picked),
+        shape((shared, slots, picked, 2 * HL), F32),
+        [],
+        [vmem] * (1 + chans),
+        (wanted, *arrived),
     )
     return result[None]
 

time: 37.5 us -> 35.5 us (0.947); the launches traced: 37.4 us -> 34.9 us
  waiting for transfers between devices: 11.5 us -> 8.58 us
  starting transfers between devices: 17.2 us -> 18 us
    ppermute x14, waiting for transfers between devices: 11.5 us -> 8.58 us  [swap(): return lax.ppermute(value, axis, [(i, i ^ distance) for i in range(size)])]
    ppermute x14, starting transfers between devices: 17.2 us -> 18 us  [swap(): return lax.ppermute(value, axis, [(i, i ^ distance) for i in range(size)])]
    pallas_call x6 -> x8, Pallas kernels: 7.92 us -> 7.55 us  [call(): pl.pallas_call(kernel, out_shape=out_shape, in_specs=[pl.BlockSpec(memory...]
  transfers between devices with their start and end apart: 14 -> 14, of which waited for: 8 -> 7; matrix products, arithmetic and copies ran while one was open for 0% -> 0% of each run, Pallas kernels for 0% -> 3%
where the time goes in v3:
time: 35.5 us; the launch traced here: 34.9 us
  starting transfers between devices  18 us (51%)
  waiting for transfers between devices  8.58 us (24%)
  Pallas kernels  7.55 us (21%)
  between operations  0.74 us (2%)
    ppermute x14, starting transfers between devices, swap(): return lax.ppermute(value, axis, [(i, i ^ distance) for i in range(size)])  18 us
    ppermute x14, waiting for transfers between devices, swap(): return lax.ppermute(value, axis, [(i, i ^ distance) for i in range(size)])  8.58 us
    pallas_call x8, Pallas kernels, call(): pl.pallas_call(kernel, out_shape=out_shape, in_specs=[pl.BlockSpec(memory...  7.55 us
  transfers between devices with their start and end apart: 14, of which 7 were waited for; matrix products, arithmetic and copies ran while one was open for 0% of the time, Pallas kernels for 3%

profile of v3, /device:TPU:0, one launch (start us, length us, event | category | flops | bytes accessed | tf_op | source)
XLA Modules:
  0.0 34.9 jit_solution(15006760561776975303)
XLA Ops:
  0.0 3.9 %shard_map.73 = (bf16[40,640]{1,0:T(8,128)(2,1)S(1)}, bf16[40,640]{1,0:T(8,128)(2,1)S(1)}, bf16[40,640]{1,0:T(8,128)(2,1)S(1)}, bf16[40,640]{1,0:T(8,128)(2,1)S(...) custom-call(s32[1,2]{1,0:T(1,128)} %src_hbm.1, ...), custom_call_target="tpu_custom_call" | custom-call | tf_op jit(solution)/shard_map/pallas_call | solution.py:239
  3.9 4.1 %collective-permute-start = (bf16[40,640]{1,0:T(8,128)(2,1)S(1)}, bf16[40,640]{1,0:T(8,128)(2,1)S(1)}, u32[]{:S(2)}, u32[]{:S(2)}) collective-permute-start(bf16[40,640]{1,0:T(8,128)(2,1)S(1)} %get-tuple-element.21), channel_id=1, source_target_pairs={{0,4},{1,5},{2,6},{3,7},{4,0},{5,1},{6,2},{7,3},{8,12},{9,13},{10,... | collective-permute-start | bytes 153608 | tf_op jit(solution)/shard_map/ppermute | solution.py:250
  8.0 1.3 %collective-permute-start.1 = (bf16[40,640]{1,0:T(8,128)(2,1)S(1)}, bf16[40,640]{1,0:T(8,128)(2,1)S(1)}, u32[]{:S(2)}, u32[]{:S(2)}) collective-permute-start(bf16[40,640]{1,0:T(8,128)(2,1)S(1)} %get-tuple-element.22), channel_id=1, source_target_pairs={{0,6},{1,7},{2,4},{3,5},{4,2},{5,3},{6,0},{7,1},{8,14},{9,15},{10,... | collective-permute-start | bytes 153608 | tf_op jit(solution)/shard_map/ppermute | solution.py:250
  9.3 0.2 collective-permute-start.2
  9.6 2.8 %collective-permute-start.7 = (bf16[64,640]{1,0:T(8,128)(2,1)S(1)}, bf16[64,640]{1,0:T(8,128)(2,1)S(1)}, u32[]{:S(2)}, u32[]{:S(2)}) collective-permute-start(bf16[64,640]{1,0:T(8,128)(2,1)S(1)} %get-tuple-element.25), channel_id=1, source_target_pairs={{0,4},{1,5},{2,6},{3,7},{4,0},{5,1},{6,2},{7,3},{8,12},{9,13},{10,... | collective-permute-start | bytes 245768 | tf_op jit(solution)/shard_map/ppermute | solution.py:250
  12.4 1.3 %collective-permute-start.8 = (bf16[64,640]{1,0:T(8,128)(2,1)S(1)}, bf16[64,640]{1,0:T(8,128)(2,1)S(1)}, u32[]{:S(2)}, u32[]{:S(2)}) collective-permute-start(bf16[64,640]{1,0:T(8,128)(2,1)S(1)} %get-tuple-element.26), channel_id=1, source_target_pairs={{0,6},{1,7},{2,4},{3,5},{4,2},{5,3},{6,0},{7,1},{8,14},{9,15},{10,... | collective-permute-start | bytes 245768 | tf_op jit(solution)/shard_map/ppermute | solution.py:250
  13.7 0.8 %collective-permute-done.1.refs_2_.refs_6_ = bf16[40,640]{1,0:T(8,128)(2,1)S(1)} collective-permute-done((bf16[40,640]{1,0:T(8,128)(2,1)S(1)}, bf16[40,640]{1,0:T(8,128)(2,1)S(1)}, u32[]{:S(2)}, u32[]{:S(2)}) %collective-permute-start.1) | collective-permute-done | bytes 51232 | tf_op jit(solution)/shard_map/ppermute | solution.py:250
  14.6 0.1 collective-permute-start.3
  14.6 1.2 %collective-permute-done.3.there = bf16[32,640]{1,0:T(8,128)(2,1)S(1)} collective-permute-done((bf16[32,640]{1,0:T(8,128)(2,1)S(1)}, bf16[32,640]{1,0:T(8,128)(2,1)S(1)}, u32[]{:S(2)}, u32[]{:S(2)}) %collective-permute-start.3) | collective-permute-done | bytes 40992 | tf_op jit(solution)/shard_map/ppermute | solution.py:250
  15.9 2.5 %collective-permute-start.4 = (bf16[16,640]{1,0:T(8,128)(2,1)S(1)}, bf16[16,640]{1,0:T(8,128)(2,1)S(1)}, u32[]{:S(2)}, u32[]{:S(2)}) collective-permute-start(bf16[16,640]{1,0:T(8,128)(2,1)S(1)} %shard_map.75.refs_3_), channel_id=1, source_target_pairs={{0,24},{8,16},{16,8},{24,0},{1,25},{9,17},{17,9},{25,1},{2,26},{10... | collective-permute-start | bytes 61448 | tf_op jit(solution)/shard_map/ppermute | solution.py:250
  18.4 0.5 %collective-permute-start.5 = (bf16[16,640]{1,0:T(8,128)(2,1)S(1)}, bf16[16,640]{1,0:T(8,128)(2,1)S(1)}, u32[]{:S(2)}, u32[]{:S(2)}) collective-permute-start(bf16[16,640]{1,0:T(8,128)(2,1)S(1)} %shard_map.75.refs_3_), channel_id=1, source_target_pairs={{0,16},{8,24},{16,0},{24,8},{1,17},{9,25},{17,1},{25,9},{2,18},{10... | collective-permute-start | bytes 61448 | tf_op jit(solution)/shard_map/ppermute | solution.py:250
  18.9 0.6 %collective-permute-done.7.refs_9_.refs_5_ = bf16[64,640]{1,0:T(8,128)(2,1)S(1)} collective-permute-done((bf16[64,640]{1,0:T(8,128)(2,1)S(1)}, bf16[64,640]{1,0:T(8,128)(2,1)S(1)}, u32[]{:S(2)}, u32[]{:S(2)}) %collective-permute-start.7) | collective-permute-done | bytes 81952 | tf_op jit(solution)/shard_map/ppermute | solution.py:250
  19.5 1.5 %collective-permute-start.6 = (bf16[16,640]{1,0:T(8,128)(2,1)S(1)}, bf16[16,640]{1,0:T(8,128)(2,1)S(1)}, u32[]{:S(2)}, u32[]{:S(2)}) collective-permute-start(bf16[16,640]{1,0:T(8,128)(2,1)S(1)} %shard_map.75.refs_3_), channel_id=1, source_target_pairs={{0,8},{8,0},{16,24},{24,16},{1,9},{9,1},{17,25},{25,17},{2,10},{10... | collective-permute-start | bytes 61448 | tf_op jit(solution)/shard_map/ppermute | solution.py:250
  21.0 1.2 %collective-permute-done.5.refs_1_.refs_9_ = bf16[16,640]{1,0:T(8,128)(2,1)S(1)} collective-permute-done((bf16[16,640]{1,0:T(8,128)(2,1)S(1)}, bf16[16,640]{1,0:T(8,128)(2,1)S(1)}, u32[]{:S(2)}, u32[]{:S(2)}) %collective-permute-start.5) | collective-permute-done | bytes 20512 | tf_op jit(solution)/shard_map/ppermute | solution.py:250
  22.2 1.1 %collective-permute-done.6.refs_2_.refs_10_ = bf16[16,640]{1,0:T(8,128)(2,1)S(1)} collective-permute-done((bf16[16,640]{1,0:T(8,128)(2,1)S(1)}, bf16[16,640]{1,0:T(8,128)(2,1)S(1)}, u32[]{:S(2)}, u32[]{:S(2)}) %collective-permute-start.6) | collective-permute-done | bytes 20512 | tf_op jit(solution)/shard_map/ppermute | solution.py:250
  23.4 0.6 %shard_map.76 = (f32[384,768]{1,0:T(8,128)S(1)}, f32[64,640]{1,0:T(8,128)S(1)}) custom-call(bf16[16,640]{1,0:T(8,128)(2,1)S(1)} %collective-permute-done.4.refs_0_.refs_8_, bf16[16,640]{1,0:T(8,128)(2,1)S(1)} %collective-permute-done.5.refs_1_.refs_9_, bf16[16,640]{1,0:T(8,128)(2,1)S(1)} %collective-permute-done.6.refs_2_.refs_10_, ...), custom_call_target="tpu_custom_call" | custom-call | tf_op jit(solution)/shard_map/pallas_call | solution.py:239
  23.9 0.9 %collective-permute-done.10.refs_0_ = bf16[192,640]{1,0:T(8,128)(2,1)S(1)} collective-permute-done((bf16[192,640]{1,0:T(8,128)(2,1)S(1)}, bf16[192,640]{1,0:T(8,128)(2,1)S(1)}, u32[]{:S(2)}, u32[]{:S(2)}) %collective-permute-start.10) | collective-permute-done | bytes 245792 | tf_op jit(solution)/shard_map/ppermute | solution.py:250
  24.9 1.4 %shard_map.78 = (bf16[96,384]{1,0:T(8,128)(2,1)S(1)}, bf16[96,384]{1,0:T(8,128)(2,1)S(1)}, bf16[96,384]{1,0:T(8,128)(2,1)S(1)}, bf16[96,384]{1,0:T(8,128)(2,1)S(1)}) custom-call(f32[384,768]{1,0:T(8,128)S(1)} %get-tuple-element.28.half, f32[64,640]{1,0:T(8,128)S(1)} %get-tuple-element.29.src, bf16[192,640]{1,0:T(8,128)(2,1)S(1)} %collective-permute-done.10.refs_0_, ...), custom_call_target="tpu_custom_call" | custom-call | tf_op jit(solution)/shard_map/pallas_call | solution.py:239
  26.3 1.6 %collective-permute-start.11 = (bf16[96,384]{1,0:T(8,128)(2,1)S(1)}, bf16[96,384]{1,0:T(8,128)(2,1)S(1)}, u32[]{:S(2)}, u32[]{:S(2)}) collective-permute-start(bf16[96,384]{1,0:T(8,128)(2,1)S(1)} %get-tuple-element.32), channel_id=1, source_target_pairs={{0,16},{8,24},{16,0},{24,8},{1,17},{9,25},{17,1},{25,9},{2,18},{10... | collective-permute-start | bytes 221192 | tf_op jit(solution)/shard_map/ppermute | solution.py:250
  27.9 1.4 %collective-permute-start.12 = (bf16[96,384]{1,0:T(8,128)(2,1)S(1)}, bf16[96,384]{1,0:T(8,128)(2,1)S(1)}, u32[]{:S(2)}, u32[]{:S(2)}) collective-permute-start(bf16[96,384]{1,0:T(8,128)(2,1)S(1)} %get-tuple-element.33), channel_id=1, source_target_pairs={{0,24},{8,16},{16,8},{24,0},{1,25},{9,17},{17,9},{25,1},{2,26},{10... | collective-permute-start | bytes 221192 | tf_op jit(solution)/shard_map/ppermute | solution.py:250
  29.3 0.5 %collective-permute-start.13 = (bf16[96,384]{1,0:T(8,128)(2,1)S(1)}, bf16[96,384]{1,0:T(8,128)(2,1)S(1)}, u32[]{:S(2)}, u32[]{:S(2)}) collective-permute-start(bf16[96,384]{1,0:T(8,128)(2,1)S(1)} %get-tuple-element.34), channel_id=1, source_target_pairs={{0,8},{8,0},{16,24},{24,16},{1,9},{9,1},{17,25},{25,17},{2,10},{10... | collective-permute-start | bytes 221192 | tf_op jit(solution)/shard_map/ppermute | solution.py:250
  30.5 0.6 %shard_map.79.wanted_ref = s32[8,128]{1,0:T(8,128)S(1)} custom-call(s32[1,3]{1,0:T(1,128)S(1)} %copy-done, s32[1]{0:T(128)S(6)} %copy.8.live, bf16[96,384]{1,0:T(8,128)(2,1)S(1)} %get-tuple-element.31._.refs_3_), custom_call_target="tpu_custom_call" | custom-call | tf_op jit(solution)/shard_map/pallas_call | solution.py:239
  31.1 2.7 %collective-permute-done.12.refs_1_ = bf16[96,384]{1,0:T(8,128)(2,1)S(1)} collective-permute-done((bf16[96,384]{1,0:T(8,128)(2,1)S(1)}, bf16[96,384]{1,0:T(8,128)(2,1)S(1)}, u32[]{:S(2)}, u32[]{:S(2)}) %collective-permute-start.12) | collective-permute-done | bytes 73760 | tf_op jit(solution)/shard_map/ppermute | solution.py:250
  33.8 1.1 %shard_map.80 = f32[48,3,2,384]{3,2,1,0:T(2,128)} custom-call(s32[8,128]{1,0:T(8,128)S(1)} %shard_map.79.wanted_ref, bf16[96,384]{1,0:T(8,128)(2,1)S(1)} %collective-permute-done.11.refs_0_, bf16[96,384]{1,0:T(8,128)(2,1)S(1)} %collective-permute-done.12.refs_1_, bf16[96,384]{1,0:T(8,128)(2,1)S(1)} %collective-permute-done.13.refs_2_, ...), custom_call_target="tpu_custom_call" | custom-call | tf_op jit(solution)/shard_map/pallas_call | solution.py:239
  (14 shorter events, 0.1 us)
Async XLA Ops:
  3.9 9.8 %collective-permute-start = (bf16[40,640]{1,0:T(8,128)(2,1)S(1)}, bf16[40,640]{1,0:T(8,128)(2,1)S(1)}, u32[]{:S(2)}, u32[]{:S(2)}) collective-permute-start(bf16[40,640]{1,0:T(8,128)(2,1)S(1)} %get-tuple-element.21), channel_id=1, source_target_pairs={{0,4},{1,5},{2,6},{3,7},{4,0},{5,1},{6,2},{7,3},{8,12},{9,13},{10,... | collective-permute-start | bytes 153608 | tf_op jit(solution)/shard_map/ppermute | solution.py:250
  8.0 6.6 %collective-permute-start.1 = (bf16[40,640]{1,0:T(8,128)(2,1)S(1)}, bf16[40,640]{1,0:T(8,128)(2,1)S(1)}, u32[]{:S(2)}, u32[]{:S(2)}) collective-permute-start(bf16[40,640]{1,0:T(8,128)(2,1)S(1)} %get-tuple-element.22), channel_id=1, source_target_pairs={{0,6},{1,7},{2,4},{3,5},{4,2},{5,3},{6,0},{7,1},{8,14},{9,15},{10,... | collective-permute-start | bytes 153608 | tf_op jit(solution)/shard_map/ppermute | solution.py:250
  9.3 5.2 %collective-permute-start.2 = (bf16[40,640]{1,0:T(8,128)(2,1)S(1)}, bf16[40,640]{1,0:T(8,128)(2,1)S(1)}, u32[]{:S(2)}, u32[]{:S(2)}) collective-permute-start(bf16[40,640]{1,0:T(8,128)(2,1)S(1)} %get-tuple-element.23), channel_id=1, source_target_pairs={{0,2},{1,3},{2,0},{3,1},{4,6},{5,7},{6,4},{7,5},{8,10},{9,11},{10,... | collective-permute-start | bytes 153608 | tf_op jit(solution)/shard_map/ppermute | solution.py:250
  9.6 9.9 %collective-permute-start.7 = (bf16[64,640]{1,0:T(8,128)(2,1)S(1)}, bf16[64,640]{1,0:T(8,128)(2,1)S(1)}, u32[]{:S(2)}, u32[]{:S(2)}) collective-permute-start(bf16[64,640]{1,0:T(8,128)(2,1)S(1)} %get-tuple-element.25), channel_id=1, source_target_pairs={{0,4},{1,5},{2,6},{3,7},{4,0},{5,1},{6,2},{7,3},{8,12},{9,13},{10,... | collective-permute-start | bytes 245768 | tf_op jit(solution)/shard_map/ppermute | solution.py:250
  12.4 8.6 %collective-permute-start.8 = (bf16[64,640]{1,0:T(8,128)(2,1)S(1)}, bf16[64,640]{1,0:T(8,128)(2,1)S(1)}, u32[]{:S(2)}, u32[]{:S(2)}) collective-permute-start(bf16[64,640]{1,0:T(8,128)(2,1)S(1)} %get-tuple-element.26), channel_id=1, source_target_pairs={{0,6},{1,7},{2,4},{3,5},{4,2},{5,3},{6,0},{7,1},{8,14},{9,15},{10,... | collective-permute-start | bytes 245768 | tf_op jit(solution)/shard_map/ppermute | solution.py:250
  13.7 7.2 %collective-permute-start.9 = (bf16[64,640]{1,0:T(8,128)(2,1)S(1)}, bf16[64,640]{1,0:T(8,128)(2,1)S(1)}, u32[]{:S(2)}, u32[]{:S(2)}) collective-permute-start(bf16[64,640]{1,0:T(8,128)(2,1)S(1)} %get-tuple-element.27), channel_id=1, source_target_pairs={{0,2},{1,3},{2,0},{3,1},{4,6},{5,7},{6,4},{7,5},{8,10},{9,11},{10,... | collective-permute-start | bytes 245768 | tf_op jit(solution)/shard_map/ppermute | solution.py:250
  14.6 1.3 %collective-permute-start.3 = (bf16[32,640]{1,0:T(8,128)(2,1)S(1)}, bf16[32,640]{1,0:T(8,128)(2,1)S(1)}, u32[]{:S(2)}, u32[]{:S(2)}) collective-permute-start(bf16[32,640]{1,0:T(8,128)(2,1)S(1)} %shard_map.74.here), channel_id=1, source_target_pairs={{0,1},{1,0},{2,3},{3,2},{4,5},{5,4},{6,7},{7,6},{8,9},{9,8},{10,11... | collective-permute-start | bytes 122888 | tf_op jit(solution)/shard_map/ppermute | solution.py:250
  15.9 5.1 %collective-permute-start.4 = (bf16[16,640]{1,0:T(8,128)(2,1)S(1)}, bf16[16,640]{1,0:T(8,128)(2,1)S(1)}, u32[]{:S(2)}, u32[]{:S(2)}) collective-permute-start(bf16[16,640]{1,0:T(8,128)(2,1)S(1)} %shard_map.75.refs_3_), channel_id=1, source_target_pairs={{0,24},{8,16},{16,8},{24,0},{1,25},{9,17},{17,9},{25,1},{2,26},{10... | collective-permute-start | bytes 61448 | tf_op jit(solution)/shard_map/ppermute | solution.py:250
  18.4 3.8 %collective-permute-start.5 = (bf16[16,640]{1,0:T(8,128)(2,1)S(1)}, bf16[16,640]{1,0:T(8,128)(2,1)S(1)}, u32[]{:S(2)}, u32[]{:S(2)}) collective-permute-start(bf16[16,640]{1,0:T(8,128)(2,1)S(1)} %shard_map.75.refs_3_), channel_id=1, source_target_pairs={{0,16},{8,24},{16,0},{24,8},{1,17},{9,25},{17,1},{25,9},{2,18},{10... | collective-permute-start | bytes 61448 | tf_op jit(solution)/shard_map/ppermute | solution.py:250
  19.5 3.8 %collective-permute-start.6 = (bf16[16,640]{1,0:T(8,128)(2,1)S(1)}, bf16[16,640]{1,0:T(8,128)(2,1)S(1)}, u32[]{:S(2)}, u32[]{:S(2)}) collective-permute-start(bf16[16,640]{1,0:T(8,128)(2,1)S(1)} %shard_map.75.refs_3_), channel_id=1, source_target_pairs={{0,8},{8,0},{16,24},{24,16},{1,9},{9,1},{17,25},{25,17},{2,10},{10... | collective-permute-start | bytes 61448 | tf_op jit(solution)/shard_map/ppermute | solution.py:250
  23.3 1.6 %collective-permute-start.10 = (bf16[192,640]{1,0:T(8,128)(2,1)S(1)}, bf16[192,640]{1,0:T(8,128)(2,1)S(1)}, u32[]{:S(2)}, u32[]{:S(2)}) collective-permute-start(bf16[192,640]{1,0:T(8,128)(2,1)S(1)} %shard_map.77), channel_id=1, source_target_pairs={{0,1},{1,0},{2,3},{3,2},{4,5},{5,4},{6,7},{7,6},{8,9},{9,8},{10,11... | collective-permute-start | bytes 737288 | tf_op jit(solution)/shard_map/ppermute | solution.py:250
  24.9 5.6 %copy-start = (s32[1,3]{1,0:T(1,128)S(1)}, s32[1,3]{1,0:T(1,128)}, u32[]{:S(2)}) copy-start(s32[1,3]{1,0:T(1,128)} %partner.1) | copy-start | bytes 40
  26.3 4.8 %collective-permute-start.11 = (bf16[96,384]{1,0:T(8,128)(2,1)S(1)}, bf16[96,384]{1,0:T(8,128)(2,1)S(1)}, u32[]{:S(2)}, u32[]{:S(2)}) collective-permute-start(bf16[96,384]{1,0:T(8,128)(2,1)S(1)} %get-tuple-element.32), channel_id=1, source_target_pairs={{0,16},{8,24},{16,0},{24,8},{1,17},{9,25},{17,1},{25,9},{2,18},{10... | collective-permute-start | bytes 221192 | tf_op jit(solution)/shard_map/ppermute | solution.py:250
  27.9 5.9 %collective-permute-start.12 = (bf16[96,384]{1,0:T(8,128)(2,1)S(1)}, bf16[96,384]{1,0:T(8,128)(2,1)S(1)}, u32[]{:S(2)}, u32[]{:S(2)}) collective-permute-start(bf16[96,384]{1,0:T(8,128)(2,1)S(1)} %get-tuple-element.33), channel_id=1, source_target_pairs={{0,24},{8,16},{16,8},{24,0},{1,25},{9,17},{17,9},{25,1},{2,26},{10... | collective-permute-start | bytes 221192 | tf_op jit(solution)/shard_map/ppermute | solution.py:250
  29.3 4.5 %collective-permute-start.13 = (bf16[96,384]{1,0:T(8,128)(2,1)S(1)}, bf16[96,384]{1,0:T(8,128)(2,1)S(1)}, u32[]{:S(2)}, u32[]{:S(2)}) collective-permute-start(bf16[96,384]{1,0:T(8,128)(2,1)S(1)} %get-tuple-element.34), channel_id=1, source_target_pairs={{0,8},{8,0},{16,24},{24,16},{1,9},{9,1},{17,25},{25,17},{2,10},{10... | collective-permute-start | bytes 221192 | tf_op jit(solution)/shard_map/ppermute | solution.py:250

commit v4 on v3

--- a/solution.py
+++ b/solution.py
@@ -53,12 +53,11 @@
 
 
 def whiten(signal, tab, band):
-    rows = signal.shape[0]
     signal = (signal - jnp.sum(signal, axis=1, keepdims=True) * (1.0 / L)).astype(BF16)
-    halves = jnp.concatenate([signal[:, :HALF], signal[:, HALF:]], axis=0)
-    spec = jnp.dot(halves, tab[...], preferred_element_type=F32)
     lane = lax.broadcasted_iota(jnp.int32, (1, WIDTH), 1)
-    spec = spec[:rows] + jnp.where(lane % 2 == 1, 1.0, -1.0).astype(F32) * spec[rows:]
+    sign = jnp.where(lane % 2 == 1, 1.0, -1.0).astype(F32)
+    spec = jnp.dot(signal[:, :HALF], tab[...], preferred_element_type=F32)
+    spec = spec + sign * jnp.dot(signal[:, HALF:], tab[...], preferred_element_type=F32)
     re, im, tail = spec[:, :MAIN], spec[:, MAIN : 2 * MAIN], spec[:, 2 * MAIN :]
     tail_sq = tail * tail
     amp = jnp.sqrt(
@@ -109,44 +108,40 @@
         rows = []
         for q in range(2):
             owner = jnp.bitwise_xor(chip, d) * 2 + jnp.bitwise_xor(core, q)
-            if size:
-                rows.append(white[pl.ds(pl.multiple_of(owner * shared + first, 8), size), :])
+            rows.append(white[pl.ds(pl.multiple_of(owner * shared + first, 8), size), :])
         if with_source:
             rows.append(source)
         out[...] = jnp.concatenate(rows, axis=0).astype(BF16)
     loads[-1].wait()
 
 
-def gather_kernel(size, *refs):
+def pack_kernel(starts, sources, *refs):
     ins, out = refs[:-1], refs[-1]
-    parts = [ref[...].astype(F32)[2 * size :] for ref in ins]
+    parts = [ref[...].astype(F32)[start : start + sources] for ref, start in zip(ins, starts)]
+    spare = out.shape[0] - len(ins) * sources
+    if spare:
+        parts.append(jnp.zeros((spare, WIDTH), F32))
     out[...] = jnp.concatenate(parts, axis=0).astype(BF16)
 
 
-def hold_kernel(first, rest, count, *refs):
-    out = refs[-1]
-    parts = [ref[...].astype(F32)[first : 2 * first] for ref in refs[:count] if first]
-    parts += [ref[...].astype(F32)[rest:] for ref in refs[count : 2 * count]]
+def gather_kernel(sizes, *refs):
+    ins, out = refs[:-1], refs[-1]
+    count = len(sizes)
+    parts = [ref[...].astype(F32)[n : 2 * n] for ref, n in zip(ins, sizes)]
+    parts += [ref[...].astype(F32) for ref in ins[count:]]
     out[...] = jnp.concatenate(parts, axis=0).astype(BF16)
 
 
-def pack_kernel(start, sources, here, there, out):
-    parts = []
-    for ref in (here, there):
-        value = ref[...].astype(F32)[start:]
-        parts += [value[i : i + sources] for i in range(0, value.shape[0], SRC_ROWS)]
-    out[...] = jnp.concatenate(parts, axis=0).astype(BF16)
-
-
 def cross_sums(count, windows, sources, size, src, rec, put):
+    block = src.shape[0] // count
     step = 16 if size % 16 == 0 else 8
     for b in range(count):
         for s in range(sources):
             for g in range(0, size, step):
                 totals = [0.0] * 4
-                for i, w in enumerate(windows):
-                    a = src[pl.ds((b * tms_of(src, count, sources) + w) * sources + s, 1), :]
-                    r = rec[pl.ds(i * size + g, step), :]
+                for w in range(windows):
+                    a = src[pl.ds(b * block + w * sources + s, 1), :]
+                    r = rec[pl.ds(w * size + g, step), :]
                     a_re, a_im, a_tail = a[:, :MAIN], a[:, MAIN : 2 * MAIN], a[:, 2 * MAIN :]
                     r_re, r_im = r[:, :MAIN], r[:, MAIN : 2 * MAIN]
                     totals[0] += a_re * r_re + a_im * r_im
@@ -156,28 +151,19 @@
                 put(pl.ds((b * sources + s) * size + g, step), jnp.concatenate(totals, axis=1))
 
 
-def tms_of(src, count, sources):
-    return src.shape[0] // (count * sources)
-
-
-def unpack_receivers(rec, rec_refs, parts, size):
-    for ref, places in zip(rec_refs, parts):
-        rows = ref[...].astype(F32)
-        for w, start, place, length in places:
-            value = rows[start : start + length]
-            here = pl.ds(w * size + place, length)
-            rec[here, :WIDTH] = value
-            rec[here, WIDTH:] = pltpu.roll(value[:, 2 * MAIN :], TAIL, 1)
-
-
-def here_kernel(count, windows, sources, size, parts, arrays, *refs):
-    src_refs, rec_refs = refs[:arrays], refs[arrays : arrays + len(parts)]
-    stack, src, rec = refs[arrays + len(parts) :]
-    start = 0
-    for ref in src_refs:
-        src[pl.ds(start, ref.shape[0]), :] = ref[...].astype(F32)
-        start += ref.shape[0]
-    unpack_receivers(rec, rec_refs, parts, size)
+def put_receivers(rec, here, value):
+    rec[here, :WIDTH] = value
+    rec[here, WIDTH:] = pltpu.roll(value[:, 2 * MAIN :], TAIL, 1)
+
+
+def here_kernel(count, windows, sources, size, places, *refs):
+    rec_refs, src_refs = refs[: len(places)], refs[len(places) : len(places) + count]
+    stack, rec, src = refs[len(places) + count :]
+    for ref, (start, n) in zip(rec_refs, places):
+        put_receivers(rec, pl.ds(start, n), ref[...].astype(F32)[:n])
+    block = src.shape[0] // count
+    for b, ref in enumerate(src_refs):
+        src[pl.ds(b * block, block), :] = ref[...].astype(F32)
 
     def put(here, value):
         stack[here, :] = value
@@ -185,26 +171,28 @@
     cross_sums(count, windows, sources, size, src, rec, put)
 
 
-def there_kernel(count, windows, sources, size, parts, half, src, *refs):
-    rec_refs = refs[: len(parts)]
-    lag = refs[len(parts)]
-    outs = refs[len(parts) + 1 : len(parts) + 1 + count]
-    rec, stack = refs[len(parts) + 1 + count :]
-    unpack_receivers(rec, rec_refs, parts, size)
+def there_kernel(count, windows, sources, size, places, half, other, lag, *refs):
+    outs, (rec, src, stack) = refs[:count], refs[count:]
+    rows = other[...].astype(F32)
+    first = 0
+    for start, n in places:
+        put_receivers(rec, pl.ds(start, n), rows[first : first + n])
+        first += n
+    src[...] = rows[first:]
+
+    pairs = half.shape[0]
 
     def put(here, value):
-        stack[here, :] = half[here, :] + value
+        value = half[here, :] + value
+        high = value.astype(BF16)
+        stack[here, :] = high
+        stack[pl.ds(pairs + here.start, here.size), :] = (value - high.astype(F32)).astype(BF16)
 
     cross_sums(count, windows, sources, size, src, rec, put)
-    cross = stack[...]
-    high = cross.astype(BF16)
-    low = (cross - high.astype(F32)).astype(BF16)
     lag_high, lag_low = lag[: WIDTH + LANES], lag[WIDTH + LANES :]
-    lagged = (
-        jnp.dot(high, lag_high, preferred_element_type=F32)
-        + jnp.dot(low, lag_high, preferred_element_type=F32)
-        + jnp.dot(high, lag_low, preferred_element_type=F32)
-    )
+    both = jnp.dot(stack[...], lag_high, preferred_element_type=F32)
+    lagged = both[:pairs] + both[pairs:]
+    lagged = lagged + jnp.dot(stack[:pairs, :], lag_low, preferred_element_type=F32)
     for b in range(count):
         outs[b][...] = lagged[b * sources * size : (b + 1) * sources * size].astype(BF16)
 
@@ -260,12 +248,13 @@
     vmem, smem, hbm = pltpu.VMEM, pltpu.SMEM, pltpu.HBM
 
     table, band = dft_half(), band_table()
-    first = 16
-    rest = shared - first
-    order = sorted(range(zs), key=lambda d: (d == 1, d))
-    layout = [(d, 0, first, True) for d in order]
-    layout += [(d, first, rest, False) for d in order]
+    order = list(reversed(range(zs)))
+    first = {d: max(8, shared // 16 * 8) for d in order}
+    layout = [(d, 0, first[d], True) for d in order]
+    late = [*range(1, zs), 0]
+    layout += [(d, first[d], shared - first[d], False) for d in late]
     rows = [2 * n + (SRC_ROWS if src else 0) for _, _, n, src in layout]
+    places = [(order.index(d) * shared + row, n) for d, row, n, _ in layout]
     lags = lag_tables(1.0 / math.sqrt(F * tms))
     *sent, lags = call(
         functools.partial(whiten_kernel, layout, shared),
@@ -285,65 +274,46 @@
         ),
     )
 
-    def across(values):
-        return [v if d == 0 else swap(v, "tm", tms, 2 * d) for d, v in zip(order, values)]
-
-    one, two = across(sent[:zs]), across(sent[zs:])
-    gathered = call(
-        functools.partial(gather_kernel, first),
-        shape((zs * SRC_ROWS, WIDTH), BF16),
+    moved = [v if d == 0 else swap(v, "tm", tms, 2 * d) for (d, *_), v in zip(layout, sent)]
+    block = -(-zs * picked // SRC_ROWS) * SRC_ROWS
+    own = call(
+        functools.partial(pack_kernel, [2 * first[d] for d in order], picked),
+        shape((block, WIDTH), BF16),
         [],
         [vmem] * zs,
-        one,
-    )
-    other_one = swap(gathered, "tm", tms, 1)
-    own = call(
-        functools.partial(pack_kernel, 0, picked),
-        shape((tms * picked, WIDTH), BF16),
+        moved[:zs],
+    )
+    blocks = list(range(2, chans)) + [1, 0]
+    spectra = [own if e == 0 else swap(own, "chan", chans, e) for e in blocks]
+    gathered = call(
+        functools.partial(gather_kernel, [n for _, _, n, _ in layout]),
+        shape((zs * shared + chans * block, WIDTH), BF16),
         [],
-        [vmem] * 2,
-        [gathered, other_one],
-    )
-    blocks = list(reversed(range(chans)))
-    spectra = [own if e == 0 else swap(own, "chan", chans, e) for e in blocks]
-    deps = spectra[:-1]
-    gathered = call(
-        functools.partial(hold_kernel, first, rest, zs),
-        shape((zs * shared, WIDTH), BF16),
-        [],
-        [vmem] * (2 * zs + len(deps)),
-        one + two + deps,
-    )
-    other_two = swap(gathered, "tm", tms, 1)
-    receivers, parts = [], []
-    for values, start, size in ((one, 0, first), (two, first, rest)):
-        if size:
-            receivers += values
-            parts += [[(d, 0, start, size)] for d in range(zs)]
+        [vmem] * (len(moved) + chans),
+        moved + spectra,
+    )
+    other = swap(gathered, "tm", tms, 1)
     pairs = chans * picked * shared
-    half, src = call(
-        functools.partial(
-            here_kernel, chans, range(zs), picked, shared, parts, len(spectra)
-        ),
-        [shape((pairs, WIDTH + LANES), F32), shape((chans * tms * picked, WIDTH), F32)],
-        [pltpu.VMEM((zs * shared, WIDTH + LANES), F32)],
-        [vmem] * (len(spectra) + len(receivers)),
-        (*spectra, *receivers),
-    )
-    places = [(d, d * first, 0, first) for d in range(zs) if first]
-    places += [(d, zs * first + d * rest, first, rest) for d in range(zs)]
+    scratch = [
+        pltpu.VMEM((zs * shared, WIDTH + LANES), F32),
+        pltpu.VMEM((chans * block, WIDTH), F32),
+    ]
+    half = call(
+        functools.partial(here_kernel, chans, zs, picked, shared, places),
+        shape((pairs, WIDTH + LANES), F32),
+        scratch,
+        [vmem] * (len(moved) + chans),
+        moved + spectra,
+    )
     done = call(
-        functools.partial(there_kernel, chans, range(zs, tms), picked, shared, [places]),
+        functools.partial(there_kernel, chans, zs, picked, shared, places),
         [shape((picked * shared, 2 * HL), BF16)] * chans,
-        [
-            pltpu.VMEM((zs * shared, WIDTH + LANES), F32),
-            pltpu.VMEM((pairs, WIDTH + LANES), F32),
-        ],
-        [vmem] * 4,
-        (half, src, other_two, lags),
+        scratch + [pltpu.VMEM((2 * pairs, WIDTH + LANES), BF16)],
+        [vmem] * 3,
+        (half, other, lags),
     )
     done = dict(zip(blocks, done))
-    ways = list(range(2, chans)) + [1, 0] if chans > 1 else [0]
+    ways = list(reversed(range(chans)))
     arrived = [done[e] if e == 0 else swap(done[e], "chan", chans, e) for e in ways]
     slots = partners.shape[1]
     wanted = call(

time: 35.5 us -> 33.6 us (0.946); the launches traced: 34.9 us -> 33.4 us
  waiting for transfers between devices: 8.58 us -> 6.49 us
  starting transfers between devices: 18 us -> 19.2 us
  Pallas kernels: 7.55 us -> 7.01 us
    ppermute x14 -> x13, waiting for transfers between devices: 8.58 us -> 6.49 us  [swap(): return lax.ppermute(value, axis, [(i, i ^ distance) for i in range(size)])]
    ppermute x14 -> x13, starting transfers between devices: 18 us -> 19.2 us  [swap(): return lax.ppermute(value, axis, [(i, i ^ distance) for i in range(size)])]
    pallas_call x8 -> x7, Pallas kernels: 7.55 us -> 7.01 us  [call(): pl.pallas_call(kernel, out_shape=out_shape, in_specs=[pl.BlockSpec(memory...]
  transfers between devices with their start and end apart: 14 -> 13, of which waited for: 7 -> 9; matrix products, arithmetic and copies ran while one was open for 0% -> 0% of each run, Pallas kernels for 3% -> 3%
where the time goes in v4:
time: 33.6 us; the launch traced here: 33.4 us
  starting transfers between devices  19.2 us (57%)
  Pallas kernels  7.01 us (21%)
  waiting for transfers between devices  6.49 us (19%)
  between operations  0.72 us (2%)
    ppermute x13, starting transfers between devices, swap(): return lax.ppermute(value, axis, [(i, i ^ distance) for i in range(size)])  19.2 us
    pallas_call x7, Pallas kernels, call(): pl.pallas_call(kernel, out_shape=out_shape, in_specs=[pl.BlockSpec(memory...  7.01 us
    ppermute x13, waiting for transfers between devices, swap(): return lax.ppermute(value, axis, [(i, i ^ distance) for i in range(size)])  6.49 us
  transfers between devices with their start and end apart: 13, of which 9 were waited for; matrix products, arithmetic and copies ran while one was open for 0% of the time, Pallas kernels for 3%

profile of v4, /device:TPU:0, one launch (start us, length us, event | category | flops | bytes accessed | tf_op | source)
XLA Modules:
  0.0 33.4 jit_solution(2154371679552767980)
XLA Ops:
  0.0 3.4 %shard_map.73 = (bf16[56,640]{1,0:T(8,128)(2,1)S(1)}, bf16[56,640]{1,0:T(8,128)(2,1)S(1)}, bf16[56,640]{1,0:T(8,128)(2,1)S(1)}, bf16[56,640]{1,0:T(8,128)(2,1)S(...) custom-call(s32[1,2]{1,0:T(1,128)} %src_hbm.1, ...), custom_call_target="tpu_custom_call" | custom-call | tf_op jit(solution)/shard_map/pallas_call | solution.py:227
  3.5 5.1 %collective-permute-start = (bf16[56,640]{1,0:T(8,128)(2,1)S(1)}, bf16[56,640]{1,0:T(8,128)(2,1)S(1)}, u32[]{:S(2)}, u32[]{:S(2)}) collective-permute-start(bf16[56,640]{1,0:T(8,128)(2,1)S(1)} %get-tuple-element.18), channel_id=1, source_target_pairs={{0,6},{1,7},{2,4},{3,5},{4,2},{5,3},{6,0},{7,1},{8,14},{9,15},{10,... | collective-permute-start | bytes 215048 | tf_op jit(solution)/shard_map/ppermute | solution.py:238
  8.6 0.6 %collective-permute-start.2 = (bf16[56,640]{1,0:T(8,128)(2,1)S(1)}, bf16[56,640]{1,0:T(8,128)(2,1)S(1)}, u32[]{:S(2)}, u32[]{:S(2)}) collective-permute-start(bf16[56,640]{1,0:T(8,128)(2,1)S(1)} %get-tuple-element.20), channel_id=1, source_target_pairs={{0,2},{1,3},{2,0},{3,1},{4,6},{5,7},{6,4},{7,5},{8,10},{9,11},{10,... | collective-permute-start | bytes 215048 | tf_op jit(solution)/shard_map/ppermute | solution.py:238
  9.2 1.4 %collective-permute-start.3 = (bf16[48,640]{1,0:T(8,128)(2,1)S(1)}, bf16[48,640]{1,0:T(8,128)(2,1)S(1)}, u32[]{:S(2)}, u32[]{:S(2)}) collective-permute-start(bf16[48,640]{1,0:T(8,128)(2,1)S(1)} %get-tuple-element.22), channel_id=1, source_target_pairs={{0,2},{1,3},{2,0},{3,1},{4,6},{5,7},{6,4},{7,5},{8,10},{9,11},{10,... | collective-permute-start | bytes 184328 | tf_op jit(solution)/shard_map/ppermute | solution.py:238
  10.6 2.9 %collective-permute-start.4 = (bf16[48,640]{1,0:T(8,128)(2,1)S(1)}, bf16[48,640]{1,0:T(8,128)(2,1)S(1)}, u32[]{:S(2)}, u32[]{:S(2)}) collective-permute-start(bf16[48,640]{1,0:T(8,128)(2,1)S(1)} %get-tuple-element.23), channel_id=1, source_target_pairs={{0,4},{1,5},{2,6},{3,7},{4,0},{5,1},{6,2},{7,3},{8,12},{9,13},{10,... | collective-permute-start | bytes 184328 | tf_op jit(solution)/shard_map/ppermute | solution.py:238
  13.5 2.0 %collective-permute-start.5 = (bf16[48,640]{1,0:T(8,128)(2,1)S(1)}, bf16[48,640]{1,0:T(8,128)(2,1)S(1)}, u32[]{:S(2)}, u32[]{:S(2)}) collective-permute-start(bf16[48,640]{1,0:T(8,128)(2,1)S(1)} %get-tuple-element.24), channel_id=1, source_target_pairs={{0,6},{1,7},{2,4},{3,5},{4,2},{5,3},{6,0},{7,1},{8,14},{9,15},{10,... | collective-permute-start | bytes 184328 | tf_op jit(solution)/shard_map/ppermute | solution.py:238
  15.5 0.5 %collective-permute-done.1.refs_1_ = bf16[56,640]{1,0:T(8,128)(2,1)S(1)} collective-permute-done((bf16[56,640]{1,0:T(8,128)(2,1)S(1)}, bf16[56,640]{1,0:T(8,128)(2,1)S(1)}, u32[]{:S(2)}, u32[]{:S(2)}) %collective-permute-start.1) | collective-permute-done | bytes 71712 | tf_op jit(solution)/shard_map/ppermute | solution.py:238
  16.0 1.3 %collective-permute-start.6 = (bf16[8,640]{1,0:T(8,128)(2,1)S(1)}, bf16[8,640]{1,0:T(8,128)(2,1)S(1)}, u32[]{:S(2)}, u32[]{:S(2)}) collective-permute-start(bf16[8,640]{1,0:T(8,128)(2,1)S(1)} %shard_map.74.refs_11_), channel_id=1, source_target_pairs={{0,16},{8,24},{16,0},{24,8},{1,17},{9,25},{17,1},{25,9},{2,18},{10... | collective-permute-start | bytes 30728 | tf_op jit(solution)/shard_map/ppermute | solution.py:238
  17.3 1.4 %collective-permute-start.7 = (bf16[8,640]{1,0:T(8,128)(2,1)S(1)}, bf16[8,640]{1,0:T(8,128)(2,1)S(1)}, u32[]{:S(2)}, u32[]{:S(2)}) collective-permute-start(bf16[8,640]{1,0:T(8,128)(2,1)S(1)} %shard_map.74.refs_11_), channel_id=1, source_target_pairs={{0,24},{8,16},{16,8},{24,0},{1,25},{9,17},{17,9},{25,1},{2,26},{10... | collective-permute-start | bytes 30728 | tf_op jit(solution)/shard_map/ppermute | solution.py:238
  18.7 0.8 %collective-permute-start.8 = (bf16[8,640]{1,0:T(8,128)(2,1)S(1)}, bf16[8,640]{1,0:T(8,128)(2,1)S(1)}, u32[]{:S(2)}, u32[]{:S(2)}) collective-permute-start(bf16[8,640]{1,0:T(8,128)(2,1)S(1)} %shard_map.74.refs_11_), channel_id=1, source_target_pairs={{0,8},{8,0},{16,24},{24,16},{1,9},{9,1},{17,25},{25,17},{2,10},{10... | collective-permute-start | bytes 30728 | tf_op jit(solution)/shard_map/ppermute | solution.py:238
  19.6 0.1 collective-permute-done.5.refs_6_
  19.7 2.1 %collective-permute-done.7.refs_9_ = bf16[8,640]{1,0:T(8,128)(2,1)S(1)} collective-permute-done((bf16[8,640]{1,0:T(8,128)(2,1)S(1)}, bf16[8,640]{1,0:T(8,128)(2,1)S(1)}, u32[]{:S(2)}, u32[]{:S(2)}) %collective-permute-start.7) | collective-permute-done | bytes 10272 | tf_op jit(solution)/shard_map/ppermute | solution.py:238
  21.9 0.5 %collective-permute-done.8.refs_10_ = bf16[8,640]{1,0:T(8,128)(2,1)S(1)} collective-permute-done((bf16[8,640]{1,0:T(8,128)(2,1)S(1)}, bf16[8,640]{1,0:T(8,128)(2,1)S(1)}, u32[]{:S(2)}, u32[]{:S(2)}) %collective-permute-start.8) | collective-permute-done | bytes 10272 | tf_op jit(solution)/shard_map/ppermute | solution.py:238
  22.5 0.6 %shard_map.75.half = f32[384,768]{1,0:T(8,128)S(1)} custom-call(bf16[56,640]{1,0:T(8,128)(2,1)S(1)} %collective-permute-done.refs_0_, bf16[56,640]{1,0:T(8,128)(2,1)S(1)} %collective-permute-done.1.refs_1_, bf16[56,640]{1,0:T(8,128)(2,1)S(1)} %collective-permute-done.2.refs_2_, bf16[56,640]{1,0:T(8,128)(2,1)S(1)} %get-tuple-element.21.refs_3_, ...), custom_call_target="tpu_custom_call" | custom-call | tf_op jit(solution)/shard_map/pallas_call | solution.py:227
  23.1 1.0 %collective-permute-done.9.other = bf16[224,640]{1,0:T(8,128)(2,1)S(1)} collective-permute-done((bf16[224,640]{1,0:T(8,128)(2,1)S(1)}, bf16[224,640]{1,0:T(8,128)(2,1)S(1)}, u32[]{:S(2)}, u32[]{:S(2)}) %collective-permute-start.9) | collective-permute-done | bytes 286752 | tf_op jit(solution)/shard_map/ppermute | solution.py:238
  24.1 1.3 %shard_map.77 = (bf16[96,384]{1,0:T(8,128)(2,1)S(1)}, bf16[96,384]{1,0:T(8,128)(2,1)S(1)}, bf16[96,384]{1,0:T(8,128)(2,1)S(1)}, bf16[96,384]{1,0:T(8,128)(2,1)S(1)}) custom-call(f32[384,768]{1,0:T(8,128)S(1)} %shard_map.75.half, bf16[224,640]{1,0:T(8,128)(2,1)S(1)} %collective-permute-done.9.other, bf16[1536,384]{1,0:T(8,128)(2,1)S(1)} %get-tuple-element.26.lag), custom_call_target="tpu_custom_call" | custom-call | tf_op jit(solution)/shard_map/pallas_call | solution.py:227
  25.4 1.6 %collective-permute-start.10 = (bf16[96,384]{1,0:T(8,128)(2,1)S(1)}, bf16[96,384]{1,0:T(8,128)(2,1)S(1)}, u32[]{:S(2)}, u32[]{:S(2)}) collective-permute-start(bf16[96,384]{1,0:T(8,128)(2,1)S(1)} %get-tuple-element.28), channel_id=1, source_target_pairs={{0,24},{8,16},{16,8},{24,0},{1,25},{9,17},{17,9},{25,1},{2,26},{10... | collective-permute-start | bytes 221192 | tf_op jit(solution)/shard_map/ppermute | solution.py:238
  26.9 0.9 %collective-permute-start.11 = (bf16[96,384]{1,0:T(8,128)(2,1)S(1)}, bf16[96,384]{1,0:T(8,128)(2,1)S(1)}, u32[]{:S(2)}, u32[]{:S(2)}) collective-permute-start(bf16[96,384]{1,0:T(8,128)(2,1)S(1)} %get-tuple-element.29), channel_id=1, source_target_pairs={{0,16},{8,24},{16,0},{24,8},{1,17},{9,25},{17,1},{25,9},{2,18},{10... | collective-permute-start | bytes 221192 | tf_op jit(solution)/shard_map/ppermute | solution.py:238
  27.9 1.1 %collective-permute-start.12 = (bf16[96,384]{1,0:T(8,128)(2,1)S(1)}, bf16[96,384]{1,0:T(8,128)(2,1)S(1)}, u32[]{:S(2)}, u32[]{:S(2)}) collective-permute-start(bf16[96,384]{1,0:T(8,128)(2,1)S(1)} %get-tuple-element.30), channel_id=1, source_target_pairs={{0,8},{8,0},{16,24},{24,16},{1,9},{9,1},{17,25},{25,17},{2,10},{10... | collective-permute-start | bytes 221192 | tf_op jit(solution)/shard_map/ppermute | solution.py:238
  29.6 0.6 %shard_map.78.wanted_ref = s32[8,128]{1,0:T(8,128)S(1)} custom-call(s32[1,3]{1,0:T(1,128)S(1)} %copy-done, s32[1]{0:T(128)S(6)} %copy.8.live, bf16[96,384]{1,0:T(8,128)(2,1)S(1)} %get-tuple-element.27._.refs_3_), custom_call_target="tpu_custom_call" | custom-call | tf_op jit(solution)/shard_map/pallas_call | solution.py:227
  30.2 0.7 %collective-permute-done.10.refs_0_ = bf16[96,384]{1,0:T(8,128)(2,1)S(1)} collective-permute-done((bf16[96,384]{1,0:T(8,128)(2,1)S(1)}, bf16[96,384]{1,0:T(8,128)(2,1)S(1)}, u32[]{:S(2)}, u32[]{:S(2)}) %collective-permute-start.10) | collective-permute-done | bytes 73760 | tf_op jit(solution)/shard_map/ppermute | solution.py:238
  30.9 1.4 %collective-permute-done.11.refs_1_ = bf16[96,384]{1,0:T(8,128)(2,1)S(1)} collective-permute-done((bf16[96,384]{1,0:T(8,128)(2,1)S(1)}, bf16[96,384]{1,0:T(8,128)(2,1)S(1)}, u32[]{:S(2)}, u32[]{:S(2)}) %collective-permute-start.11) | collective-permute-done | bytes 73760 | tf_op jit(solution)/shard_map/ppermute | solution.py:238
  32.2 0.1 collective-permute-done.12.refs_2_
  32.3 1.1 %shard_map.79 = f32[48,3,2,384]{3,2,1,0:T(2,128)} custom-call(s32[8,128]{1,0:T(8,128)S(1)} %shard_map.78.wanted_ref, bf16[96,384]{1,0:T(8,128)(2,1)S(1)} %collective-permute-done.10.refs_0_, bf16[96,384]{1,0:T(8,128)(2,1)S(1)} %collective-permute-done.11.refs_1_, bf16[96,384]{1,0:T(8,128)(2,1)S(1)} %collective-permute-done.12.refs_2_, ...), custom_call_target="tpu_custom_call" | custom-call | tf_op jit(solution)/shard_map/pallas_call | solution.py:227
  (11 shorter events, 0.2 us)
Async XLA Ops:
  3.5 10.1 %collective-permute-start = (bf16[56,640]{1,0:T(8,128)(2,1)S(1)}, bf16[56,640]{1,0:T(8,128)(2,1)S(1)}, u32[]{:S(2)}, u32[]{:S(2)}) collective-permute-start(bf16[56,640]{1,0:T(8,128)(2,1)S(1)} %get-tuple-element.18), channel_id=1, source_target_pairs={{0,6},{1,7},{2,4},{3,5},{4,2},{5,3},{6,0},{7,1},{8,14},{9,15},{10,... | collective-permute-start | bytes 215048 | tf_op jit(solution)/shard_map/ppermute | solution.py:238
  8.6 7.4 %collective-permute-start.1 = (bf16[56,640]{1,0:T(8,128)(2,1)S(1)}, bf16[56,640]{1,0:T(8,128)(2,1)S(1)}, u32[]{:S(2)}, u32[]{:S(2)}) collective-permute-start(bf16[56,640]{1,0:T(8,128)(2,1)S(1)} %get-tuple-element.19), channel_id=1, source_target_pairs={{0,4},{1,5},{2,6},{3,7},{4,0},{5,1},{6,2},{7,3},{8,12},{9,13},{10,... | collective-permute-start | bytes 215048 | tf_op jit(solution)/shard_map/ppermute | solution.py:238
  8.6 7.4 %collective-permute-start.2 = (bf16[56,640]{1,0:T(8,128)(2,1)S(1)}, bf16[56,640]{1,0:T(8,128)(2,1)S(1)}, u32[]{:S(2)}, u32[]{:S(2)}) collective-permute-start(bf16[56,640]{1,0:T(8,128)(2,1)S(1)} %get-tuple-element.20), channel_id=1, source_target_pairs={{0,2},{1,3},{2,0},{3,1},{4,6},{5,7},{6,4},{7,5},{8,10},{9,11},{10,... | collective-permute-start | bytes 215048 | tf_op jit(solution)/shard_map/ppermute | solution.py:238
  9.2 9.5 %collective-permute-start.3 = (bf16[48,640]{1,0:T(8,128)(2,1)S(1)}, bf16[48,640]{1,0:T(8,128)(2,1)S(1)}, u32[]{:S(2)}, u32[]{:S(2)}) collective-permute-start(bf16[48,640]{1,0:T(8,128)(2,1)S(1)} %get-tuple-element.22), channel_id=1, source_target_pairs={{0,2},{1,3},{2,0},{3,1},{4,6},{5,7},{6,4},{7,5},{8,10},{9,11},{10,... | collective-permute-start | bytes 184328 | tf_op jit(solution)/shard_map/ppermute | solution.py:238
  10.6 9.0 %collective-permute-start.4 = (bf16[48,640]{1,0:T(8,128)(2,1)S(1)}, bf16[48,640]{1,0:T(8,128)(2,1)S(1)}, u32[]{:S(2)}, u32[]{:S(2)}) collective-permute-start(bf16[48,640]{1,0:T(8,128)(2,1)S(1)} %get-tuple-element.23), channel_id=1, source_target_pairs={{0,4},{1,5},{2,6},{3,7},{4,0},{5,1},{6,2},{7,3},{8,12},{9,13},{10,... | collective-permute-start | bytes 184328 | tf_op jit(solution)/shard_map/ppermute | solution.py:238
  13.5 6.1 %collective-permute-start.5 = (bf16[48,640]{1,0:T(8,128)(2,1)S(1)}, bf16[48,640]{1,0:T(8,128)(2,1)S(1)}, u32[]{:S(2)}, u32[]{:S(2)}) collective-permute-start(bf16[48,640]{1,0:T(8,128)(2,1)S(1)} %get-tuple-element.24), channel_id=1, source_target_pairs={{0,6},{1,7},{2,4},{3,5},{4,2},{5,3},{6,0},{7,1},{8,14},{9,15},{10,... | collective-permute-start | bytes 184328 | tf_op jit(solution)/shard_map/ppermute | solution.py:238
  16.0 3.7 %collective-permute-start.6 = (bf16[8,640]{1,0:T(8,128)(2,1)S(1)}, bf16[8,640]{1,0:T(8,128)(2,1)S(1)}, u32[]{:S(2)}, u32[]{:S(2)}) collective-permute-start(bf16[8,640]{1,0:T(8,128)(2,1)S(1)} %shard_map.74.refs_11_), channel_id=1, source_target_pairs={{0,16},{8,24},{16,0},{24,8},{1,17},{9,25},{17,1},{25,9},{2,18},{10... | collective-permute-start | bytes 30728 | tf_op jit(solution)/shard_map/ppermute | solution.py:238
  17.3 4.6 %collective-permute-start.7 = (bf16[8,640]{1,0:T(8,128)(2,1)S(1)}, bf16[8,640]{1,0:T(8,128)(2,1)S(1)}, u32[]{:S(2)}, u32[]{:S(2)}) collective-permute-start(bf16[8,640]{1,0:T(8,128)(2,1)S(1)} %shard_map.74.refs_11_), channel_id=1, source_target_pairs={{0,24},{8,16},{16,8},{24,0},{1,25},{9,17},{17,9},{25,1},{2,26},{10... | collective-permute-start | bytes 30728 | tf_op jit(solution)/shard_map/ppermute | solution.py:238
  18.7 3.7 %collective-permute-start.8 = (bf16[8,640]{1,0:T(8,128)(2,1)S(1)}, bf16[8,640]{1,0:T(8,128)(2,1)S(1)}, u32[]{:S(2)}, u32[]{:S(2)}) collective-permute-start(bf16[8,640]{1,0:T(8,128)(2,1)S(1)} %shard_map.74.refs_11_), channel_id=1, source_target_pairs={{0,8},{8,0},{16,24},{24,16},{1,9},{9,1},{17,25},{25,17},{2,10},{10... | collective-permute-start | bytes 30728 | tf_op jit(solution)/shard_map/ppermute | solution.py:238
  22.4 1.6 %collective-permute-start.9 = (bf16[224,640]{1,0:T(8,128)(2,1)S(1)}, bf16[224,640]{1,0:T(8,128)(2,1)S(1)}, u32[]{:S(2)}, u32[]{:S(2)}) collective-permute-start(bf16[224,640]{1,0:T(8,128)(2,1)S(1)} %shard_map.76), channel_id=1, source_target_pairs={{0,1},{1,0},{2,3},{3,2},{4,5},{5,4},{6,7},{7,6},{8,9},{9,8},{10,11... | collective-permute-start | bytes 860168 | tf_op jit(solution)/shard_map/ppermute | solution.py:238
  24.1 5.5 %copy-start = (s32[1,3]{1,0:T(1,128)S(1)}, s32[1,3]{1,0:T(1,128)}, u32[]{:S(2)}) copy-start(s32[1,3]{1,0:T(1,128)} %partner.1) | copy-start | bytes 40
  25.4 5.5 %collective-permute-start.10 = (bf16[96,384]{1,0:T(8,128)(2,1)S(1)}, bf16[96,384]{1,0:T(8,128)(2,1)S(1)}, u32[]{:S(2)}, u32[]{:S(2)}) collective-permute-start(bf16[96,384]{1,0:T(8,128)(2,1)S(1)} %get-tuple-element.28), channel_id=1, source_target_pairs={{0,24},{8,16},{16,8},{24,0},{1,25},{9,17},{17,9},{25,1},{2,26},{10... | collective-permute-start | bytes 221192 | tf_op jit(solution)/shard_map/ppermute | solution.py:238
  26.9 5.3 %collective-permute-start.11 = (bf16[96,384]{1,0:T(8,128)(2,1)S(1)}, bf16[96,384]{1,0:T(8,128)(2,1)S(1)}, u32[]{:S(2)}, u32[]{:S(2)}) collective-permute-start(bf16[96,384]{1,0:T(8,128)(2,1)S(1)} %get-tuple-element.29), channel_id=1, source_target_pairs={{0,16},{8,24},{16,0},{24,8},{1,17},{9,25},{17,1},{25,9},{2,18},{10... | collective-permute-start | bytes 221192 | tf_op jit(solution)/shard_map/ppermute | solution.py:238
  27.9 4.5 %collective-permute-start.12 = (bf16[96,384]{1,0:T(8,128)(2,1)S(1)}, bf16[96,384]{1,0:T(8,128)(2,1)S(1)}, u32[]{:S(2)}, u32[]{:S(2)}) collective-permute-start(bf16[96,384]{1,0:T(8,128)(2,1)S(1)} %get-tuple-element.30), channel_id=1, source_target_pairs={{0,8},{8,0},{16,24},{24,16},{1,9},{9,1},{17,25},{25,17},{2,10},{10... | collective-permute-start | bytes 221192 | tf_op jit(solution)/shard_map/ppermute | solution.py:238

commit v5 on v4

--- a/solution.py
+++ b/solution.py
@@ -158,17 +158,23 @@
 
 def here_kernel(count, windows, sources, size, places, *refs):
     rec_refs, src_refs = refs[: len(places)], refs[len(places) : len(places) + count]
-    stack, rec, src = refs[len(places) + count :]
+    lag, half, rec, src, stack = refs[len(places) + count :]
     for ref, (start, n) in zip(rec_refs, places):
         put_receivers(rec, pl.ds(start, n), ref[...].astype(F32)[:n])
     block = src.shape[0] // count
     for b, ref in enumerate(src_refs):
         src[pl.ds(b * block, block), :] = ref[...].astype(F32)
+    pairs = half.shape[0]
 
     def put(here, value):
-        stack[here, :] = value
+        high = value.astype(BF16)
+        stack[here, :] = high
+        stack[pl.ds(pairs + here.start, here.size), :] = (value - high.astype(F32)).astype(BF16)
 
     cross_sums(count, windows, sources, size, src, rec, put)
+    both = jnp.dot(stack[...], lag[: WIDTH + LANES], preferred_element_type=F32)
+    low = jnp.dot(stack[:pairs, :], lag[WIDTH + LANES :], preferred_element_type=F32)
+    half[...] = both[:pairs] + both[pairs:] + low
 
 
 def there_kernel(count, windows, sources, size, places, half, other, lag, *refs):
@@ -180,19 +186,11 @@
         first += n
     src[...] = rows[first:]
 
-    pairs = half.shape[0]
-
     def put(here, value):
-        value = half[here, :] + value
-        high = value.astype(BF16)
-        stack[here, :] = high
-        stack[pl.ds(pairs + here.start, here.size), :] = (value - high.astype(F32)).astype(BF16)
+        stack[here, :] = value.astype(BF16)
 
     cross_sums(count, windows, sources, size, src, rec, put)
-    lag_high, lag_low = lag[: WIDTH + LANES], lag[WIDTH + LANES :]
-    both = jnp.dot(stack[...], lag_high, preferred_element_type=F32)
-    lagged = both[:pairs] + both[pairs:]
-    lagged = lagged + jnp.dot(stack[:pairs, :], lag_low, preferred_element_type=F32)
+    lagged = half[...] + jnp.dot(stack[...], lag[: WIDTH + LANES], preferred_element_type=F32)
     for b in range(count):
         outs[b][...] = lagged[b * sources * size : (b + 1) * sources * size].astype(BF16)
 
@@ -300,15 +298,15 @@
     ]
     half = call(
         functools.partial(here_kernel, chans, zs, picked, shared, places),
-        shape((pairs, WIDTH + LANES), F32),
-        scratch,
-        [vmem] * (len(moved) + chans),
-        moved + spectra,
+        shape((pairs, 2 * HL), F32),
+        scratch + [pltpu.VMEM((2 * pairs, WIDTH + LANES), BF16)],
+        [vmem] * (len(moved) + chans + 1),
+        moved + spectra + [lags],
     )
     done = call(
         functools.partial(there_kernel, chans, zs, picked, shared, places),
         [shape((picked * shared, 2 * HL), BF16)] * chans,
-        scratch + [pltpu.VMEM((2 * pairs, WIDTH + LANES), BF16)],
+        scratch + [pltpu.VMEM((pairs, WIDTH + LANES), BF16)],
         [vmem] * 3,
         (half, other, lags),
     )

time: 33.6 us -> 33 us (0.982)
  waiting for transfers between devices: 6.49 us -> 5.85 us
    ppermute x13, waiting for transfers between devices: 6.49 us -> 5.85 us  [swap(): return lax.ppermute(value, axis, [(i, i ^ distance) for i in range(size)])]
  transfers between devices with their start and end apart: 13 -> 13, of which waited for: 9 -> 9; matrix products, arithmetic and copies ran while one was open for 0% -> 0% of each run, Pallas kernels for 3% -> 6%
where the time goes in v5:
time: 33 us; the launch traced here: 32.9 us
  starting transfers between devices  19.2 us (58%)
  Pallas kernels  7.1 us (22%)
  waiting for transfers between devices  5.85 us (18%)
  between operations  0.73 us (2%)
    ppermute x13, starting transfers between devices, swap(): return lax.ppermute(value, axis, [(i, i ^ distance) for i in range(size)])  19.2 us
    pallas_call x7, Pallas kernels, call(): pl.pallas_call(kernel, out_shape=out_shape, in_specs=[pl.BlockSpec(memory...  7.1 us
    ppermute x13, waiting for transfers between devices, swap(): return lax.ppermute(value, axis, [(i, i ^ distance) for i in range(size)])  5.85 us
  transfers between devices with their start and end apart: 13, of which 9 were waited for; matrix products, arithmetic and copies ran while one was open for 0% of the time, Pallas kernels for 6%

profile of v5, /device:TPU:0, one launch (start us, length us, event | category | flops | bytes accessed | tf_op | source)
XLA Modules:
  0.0 32.9 jit_solution(2957834566839982034)
XLA Ops:
  0.0 3.4 %shard_map.73 = (bf16[56,640]{1,0:T(8,128)(2,1)S(1)}, bf16[56,640]{1,0:T(8,128)(2,1)S(1)}, bf16[56,640]{1,0:T(8,128)(2,1)S(1)}, bf16[56,640]{1,0:T(8,128)(2,1)S(...) custom-call(s32[1,2]{1,0:T(1,128)} %src_hbm.1, ...), custom_call_target="tpu_custom_call" | custom-call | tf_op jit(solution)/shard_map/pallas_call | solution.py:225
  3.5 5.1 %collective-permute-start = (bf16[56,640]{1,0:T(8,128)(2,1)S(1)}, bf16[56,640]{1,0:T(8,128)(2,1)S(1)}, u32[]{:S(2)}, u32[]{:S(2)}) collective-permute-start(bf16[56,640]{1,0:T(8,128)(2,1)S(1)} %get-tuple-element.18), channel_id=1, source_target_pairs={{0,6},{1,7},{2,4},{3,5},{4,2},{5,3},{6,0},{7,1},{8,14},{9,15},{10,... | collective-permute-start | bytes 215048 | tf_op jit(solution)/shard_map/ppermute | solution.py:236
  8.6 0.6 %collective-permute-start.2 = (bf16[56,640]{1,0:T(8,128)(2,1)S(1)}, bf16[56,640]{1,0:T(8,128)(2,1)S(1)}, u32[]{:S(2)}, u32[]{:S(2)}) collective-permute-start(bf16[56,640]{1,0:T(8,128)(2,1)S(1)} %get-tuple-element.20), channel_id=1, source_target_pairs={{0,2},{1,3},{2,0},{3,1},{4,6},{5,7},{6,4},{7,5},{8,10},{9,11},{10,... | collective-permute-start | bytes 215048 | tf_op jit(solution)/shard_map/ppermute | solution.py:236
  9.2 1.4 %collective-permute-start.3 = (bf16[48,640]{1,0:T(8,128)(2,1)S(1)}, bf16[48,640]{1,0:T(8,128)(2,1)S(1)}, u32[]{:S(2)}, u32[]{:S(2)}) collective-permute-start(bf16[48,640]{1,0:T(8,128)(2,1)S(1)} %get-tuple-element.22), channel_id=1, source_target_pairs={{0,2},{1,3},{2,0},{3,1},{4,6},{5,7},{6,4},{7,5},{8,10},{9,11},{10,... | collective-permute-start | bytes 184328 | tf_op jit(solution)/shard_map/ppermute | solution.py:236
  10.6 2.9 %collective-permute-start.4 = (bf16[48,640]{1,0:T(8,128)(2,1)S(1)}, bf16[48,640]{1,0:T(8,128)(2,1)S(1)}, u32[]{:S(2)}, u32[]{:S(2)}) collective-permute-start(bf16[48,640]{1,0:T(8,128)(2,1)S(1)} %get-tuple-element.23), channel_id=1, source_target_pairs={{0,4},{1,5},{2,6},{3,7},{4,0},{5,1},{6,2},{7,3},{8,12},{9,13},{10,... | collective-permute-start | bytes 184328 | tf_op jit(solution)/shard_map/ppermute | solution.py:236
  13.5 2.0 %collective-permute-start.5 = (bf16[48,640]{1,0:T(8,128)(2,1)S(1)}, bf16[48,640]{1,0:T(8,128)(2,1)S(1)}, u32[]{:S(2)}, u32[]{:S(2)}) collective-permute-start(bf16[48,640]{1,0:T(8,128)(2,1)S(1)} %get-tuple-element.24), channel_id=1, source_target_pairs={{0,6},{1,7},{2,4},{3,5},{4,2},{5,3},{6,0},{7,1},{8,14},{9,15},{10,... | collective-permute-start | bytes 184328 | tf_op jit(solution)/shard_map/ppermute | solution.py:236
  15.5 0.5 %collective-permute-done.1.refs_1_ = bf16[56,640]{1,0:T(8,128)(2,1)S(1)} collective-permute-done((bf16[56,640]{1,0:T(8,128)(2,1)S(1)}, bf16[56,640]{1,0:T(8,128)(2,1)S(1)}, u32[]{:S(2)}, u32[]{:S(2)}) %collective-permute-start.1) | collective-permute-done | bytes 71712 | tf_op jit(solution)/shard_map/ppermute | solution.py:236
  16.0 1.3 %collective-permute-start.6 = (bf16[8,640]{1,0:T(8,128)(2,1)S(1)}, bf16[8,640]{1,0:T(8,128)(2,1)S(1)}, u32[]{:S(2)}, u32[]{:S(2)}) collective-permute-start(bf16[8,640]{1,0:T(8,128)(2,1)S(1)} %shard_map.74.refs_11_), channel_id=1, source_target_pairs={{0,16},{8,24},{16,0},{24,8},{1,17},{9,25},{17,1},{25,9},{2,18},{10... | collective-permute-start | bytes 30728 | tf_op jit(solution)/shard_map/ppermute | solution.py:236
  17.3 1.4 %collective-permute-start.7 = (bf16[8,640]{1,0:T(8,128)(2,1)S(1)}, bf16[8,640]{1,0:T(8,128)(2,1)S(1)}, u32[]{:S(2)}, u32[]{:S(2)}) collective-permute-start(bf16[8,640]{1,0:T(8,128)(2,1)S(1)} %shard_map.74.refs_11_), channel_id=1, source_target_pairs={{0,24},{8,16},{16,8},{24,0},{1,25},{9,17},{17,9},{25,1},{2,26},{10... | collective-permute-start | bytes 30728 | tf_op jit(solution)/shard_map/ppermute | solution.py:236
  18.7 0.8 %collective-permute-start.8 = (bf16[8,640]{1,0:T(8,128)(2,1)S(1)}, bf16[8,640]{1,0:T(8,128)(2,1)S(1)}, u32[]{:S(2)}, u32[]{:S(2)}) collective-permute-start(bf16[8,640]{1,0:T(8,128)(2,1)S(1)} %shard_map.74.refs_11_), channel_id=1, source_target_pairs={{0,8},{8,0},{16,24},{24,16},{1,9},{9,1},{17,25},{25,17},{2,10},{10... | collective-permute-start | bytes 30728 | tf_op jit(solution)/shard_map/ppermute | solution.py:236
  19.6 0.1 collective-permute-done.5.refs_6_
  19.7 0.1 collective-permute-done.6.refs_8_
  19.7 2.1 %collective-permute-done.7.refs_9_ = bf16[8,640]{1,0:T(8,128)(2,1)S(1)} collective-permute-done((bf16[8,640]{1,0:T(8,128)(2,1)S(1)}, bf16[8,640]{1,0:T(8,128)(2,1)S(1)}, u32[]{:S(2)}, u32[]{:S(2)}) %collective-permute-start.7) | collective-permute-done | bytes 10272 | tf_op jit(solution)/shard_map/ppermute | solution.py:236
  21.9 0.5 %collective-permute-done.8.refs_10_ = bf16[8,640]{1,0:T(8,128)(2,1)S(1)} collective-permute-done((bf16[8,640]{1,0:T(8,128)(2,1)S(1)}, bf16[8,640]{1,0:T(8,128)(2,1)S(1)}, u32[]{:S(2)}, u32[]{:S(2)}) %collective-permute-start.8) | collective-permute-done | bytes 10272 | tf_op jit(solution)/shard_map/ppermute | solution.py:236
  22.5 1.3 %shard_map.75.half = f32[384,384]{1,0:T(8,128)S(1)} custom-call(bf16[56,640]{1,0:T(8,128)(2,1)S(1)} %collective-permute-done.refs_0_, bf16[56,640]{1,0:T(8,128)(2,1)S(1)} %collective-permute-done.1.refs_1_, bf16[56,640]{1,0:T(8,128)(2,1)S(1)} %collective-permute-done.2.refs_2_, bf16[56,640]{1,0:T(8,128)(2,1)S(1)} %get-tuple-element.21.refs_3_, ...), custom_call_target="tpu_custom_call" | custom-call | tf_op jit(solution)/shard_map/pallas_call | solution.py:225
  23.8 0.3 collective-permute-done.9.other
  24.1 0.7 %shard_map.77 = (bf16[96,384]{1,0:T(8,128)(2,1)S(1)}, bf16[96,384]{1,0:T(8,128)(2,1)S(1)}, bf16[96,384]{1,0:T(8,128)(2,1)S(1)}, bf16[96,384]{1,0:T(8,128)(2,1)S(1)}) custom-call(f32[384,384]{1,0:T(8,128)S(1)} %shard_map.75.half, bf16[224,640]{1,0:T(8,128)(2,1)S(1)} %collective-permute-done.9.other, bf16[1536,384]{1,0:T(8,128)(2,1)S(1)} %get-tuple-element.26.refs_12_.lag), custom_call_target="tpu_custom_call" | custom-call | tf_op jit(solution)/shard_map/pallas_call | solution.py:225
  24.8 1.6 %collective-permute-start.10 = (bf16[96,384]{1,0:T(8,128)(2,1)S(1)}, bf16[96,384]{1,0:T(8,128)(2,1)S(1)}, u32[]{:S(2)}, u32[]{:S(2)}) collective-permute-start(bf16[96,384]{1,0:T(8,128)(2,1)S(1)} %get-tuple-element.28), channel_id=1, source_target_pairs={{0,24},{8,16},{16,8},{24,0},{1,25},{9,17},{17,9},{25,1},{2,26},{10... | collective-permute-start | bytes 221192 | tf_op jit(solution)/shard_map/ppermute | solution.py:236
  26.3 0.9 %collective-permute-start.11 = (bf16[96,384]{1,0:T(8,128)(2,1)S(1)}, bf16[96,384]{1,0:T(8,128)(2,1)S(1)}, u32[]{:S(2)}, u32[]{:S(2)}) collective-permute-start(bf16[96,384]{1,0:T(8,128)(2,1)S(1)} %get-tuple-element.29), channel_id=1, source_target_pairs={{0,16},{8,24},{16,0},{24,8},{1,17},{9,25},{17,1},{25,9},{2,18},{10... | collective-permute-start | bytes 221192 | tf_op jit(solution)/shard_map/ppermute | solution.py:236
  27.3 1.1 %collective-permute-start.12 = (bf16[96,384]{1,0:T(8,128)(2,1)S(1)}, bf16[96,384]{1,0:T(8,128)(2,1)S(1)}, u32[]{:S(2)}, u32[]{:S(2)}) collective-permute-start(bf16[96,384]{1,0:T(8,128)(2,1)S(1)} %get-tuple-element.30), channel_id=1, source_target_pairs={{0,8},{8,0},{16,24},{24,16},{1,9},{9,1},{17,25},{25,17},{2,10},{10... | collective-permute-start | bytes 221192 | tf_op jit(solution)/shard_map/ppermute | solution.py:236
  29.0 0.6 %shard_map.78.wanted_ref = s32[8,128]{1,0:T(8,128)S(1)} custom-call(s32[1,3]{1,0:T(1,128)S(1)} %copy-done, s32[1]{0:T(128)S(6)} %copy.8.live, bf16[96,384]{1,0:T(8,128)(2,1)S(1)} %get-tuple-element.27._.refs_3_), custom_call_target="tpu_custom_call" | custom-call | tf_op jit(solution)/shard_map/pallas_call | solution.py:225
  29.6 0.7 %collective-permute-done.10.refs_0_ = bf16[96,384]{1,0:T(8,128)(2,1)S(1)} collective-permute-done((bf16[96,384]{1,0:T(8,128)(2,1)S(1)}, bf16[96,384]{1,0:T(8,128)(2,1)S(1)}, u32[]{:S(2)}, u32[]{:S(2)}) %collective-permute-start.10) | collective-permute-done | bytes 73760 | tf_op jit(solution)/shard_map/ppermute | solution.py:236
  30.3 1.5 %collective-permute-done.11.refs_1_ = bf16[96,384]{1,0:T(8,128)(2,1)S(1)} collective-permute-done((bf16[96,384]{1,0:T(8,128)(2,1)S(1)}, bf16[96,384]{1,0:T(8,128)(2,1)S(1)}, u32[]{:S(2)}, u32[]{:S(2)}) %collective-permute-start.11) | collective-permute-done | bytes 73760 | tf_op jit(solution)/shard_map/ppermute | solution.py:236
  31.8 1.1 %shard_map.79 = f32[48,3,2,384]{3,2,1,0:T(2,128)} custom-call(s32[8,128]{1,0:T(8,128)S(1)} %shard_map.78.wanted_ref, bf16[96,384]{1,0:T(8,128)(2,1)S(1)} %collective-permute-done.10.refs_0_, bf16[96,384]{1,0:T(8,128)(2,1)S(1)} %collective-permute-done.11.refs_1_, bf16[96,384]{1,0:T(8,128)(2,1)S(1)} %collective-permute-done.12.refs_2_, ...), custom_call_target="tpu_custom_call" | custom-call | tf_op jit(solution)/shard_map/pallas_call | solution.py:225
  (11 shorter events, 0.2 us)
Async XLA Ops:
  3.5 10.1 %collective-permute-start = (bf16[56,640]{1,0:T(8,128)(2,1)S(1)}, bf16[56,640]{1,0:T(8,128)(2,1)S(1)}, u32[]{:S(2)}, u32[]{:S(2)}) collective-permute-start(bf16[56,640]{1,0:T(8,128)(2,1)S(1)} %get-tuple-element.18), channel_id=1, source_target_pairs={{0,6},{1,7},{2,4},{3,5},{4,2},{5,3},{6,0},{7,1},{8,14},{9,15},{10,... | collective-permute-start | bytes 215048 | tf_op jit(solution)/shard_map/ppermute | solution.py:236
  8.6 7.4 %collective-permute-start.1 = (bf16[56,640]{1,0:T(8,128)(2,1)S(1)}, bf16[56,640]{1,0:T(8,128)(2,1)S(1)}, u32[]{:S(2)}, u32[]{:S(2)}) collective-permute-start(bf16[56,640]{1,0:T(8,128)(2,1)S(1)} %get-tuple-element.19), channel_id=1, source_target_pairs={{0,4},{1,5},{2,6},{3,7},{4,0},{5,1},{6,2},{7,3},{8,12},{9,13},{10,... | collective-permute-start | bytes 215048 | tf_op jit(solution)/shard_map/ppermute | solution.py:236
  8.6 7.4 %collective-permute-start.2 = (bf16[56,640]{1,0:T(8,128)(2,1)S(1)}, bf16[56,640]{1,0:T(8,128)(2,1)S(1)}, u32[]{:S(2)}, u32[]{:S(2)}) collective-permute-start(bf16[56,640]{1,0:T(8,128)(2,1)S(1)} %get-tuple-element.20), channel_id=1, source_target_pairs={{0,2},{1,3},{2,0},{3,1},{4,6},{5,7},{6,4},{7,5},{8,10},{9,11},{10,... | collective-permute-start | bytes 215048 | tf_op jit(solution)/shard_map/ppermute | solution.py:236
  9.2 9.5 %collective-permute-start.3 = (bf16[48,640]{1,0:T(8,128)(2,1)S(1)}, bf16[48,640]{1,0:T(8,128)(2,1)S(1)}, u32[]{:S(2)}, u32[]{:S(2)}) collective-permute-start(bf16[48,640]{1,0:T(8,128)(2,1)S(1)} %get-tuple-element.22), channel_id=1, source_target_pairs={{0,2},{1,3},{2,0},{3,1},{4,6},{5,7},{6,4},{7,5},{8,10},{9,11},{10,... | collective-permute-start | bytes 184328 | tf_op jit(solution)/shard_map/ppermute | solution.py:236
  10.6 9.0 %collective-permute-start.4 = (bf16[48,640]{1,0:T(8,128)(2,1)S(1)}, bf16[48,640]{1,0:T(8,128)(2,1)S(1)}, u32[]{:S(2)}, u32[]{:S(2)}) collective-permute-start(bf16[48,640]{1,0:T(8,128)(2,1)S(1)} %get-tuple-element.23), channel_id=1, source_target_pairs={{0,4},{1,5},{2,6},{3,7},{4,0},{5,1},{6,2},{7,3},{8,12},{9,13},{10,... | collective-permute-start | bytes 184328 | tf_op jit(solution)/shard_map/ppermute | solution.py:236
  13.5 6.1 %collective-permute-start.5 = (bf16[48,640]{1,0:T(8,128)(2,1)S(1)}, bf16[48,640]{1,0:T(8,128)(2,1)S(1)}, u32[]{:S(2)}, u32[]{:S(2)}) collective-permute-start(bf16[48,640]{1,0:T(8,128)(2,1)S(1)} %get-tuple-element.24), channel_id=1, source_target_pairs={{0,6},{1,7},{2,4},{3,5},{4,2},{5,3},{6,0},{7,1},{8,14},{9,15},{10,... | collective-permute-start | bytes 184328 | tf_op jit(solution)/shard_map/ppermute | solution.py:236
  16.0 3.7 %collective-permute-start.6 = (bf16[8,640]{1,0:T(8,128)(2,1)S(1)}, bf16[8,640]{1,0:T(8,128)(2,1)S(1)}, u32[]{:S(2)}, u32[]{:S(2)}) collective-permute-start(bf16[8,640]{1,0:T(8,128)(2,1)S(1)} %shard_map.74.refs_11_), channel_id=1, source_target_pairs={{0,16},{8,24},{16,0},{24,8},{1,17},{9,25},{17,1},{25,9},{2,18},{10... | collective-permute-start | bytes 30728 | tf_op jit(solution)/shard_map/ppermute | solution.py:236
  17.3 4.6 %collective-permute-start.7 = (bf16[8,640]{1,0:T(8,128)(2,1)S(1)}, bf16[8,640]{1,0:T(8,128)(2,1)S(1)}, u32[]{:S(2)}, u32[]{:S(2)}) collective-permute-start(bf16[8,640]{1,0:T(8,128)(2,1)S(1)} %shard_map.74.refs_11_), channel_id=1, source_target_pairs={{0,24},{8,16},{16,8},{24,0},{1,25},{9,17},{17,9},{25,1},{2,26},{10... | collective-permute-start | bytes 30728 | tf_op jit(solution)/shard_map/ppermute | solution.py:236
  18.7 3.7 %collective-permute-start.8 = (bf16[8,640]{1,0:T(8,128)(2,1)S(1)}, bf16[8,640]{1,0:T(8,128)(2,1)S(1)}, u32[]{:S(2)}, u32[]{:S(2)}) collective-permute-start(bf16[8,640]{1,0:T(8,128)(2,1)S(1)} %shard_map.74.refs_11_), channel_id=1, source_target_pairs={{0,8},{8,0},{16,24},{24,16},{1,9},{9,1},{17,25},{25,17},{2,10},{10... | collective-permute-start | bytes 30728 | tf_op jit(solution)/shard_map/ppermute | solution.py:236
  22.4 1.6 %collective-permute-start.9 = (bf16[224,640]{1,0:T(8,128)(2,1)S(1)}, bf16[224,640]{1,0:T(8,128)(2,1)S(1)}, u32[]{:S(2)}, u32[]{:S(2)}) collective-permute-start(bf16[224,640]{1,0:T(8,128)(2,1)S(1)} %shard_map.76), channel_id=1, source_target_pairs={{0,1},{1,0},{2,3},{3,2},{4,5},{5,4},{6,7},{7,6},{8,9},{9,8},{10,11... | collective-permute-start | bytes 860168 | tf_op jit(solution)/shard_map/ppermute | solution.py:236
  23.8 5.2 %copy-start = (s32[1,3]{1,0:T(1,128)S(1)}, s32[1,3]{1,0:T(1,128)}, u32[]{:S(2)}) copy-start(s32[1,3]{1,0:T(1,128)} %partner.1) | copy-start | bytes 40
  24.8 5.5 %collective-permute-start.10 = (bf16[96,384]{1,0:T(8,128)(2,1)S(1)}, bf16[96,384]{1,0:T(8,128)(2,1)S(1)}, u32[]{:S(2)}, u32[]{:S(2)}) collective-permute-start(bf16[96,384]{1,0:T(8,128)(2,1)S(1)} %get-tuple-element.28), channel_id=1, source_target_pairs={{0,24},{8,16},{16,8},{24,0},{1,25},{9,17},{17,9},{25,1},{2,26},{10... | collective-permute-start | bytes 221192 | tf_op jit(solution)/shard_map/ppermute | solution.py:236
  26.3 5.4 %collective-permute-start.11 = (bf16[96,384]{1,0:T(8,128)(2,1)S(1)}, bf16[96,384]{1,0:T(8,128)(2,1)S(1)}, u32[]{:S(2)}, u32[]{:S(2)}) collective-permute-start(bf16[96,384]{1,0:T(8,128)(2,1)S(1)} %get-tuple-element.29), channel_id=1, source_target_pairs={{0,16},{8,24},{16,0},{24,8},{1,17},{9,25},{17,1},{25,9},{2,18},{10... | collective-permute-start | bytes 221192 | tf_op jit(solution)/shard_map/ppermute | solution.py:236
  27.3 4.5 %collective-permute-start.12 = (bf16[96,384]{1,0:T(8,128)(2,1)S(1)}, bf16[96,384]{1,0:T(8,128)(2,1)S(1)}, u32[]{:S(2)}, u32[]{:S(2)}) collective-permute-start(bf16[96,384]{1,0:T(8,128)(2,1)S(1)} %get-tuple-element.30), channel_id=1, source_target_pairs={{0,8},{8,0},{16,24},{24,16},{1,9},{9,1},{17,25},{25,17},{2,10},{10... | collective-permute-start | bytes 221192 | tf_op jit(solution)/shard_map/ppermute | solution.py:236

commit v6 on v5

--- a/solution.py
+++ b/solution.py
@@ -33,14 +33,6 @@
     return table.astype(ml_dtypes.bfloat16)
 
 
-def band_table():
-    bins = np.concatenate([np.arange(F), np.arange(MAIN, F)])
-    centre = np.clip(bins, SMOOTH, F - 1 - SMOOTH)
-    band = np.abs(bins[:, None] - centre[None, :]) <= SMOOTH
-    band[F:] = False
-    return band.astype(ml_dtypes.bfloat16)
-
-
 def lag_tables(scale):
     k = np.arange(F)[:, None] + 1
     j = np.arange(2 * HL)[None, :] - HL
@@ -50,6 +42,15 @@
     high = table.astype(ml_dtypes.bfloat16)
     low = (table - high.astype(np.float32)).astype(ml_dtypes.bfloat16)
     return np.concatenate([high, low], axis=0)
+
+
+def band_matrix():
+    row = lax.broadcasted_iota(jnp.int32, (MAIN + 2 * TAIL, MAIN + 2 * TAIL), 0)
+    column = lax.broadcasted_iota(jnp.int32, (MAIN + 2 * TAIL, MAIN + 2 * TAIL), 1)
+    column = jnp.where(column >= F, column - TAIL, column)
+    centre = jnp.clip(column, SMOOTH, F - 1 - SMOOTH)
+    inside = (jnp.abs(row - centre) <= SMOOTH) & (row < F)
+    return jnp.where(inside, 1.0, 0.0).astype(BF16)
 
 
 def whiten(signal, tab, band):
@@ -76,7 +77,7 @@
     ref[here, :MAIN], ref[here, MAIN : 2 * MAIN], ref[here, 2 * MAIN :] = parts
 
 
-def whiten_kernel(layout, shared, src_hbm, rec_hbm, tab_hbm, band_hbm, lag_hbm, *rest):
+def whiten_kernel(layout, shared, src_hbm, rec_hbm, tab_hbm, lag_hbm, *rest):
     outs = rest[: len(layout)]
     lag, rec, tab, band, white, picked, sem = rest[len(layout) :]
     loads = [
@@ -86,13 +87,13 @@
                 (rec_hbm.at[0], rec),
                 (tab_hbm, tab),
                 (src_hbm, picked),
-                (band_hbm, band),
                 (lag_hbm, lag),
             ]
         )
     ]
     for load in loads:
         load.start()
+    band[...] = band_matrix()
     loads[0].wait()
     signal = rec[...].astype(F32)
     for load in loads[1:-1]:
@@ -206,27 +207,32 @@
 
 
 def finish_kernel(order, slots, sources, wanted_ref, *refs):
-    ins, out = refs[:-1], refs[-1]
+    ins, out, buffer, sem = refs[:-3], refs[-3], refs[-2], refs[-1]
     size = out.shape[0]
+    copies = []
     for p in range(slots):
         wanted = jnp.broadcast_to(wanted_ref[p : p + 1, :1], (1, 2 * HL))
-        value = jnp.zeros((sources * size, 2 * HL), F32)
-        for e, ref in zip(order, ins):
-            value = jnp.where(wanted == e, ref[...].astype(F32), value)
         for s in range(sources):
-            out[:, p, s, :] = value[s * size : (s + 1) * size]
+            value = jnp.zeros((size, 2 * HL), F32)
+            for e, ref in zip(order, ins):
+                value = jnp.where(wanted == e, ref[s * size : (s + 1) * size, :].astype(F32), value)
+            buffer[p, :, s, :] = value
+        copies.append(pltpu.make_async_copy(buffer.at[p], out.at[:, p], sem.at[p]))
+        copies[-1].start()
+    for copy in copies:
+        copy.wait()
 
 
 def in_hbm(value):
     return pltpu.with_memory_space_constraint(value, pltpu.HBM)
 
 
-def call(kernel, out_shape, scratch, spaces, args):
+def call(kernel, out_shape, scratch, spaces, args, out_space=pltpu.VMEM):
     return pl.pallas_call(
         kernel,
         out_shape=out_shape,
         in_specs=[pl.BlockSpec(memory_space=space) for space in spaces],
-        out_specs=jax.tree.map(lambda _: pl.BlockSpec(memory_space=pltpu.VMEM), out_shape),
+        out_specs=jax.tree.map(lambda _: pl.BlockSpec(memory_space=out_space), out_shape),
         scratch_shapes=scratch,
         compiler_params=pltpu.CompilerParams(vmem_limit_bytes=40 * 1024 * 1024),
     )(*args)
@@ -245,7 +251,7 @@
     shape = jax.ShapeDtypeStruct
     vmem, smem, hbm = pltpu.VMEM, pltpu.SMEM, pltpu.HBM
 
-    table, band = dft_half(), band_table()
+    table = dft_half()
     order = list(reversed(range(zs)))
     first = {d: max(8, shared // 16 * 8) for d in order}
     layout = [(d, 0, first[d], True) for d in order]
@@ -260,15 +266,15 @@
         [
             pltpu.VMEM((channels, L), BF16),
             pltpu.VMEM(table.shape, BF16),
-            pltpu.VMEM(band.shape, BF16),
+            pltpu.VMEM((MAIN + 2 * TAIL, MAIN + 2 * TAIL), BF16),
             pltpu.VMEM((channels, WIDTH), F32),
             pltpu.SMEM(sources.shape, jnp.int32),
             pltpu.SemaphoreType.DMA((5,)),
         ],
-        [hbm] * 5,
+        [hbm] * 4,
         (
             *(in_hbm(value) for value in (sources, records)),
-            *(in_hbm(jnp.asarray(constant)) for constant in (table, band, lags)),
+            *(in_hbm(jnp.asarray(constant)) for constant in (table, lags)),
         ),
     )
 
@@ -324,9 +330,13 @@
     result = call(
         functools.partial(finish_kernel, ways, slots, picked),
         shape((shared, slots, picked, 2 * HL), F32),
-        [],
+        [
+            pltpu.VMEM((slots, shared, picked, 2 * HL), F32),
+            pltpu.SemaphoreType.DMA((slots,)),
+        ],
         [vmem] * (1 + chans),
         (wanted, *arrived),
+        out_space=hbm,
     )
     return result[None]
 

time: 33 us -> 32.9 us (level)
  no operation moved by 1% of the time
where the time goes in v6:
time: 32.9 us; the launch traced here: 32.8 us
  starting transfers between devices  19.2 us (58%)
  Pallas kernels  6.97 us (21%)
  waiting for transfers between devices  5.85 us (18%)
  between operations  0.73 us (2%)
    ppermute x13, starting transfers between devices, swap(): return lax.ppermute(value, axis, [(i, i ^ distance) for i in range(size)])  19.2 us
    pallas_call x7, Pallas kernels, call(): pl.pallas_call(kernel, out_shape=out_shape, in_specs=[pl.BlockSpec(memory...  6.97 us
    ppermute x13, waiting for transfers between devices, swap(): return lax.ppermute(value, axis, [(i, i ^ distance) for i in range(size)])  5.85 us
  transfers between devices with their start and end apart: 13, of which 9 were waited for; matrix products, arithmetic and copies ran while one was open for 0% of the time, Pallas kernels for 6%

profile of v6, /device:TPU:0, one launch (start us, length us, event | category | flops | bytes accessed | tf_op | source)
XLA Modules:
  0.0 32.8 jit_solution(14198963494350832856)
XLA Ops:
  0.0 3.4 %shard_map.64 = (bf16[56,640]{1,0:T(8,128)(2,1)S(1)}, bf16[56,640]{1,0:T(8,128)(2,1)S(1)}, bf16[56,640]{1,0:T(8,128)(2,1)S(1)}, bf16[56,640]{1,0:T(8,128)(2,1)S(...) custom-call(s32[1,2]{1,0:T(1,128)} %src_hbm.1, ...), custom_call_target="tpu_custom_call" | custom-call | tf_op jit(solution)/shard_map/pallas_call | solution.py:231
  3.4 5.1 %collective-permute-start = (bf16[56,640]{1,0:T(8,128)(2,1)S(1)}, bf16[56,640]{1,0:T(8,128)(2,1)S(1)}, u32[]{:S(2)}, u32[]{:S(2)}) collective-permute-start(bf16[56,640]{1,0:T(8,128)(2,1)S(1)} %get-tuple-element.18), channel_id=1, source_target_pairs={{0,6},{1,7},{2,4},{3,5},{4,2},{5,3},{6,0},{7,1},{8,14},{9,15},{10,... | collective-permute-start | bytes 215048 | tf_op jit(solution)/shard_map/ppermute | solution.py:242
  8.5 0.6 %collective-permute-start.2 = (bf16[56,640]{1,0:T(8,128)(2,1)S(1)}, bf16[56,640]{1,0:T(8,128)(2,1)S(1)}, u32[]{:S(2)}, u32[]{:S(2)}) collective-permute-start(bf16[56,640]{1,0:T(8,128)(2,1)S(1)} %get-tuple-element.20), channel_id=1, source_target_pairs={{0,2},{1,3},{2,0},{3,1},{4,6},{5,7},{6,4},{7,5},{8,10},{9,11},{10,... | collective-permute-start | bytes 215048 | tf_op jit(solution)/shard_map/ppermute | solution.py:242
  9.2 1.4 %collective-permute-start.3 = (bf16[48,640]{1,0:T(8,128)(2,1)S(1)}, bf16[48,640]{1,0:T(8,128)(2,1)S(1)}, u32[]{:S(2)}, u32[]{:S(2)}) collective-permute-start(bf16[48,640]{1,0:T(8,128)(2,1)S(1)} %get-tuple-element.22), channel_id=1, source_target_pairs={{0,2},{1,3},{2,0},{3,1},{4,6},{5,7},{6,4},{7,5},{8,10},{9,11},{10,... | collective-permute-start | bytes 184328 | tf_op jit(solution)/shard_map/ppermute | solution.py:242
  10.6 2.9 %collective-permute-start.4 = (bf16[48,640]{1,0:T(8,128)(2,1)S(1)}, bf16[48,640]{1,0:T(8,128)(2,1)S(1)}, u32[]{:S(2)}, u32[]{:S(2)}) collective-permute-start(bf16[48,640]{1,0:T(8,128)(2,1)S(1)} %get-tuple-element.23), channel_id=1, source_target_pairs={{0,4},{1,5},{2,6},{3,7},{4,0},{5,1},{6,2},{7,3},{8,12},{9,13},{10,... | collective-permute-start | bytes 184328 | tf_op jit(solution)/shard_map/ppermute | solution.py:242
  13.5 2.0 %collective-permute-start.5 = (bf16[48,640]{1,0:T(8,128)(2,1)S(1)}, bf16[48,640]{1,0:T(8,128)(2,1)S(1)}, u32[]{:S(2)}, u32[]{:S(2)}) collective-permute-start(bf16[48,640]{1,0:T(8,128)(2,1)S(1)} %get-tuple-element.24), channel_id=1, source_target_pairs={{0,6},{1,7},{2,4},{3,5},{4,2},{5,3},{6,0},{7,1},{8,14},{9,15},{10,... | collective-permute-start | bytes 184328 | tf_op jit(solution)/shard_map/ppermute | solution.py:242
  15.4 0.5 %collective-permute-done.1.refs_1_ = bf16[56,640]{1,0:T(8,128)(2,1)S(1)} collective-permute-done((bf16[56,640]{1,0:T(8,128)(2,1)S(1)}, bf16[56,640]{1,0:T(8,128)(2,1)S(1)}, u32[]{:S(2)}, u32[]{:S(2)}) %collective-permute-start.1) | collective-permute-done | bytes 71712 | tf_op jit(solution)/shard_map/ppermute | solution.py:242
  15.9 1.3 %collective-permute-start.6 = (bf16[8,640]{1,0:T(8,128)(2,1)S(1)}, bf16[8,640]{1,0:T(8,128)(2,1)S(1)}, u32[]{:S(2)}, u32[]{:S(2)}) collective-permute-start(bf16[8,640]{1,0:T(8,128)(2,1)S(1)} %shard_map.65.refs_11_), channel_id=1, source_target_pairs={{0,16},{8,24},{16,0},{24,8},{1,17},{9,25},{17,1},{25,9},{2,18},{10... | collective-permute-start | bytes 30728 | tf_op jit(solution)/shard_map/ppermute | solution.py:242
  17.3 1.4 %collective-permute-start.7 = (bf16[8,640]{1,0:T(8,128)(2,1)S(1)}, bf16[8,640]{1,0:T(8,128)(2,1)S(1)}, u32[]{:S(2)}, u32[]{:S(2)}) collective-permute-start(bf16[8,640]{1,0:T(8,128)(2,1)S(1)} %shard_map.65.refs_11_), channel_id=1, source_target_pairs={{0,24},{8,16},{16,8},{24,0},{1,25},{9,17},{17,9},{25,1},{2,26},{10... | collective-permute-start | bytes 30728 | tf_op jit(solution)/shard_map/ppermute | solution.py:242
  18.7 0.8 %collective-permute-start.8 = (bf16[8,640]{1,0:T(8,128)(2,1)S(1)}, bf16[8,640]{1,0:T(8,128)(2,1)S(1)}, u32[]{:S(2)}, u32[]{:S(2)}) collective-permute-start(bf16[8,640]{1,0:T(8,128)(2,1)S(1)} %shard_map.65.refs_11_), channel_id=1, source_target_pairs={{0,8},{8,0},{16,24},{24,16},{1,9},{9,1},{17,25},{25,17},{2,10},{10... | collective-permute-start | bytes 30728 | tf_op jit(solution)/shard_map/ppermute | solution.py:242
  19.5 0.1 collective-permute-done.5.refs_6_
  19.6 0.1 collective-permute-done.6.refs_8_
  19.7 2.1 %collective-permute-done.7.refs_9_ = bf16[8,640]{1,0:T(8,128)(2,1)S(1)} collective-permute-done((bf16[8,640]{1,0:T(8,128)(2,1)S(1)}, bf16[8,640]{1,0:T(8,128)(2,1)S(1)}, u32[]{:S(2)}, u32[]{:S(2)}) %collective-permute-start.7) | collective-permute-done | bytes 10272 | tf_op jit(solution)/shard_map/ppermute | solution.py:242
  21.8 0.5 %collective-permute-done.8.refs_10_ = bf16[8,640]{1,0:T(8,128)(2,1)S(1)} collective-permute-done((bf16[8,640]{1,0:T(8,128)(2,1)S(1)}, bf16[8,640]{1,0:T(8,128)(2,1)S(1)}, u32[]{:S(2)}, u32[]{:S(2)}) %collective-permute-start.8) | collective-permute-done | bytes 10272 | tf_op jit(solution)/shard_map/ppermute | solution.py:242
  22.5 1.3 %shard_map.66.half = f32[384,384]{1,0:T(8,128)S(1)} custom-call(bf16[56,640]{1,0:T(8,128)(2,1)S(1)} %collective-permute-done.refs_0_, bf16[56,640]{1,0:T(8,128)(2,1)S(1)} %collective-permute-done.1.refs_1_, bf16[56,640]{1,0:T(8,128)(2,1)S(1)} %collective-permute-done.2.refs_2_, bf16[56,640]{1,0:T(8,128)(2,1)S(1)} %get-tuple-element.21.refs_3_, ...), custom_call_target="tpu_custom_call" | custom-call | tf_op jit(solution)/shard_map/pallas_call | solution.py:231
  23.8 0.3 collective-permute-done.9.other
  24.0 0.7 %shard_map.68 = (bf16[96,384]{1,0:T(8,128)(2,1)S(1)}, bf16[96,384]{1,0:T(8,128)(2,1)S(1)}, bf16[96,384]{1,0:T(8,128)(2,1)S(1)}, bf16[96,384]{1,0:T(8,128)(2,1)S(1)}) custom-call(f32[384,384]{1,0:T(8,128)S(1)} %shard_map.66.half, bf16[224,640]{1,0:T(8,128)(2,1)S(1)} %collective-permute-done.9.other, bf16[1536,384]{1,0:T(8,128)(2,1)S(1)} %get-tuple-element.26.refs_12_.lag), custom_call_target="tpu_custom_call" | custom-call | tf_op jit(solution)/shard_map/pallas_call | solution.py:231
  24.7 1.6 %collective-permute-start.10 = (bf16[96,384]{1,0:T(8,128)(2,1)S(1)}, bf16[96,384]{1,0:T(8,128)(2,1)S(1)}, u32[]{:S(2)}, u32[]{:S(2)}) collective-permute-start(bf16[96,384]{1,0:T(8,128)(2,1)S(1)} %get-tuple-element.28), channel_id=1, source_target_pairs={{0,24},{8,16},{16,8},{24,0},{1,25},{9,17},{17,9},{25,1},{2,26},{10... | collective-permute-start | bytes 221192 | tf_op jit(solution)/shard_map/ppermute | solution.py:242
  26.3 0.9 %collective-permute-start.11 = (bf16[96,384]{1,0:T(8,128)(2,1)S(1)}, bf16[96,384]{1,0:T(8,128)(2,1)S(1)}, u32[]{:S(2)}, u32[]{:S(2)}) collective-permute-start(bf16[96,384]{1,0:T(8,128)(2,1)S(1)} %get-tuple-element.29), channel_id=1, source_target_pairs={{0,16},{8,24},{16,0},{24,8},{1,17},{9,25},{17,1},{25,9},{2,18},{10... | collective-permute-start | bytes 221192 | tf_op jit(solution)/shard_map/ppermute | solution.py:242
  27.2 1.1 %collective-permute-start.12 = (bf16[96,384]{1,0:T(8,128)(2,1)S(1)}, bf16[96,384]{1,0:T(8,128)(2,1)S(1)}, u32[]{:S(2)}, u32[]{:S(2)}) collective-permute-start(bf16[96,384]{1,0:T(8,128)(2,1)S(1)} %get-tuple-element.30), channel_id=1, source_target_pairs={{0,8},{8,0},{16,24},{24,16},{1,9},{9,1},{17,25},{25,17},{2,10},{10... | collective-permute-start | bytes 221192 | tf_op jit(solution)/shard_map/ppermute | solution.py:242
  29.0 0.6 %shard_map.69.wanted_ref = s32[8,128]{1,0:T(8,128)S(1)} custom-call(s32[1,3]{1,0:T(1,128)S(1)} %copy-done, s32[1]{0:T(128)S(6)} %copy.7.live, bf16[96,384]{1,0:T(8,128)(2,1)S(1)} %get-tuple-element.27._.refs_3_), custom_call_target="tpu_custom_call" | custom-call | tf_op jit(solution)/shard_map/pallas_call | solution.py:231
  29.5 0.7 %collective-permute-done.10.refs_0_ = bf16[96,384]{1,0:T(8,128)(2,1)S(1)} collective-permute-done((bf16[96,384]{1,0:T(8,128)(2,1)S(1)}, bf16[96,384]{1,0:T(8,128)(2,1)S(1)}, u32[]{:S(2)}, u32[]{:S(2)}) %collective-permute-start.10) | collective-permute-done | bytes 73760 | tf_op jit(solution)/shard_map/ppermute | solution.py:242
  30.2 1.5 %collective-permute-done.11.refs_1_ = bf16[96,384]{1,0:T(8,128)(2,1)S(1)} collective-permute-done((bf16[96,384]{1,0:T(8,128)(2,1)S(1)}, bf16[96,384]{1,0:T(8,128)(2,1)S(1)}, u32[]{:S(2)}, u32[]{:S(2)}) %collective-permute-start.11) | collective-permute-done | bytes 73760 | tf_op jit(solution)/shard_map/ppermute | solution.py:242
  31.8 1.0 %shard_map.70 = f32[48,3,2,384]{3,2,1,0:T(2,128)} custom-call(s32[8,128]{1,0:T(8,128)S(1)} %shard_map.69.wanted_ref, bf16[96,384]{1,0:T(8,128)(2,1)S(1)} %collective-permute-done.10.refs_0_, bf16[96,384]{1,0:T(8,128)(2,1)S(1)} %collective-permute-done.11.refs_1_, bf16[96,384]{1,0:T(8,128)(2,1)S(1)} %collective-permute-done.12.refs_2_, ...), custom_call_target="tpu_custom_call" | custom-call | tf_op jit(solution)/shard_map/pallas_call | solution.py:231
  (11 shorter events, 0.2 us)
Async XLA Ops:
  3.4 10.1 %collective-permute-start = (bf16[56,640]{1,0:T(8,128)(2,1)S(1)}, bf16[56,640]{1,0:T(8,128)(2,1)S(1)}, u32[]{:S(2)}, u32[]{:S(2)}) collective-permute-start(bf16[56,640]{1,0:T(8,128)(2,1)S(1)} %get-tuple-element.18), channel_id=1, source_target_pairs={{0,6},{1,7},{2,4},{3,5},{4,2},{5,3},{6,0},{7,1},{8,14},{9,15},{10,... | collective-permute-start | bytes 215048 | tf_op jit(solution)/shard_map/ppermute | solution.py:242
  8.5 7.4 %collective-permute-start.1 = (bf16[56,640]{1,0:T(8,128)(2,1)S(1)}, bf16[56,640]{1,0:T(8,128)(2,1)S(1)}, u32[]{:S(2)}, u32[]{:S(2)}) collective-permute-start(bf16[56,640]{1,0:T(8,128)(2,1)S(1)} %get-tuple-element.19), channel_id=1, source_target_pairs={{0,4},{1,5},{2,6},{3,7},{4,0},{5,1},{6,2},{7,3},{8,12},{9,13},{10,... | collective-permute-start | bytes 215048 | tf_op jit(solution)/shard_map/ppermute | solution.py:242
  8.5 7.4 %collective-permute-start.2 = (bf16[56,640]{1,0:T(8,128)(2,1)S(1)}, bf16[56,640]{1,0:T(8,128)(2,1)S(1)}, u32[]{:S(2)}, u32[]{:S(2)}) collective-permute-start(bf16[56,640]{1,0:T(8,128)(2,1)S(1)} %get-tuple-element.20), channel_id=1, source_target_pairs={{0,2},{1,3},{2,0},{3,1},{4,6},{5,7},{6,4},{7,5},{8,10},{9,11},{10,... | collective-permute-start | bytes 215048 | tf_op jit(solution)/shard_map/ppermute | solution.py:242
  9.2 9.5 %collective-permute-start.3 = (bf16[48,640]{1,0:T(8,128)(2,1)S(1)}, bf16[48,640]{1,0:T(8,128)(2,1)S(1)}, u32[]{:S(2)}, u32[]{:S(2)}) collective-permute-start(bf16[48,640]{1,0:T(8,128)(2,1)S(1)} %get-tuple-element.22), channel_id=1, source_target_pairs={{0,2},{1,3},{2,0},{3,1},{4,6},{5,7},{6,4},{7,5},{8,10},{9,11},{10,... | collective-permute-start | bytes 184328 | tf_op jit(solution)/shard_map/ppermute | solution.py:242
  10.6 9.0 %collective-permute-start.4 = (bf16[48,640]{1,0:T(8,128)(2,1)S(1)}, bf16[48,640]{1,0:T(8,128)(2,1)S(1)}, u32[]{:S(2)}, u32[]{:S(2)}) collective-permute-start(bf16[48,640]{1,0:T(8,128)(2,1)S(1)} %get-tuple-element.23), channel_id=1, source_target_pairs={{0,4},{1,5},{2,6},{3,7},{4,0},{5,1},{6,2},{7,3},{8,12},{9,13},{10,... | collective-permute-start | bytes 184328 | tf_op jit(solution)/shard_map/ppermute | solution.py:242
  13.5 6.1 %collective-permute-start.5 = (bf16[48,640]{1,0:T(8,128)(2,1)S(1)}, bf16[48,640]{1,0:T(8,128)(2,1)S(1)}, u32[]{:S(2)}, u32[]{:S(2)}) collective-permute-start(bf16[48,640]{1,0:T(8,128)(2,1)S(1)} %get-tuple-element.24), channel_id=1, source_target_pairs={{0,6},{1,7},{2,4},{3,5},{4,2},{5,3},{6,0},{7,1},{8,14},{9,15},{10,... | collective-permute-start | bytes 184328 | tf_op jit(solution)/shard_map/ppermute | solution.py:242
  15.9 3.7 %collective-permute-start.6 = (bf16[8,640]{1,0:T(8,128)(2,1)S(1)}, bf16[8,640]{1,0:T(8,128)(2,1)S(1)}, u32[]{:S(2)}, u32[]{:S(2)}) collective-permute-start(bf16[8,640]{1,0:T(8,128)(2,1)S(1)} %shard_map.65.refs_11_), channel_id=1, source_target_pairs={{0,16},{8,24},{16,0},{24,8},{1,17},{9,25},{17,1},{25,9},{2,18},{10... | collective-permute-start | bytes 30728 | tf_op jit(solution)/shard_map/ppermute | solution.py:242
  17.3 4.6 %collective-permute-start.7 = (bf16[8,640]{1,0:T(8,128)(2,1)S(1)}, bf16[8,640]{1,0:T(8,128)(2,1)S(1)}, u32[]{:S(2)}, u32[]{:S(2)}) collective-permute-start(bf16[8,640]{1,0:T(8,128)(2,1)S(1)} %shard_map.65.refs_11_), channel_id=1, source_target_pairs={{0,24},{8,16},{16,8},{24,0},{1,25},{9,17},{17,9},{25,1},{2,26},{10... | collective-permute-start | bytes 30728 | tf_op jit(solution)/shard_map/ppermute | solution.py:242
  18.7 3.7 %collective-permute-start.8 = (bf16[8,640]{1,0:T(8,128)(2,1)S(1)}, bf16[8,640]{1,0:T(8,128)(2,1)S(1)}, u32[]{:S(2)}, u32[]{:S(2)}) collective-permute-start(bf16[8,640]{1,0:T(8,128)(2,1)S(1)} %shard_map.65.refs_11_), channel_id=1, source_target_pairs={{0,8},{8,0},{16,24},{24,16},{1,9},{9,1},{17,25},{25,17},{2,10},{10... | collective-permute-start | bytes 30728 | tf_op jit(solution)/shard_map/ppermute | solution.py:242
  22.4 1.6 %collective-permute-start.9 = (bf16[224,640]{1,0:T(8,128)(2,1)S(1)}, bf16[224,640]{1,0:T(8,128)(2,1)S(1)}, u32[]{:S(2)}, u32[]{:S(2)}) collective-permute-start(bf16[224,640]{1,0:T(8,128)(2,1)S(1)} %shard_map.67), channel_id=1, source_target_pairs={{0,1},{1,0},{2,3},{3,2},{4,5},{5,4},{6,7},{7,6},{8,9},{9,8},{10,11... | collective-permute-start | bytes 860168 | tf_op jit(solution)/shard_map/ppermute | solution.py:242
  23.7 5.2 %copy-start = (s32[1,3]{1,0:T(1,128)S(1)}, s32[1,3]{1,0:T(1,128)}, u32[]{:S(2)}) copy-start(s32[1,3]{1,0:T(1,128)} %partner.1) | copy-start | bytes 40
  24.7 5.5 %collective-permute-start.10 = (bf16[96,384]{1,0:T(8,128)(2,1)S(1)}, bf16[96,384]{1,0:T(8,128)(2,1)S(1)}, u32[]{:S(2)}, u32[]{:S(2)}) collective-permute-start(bf16[96,384]{1,0:T(8,128)(2,1)S(1)} %get-tuple-element.28), channel_id=1, source_target_pairs={{0,24},{8,16},{16,8},{24,0},{1,25},{9,17},{17,9},{25,1},{2,26},{10... | collective-permute-start | bytes 221192 | tf_op jit(solution)/shard_map/ppermute | solution.py:242
  26.3 5.4 %collective-permute-start.11 = (bf16[96,384]{1,0:T(8,128)(2,1)S(1)}, bf16[96,384]{1,0:T(8,128)(2,1)S(1)}, u32[]{:S(2)}, u32[]{:S(2)}) collective-permute-start(bf16[96,384]{1,0:T(8,128)(2,1)S(1)} %get-tuple-element.29), channel_id=1, source_target_pairs={{0,16},{8,24},{16,0},{24,8},{1,17},{9,25},{17,1},{25,9},{2,18},{10... | collective-permute-start | bytes 221192 | tf_op jit(solution)/shard_map/ppermute | solution.py:242
  27.2 4.5 %collective-permute-start.12 = (bf16[96,384]{1,0:T(8,128)(2,1)S(1)}, bf16[96,384]{1,0:T(8,128)(2,1)S(1)}, u32[]{:S(2)}, u32[]{:S(2)}) collective-permute-start(bf16[96,384]{1,0:T(8,128)(2,1)S(1)} %get-tuple-element.30), channel_id=1, source_target_pairs={{0,8},{8,0},{16,24},{24,16},{1,9},{9,1},{17,25},{25,17},{2,10},{10... | collective-permute-start | bytes 221192 | tf_op jit(solution)/shard_map/ppermute | solution.py:242

commit v7 on v6

--- a/solution.py
+++ b/solution.py
@@ -20,6 +20,7 @@
 WIDTH = 2 * F
 HALF = L // 2
 SRC_ROWS = 8
+PIECES = 1
 F32 = jnp.float32
 BF16 = jnp.bfloat16
 
@@ -54,7 +55,6 @@
 
 
 def whiten(signal, tab, band):
-    signal = (signal - jnp.sum(signal, axis=1, keepdims=True) * (1.0 / L)).astype(BF16)
     lane = lax.broadcasted_iota(jnp.int32, (1, WIDTH), 1)
     sign = jnp.where(lane % 2 == 1, 1.0, -1.0).astype(F32)
     spec = jnp.dot(signal[:, :HALF], tab[...], preferred_element_type=F32)
@@ -80,11 +80,13 @@
 def whiten_kernel(layout, shared, src_hbm, rec_hbm, tab_hbm, lag_hbm, *rest):
     outs = rest[: len(layout)]
     lag, rec, tab, band, white, picked, sem = rest[len(layout) :]
+    step = rec.shape[0] // PIECES
+    pieces = [pl.ds(i * step, step) for i in range(PIECES)]
     loads = [
         pltpu.make_async_copy(*pair, sem.at[i])
         for i, pair in enumerate(
             [
-                (rec_hbm.at[0], rec),
+                *[(rec_hbm.at[0, here], rec.at[here]) for here in pieces],
                 (tab_hbm, tab),
                 (src_hbm, picked),
                 (lag_hbm, lag),
@@ -94,11 +96,14 @@
     for load in loads:
         load.start()
     band[...] = band_matrix()
-    loads[0].wait()
-    signal = rec[...].astype(F32)
-    for load in loads[1:-1]:
+    for here, load in zip(pieces, loads):
         load.wait()
-    keep(white, slice(None), whiten(signal, tab, band))
+        signal = rec[here, :].astype(F32)
+        mean = jnp.sum(signal, axis=1, keepdims=True) * (1.0 / L)
+        rec[here, :] = (signal - mean).astype(BF16)
+    for load in loads[PIECES:-1]:
+        load.wait()
+    keep(white, slice(None), whiten(rec[...], tab, band))
     place = lax.axis_index("tm")
     chip, core = place // 2, lax.rem(place, 2)
     row_id = lax.broadcasted_iota(jnp.int32, (SRC_ROWS, WIDTH), 0)
@@ -133,10 +138,10 @@
     out[...] = jnp.concatenate(parts, axis=0).astype(BF16)
 
 
-def cross_sums(count, windows, sources, size, src, rec, put):
+def cross_sums(count, windows, sources, size, src, rec, put, blocks=None):
     block = src.shape[0] // count
     step = 16 if size % 16 == 0 else 8
-    for b in range(count):
+    for b in blocks or range(count):
         for s in range(sources):
             for g in range(0, size, step):
                 totals = [0.0] * 4
@@ -178,22 +183,34 @@
     half[...] = both[:pairs] + both[pairs:] + low
 
 
-def there_kernel(count, windows, sources, size, places, half, other, lag, *refs):
-    outs, (rec, src, stack) = refs[:count], refs[count:]
+def there_kernel(travel, windows, sources, size, places, half, other, lag, *refs):
+    outs, (rec, src, stack) = refs[: len(travel)], refs[len(travel) :]
     rows = other[...].astype(F32)
     first = 0
     for start, n in places:
         put_receivers(rec, pl.ds(start, n), rows[first : first + n])
         first += n
     src[...] = rows[first:]
-
-    def put(here, value):
-        stack[here, :] = value.astype(BF16)
-
-    cross_sums(count, windows, sources, size, src, rec, put)
-    lagged = half[...] + jnp.dot(stack[...], lag[: WIDTH + LANES], preferred_element_type=F32)
-    for b in range(count):
-        outs[b][...] = lagged[b * sources * size : (b + 1) * sources * size].astype(BF16)
+    lag_sums(travel, windows, sources, size, half, src, rec, lag, stack, outs)
+
+
+def stay_kernel(travel, windows, sources, size, half, rec, src, lag, _, out, stack):
+    lag_sums(travel, windows, sources, size, half, src, rec, lag, stack, [out])
+
+
+def lag_sums(blocks, windows, sources, size, half, src, rec, lag, stack, outs):
+    pairs = sources * size
+    count = half.shape[0] // pairs
+    for i, b in enumerate(blocks):
+
+        def put(here, value, i=i, b=b):
+            stack[pl.ds((i - b) * pairs + here.start, here.size), :] = value.astype(BF16)
+
+        cross_sums(count, windows, sources, size, src, rec, put, [b])
+    lagged = jnp.dot(stack[...], lag[: WIDTH + LANES], preferred_element_type=F32)
+    for i, (b, out) in enumerate(zip(blocks, outs)):
+        value = lagged[i * pairs : (i + 1) * pairs] + half[pl.ds(b * pairs, pairs), :]
+        out[...] = value.astype(BF16)
 
 
 def wanted_kernel(partner, live, _, wanted):
@@ -269,7 +286,7 @@
             pltpu.VMEM((MAIN + 2 * TAIL, MAIN + 2 * TAIL), BF16),
             pltpu.VMEM((channels, WIDTH), F32),
             pltpu.SMEM(sources.shape, jnp.int32),
-            pltpu.SemaphoreType.DMA((5,)),
+            pltpu.SemaphoreType.DMA((3 + PIECES,)),
         ],
         [hbm] * 4,
         (
@@ -309,14 +326,24 @@
         [vmem] * (len(moved) + chans + 1),
         moved + spectra + [lags],
     )
-    done = call(
-        functools.partial(there_kernel, chans, zs, picked, shared, places),
-        [shape((picked * shared, 2 * HL), BF16)] * chans,
-        scratch + [pltpu.VMEM((pairs, WIDTH + LANES), BF16)],
+    travel = [i for i, e in enumerate(blocks) if e]
+    results = [shape((picked * shared, 2 * HL), BF16)] * len(travel)
+    kept = [shape((zs * shared, WIDTH + LANES), F32), shape((chans * block, WIDTH), F32)]
+    *done, rec, src = call(
+        functools.partial(there_kernel, travel, zs, picked, shared, places),
+        results + kept,
+        [pltpu.VMEM((len(travel) * picked * shared, WIDTH + LANES), BF16)],
         [vmem] * 3,
         (half, other, lags),
     )
-    done = dict(zip(blocks, done))
+    done = {blocks[i]: value for i, value in zip(travel, done)}
+    done[0] = call(
+        functools.partial(stay_kernel, [blocks.index(0)], zs, picked, shared),
+        shape((picked * shared, 2 * HL), BF16),
+        [pltpu.VMEM((picked * shared, WIDTH + LANES), BF16)],
+        [vmem] * 5,
+        (half, rec, src, lags, done[1]),
+    )
     ways = list(reversed(range(chans)))
     arrived = [done[e] if e == 0 else swap(done[e], "chan", chans, e) for e in ways]
     slots = partners.shape[1]
@@ -325,7 +352,7 @@
         shape((-(-slots // 8) * 8, LANES), jnp.int32),
         [],
         [smem, smem, vmem],
-        (partners, counts, done[0]),
+        (partners, counts, done[1]),
     )
     result = call(
         functools.partial(finish_kernel, ways, slots, picked),

time: 32.9 us -> 32.7 us (level)
  waiting for transfers between devices: 5.85 us -> 5.2 us
  local copies, waits for them, and re-layouts: 0.01 us -> 0.35 us
    ppermute x13, waiting for transfers between devices: 5.85 us -> 5.2 us  [swap(): return lax.ppermute(value, axis, [(i, i ^ distance) for i in range(size)])]
    unnamed x2, local copies, waits for them, and re-layouts: 0.01 us -> 0.35 us
    pallas_call x7 -> x8, Pallas kernels: 6.97 us -> 7.09 us  [call(): pl.pallas_call(kernel, out_shape=out_shape, in_specs=[pl.BlockSpec(memory...]
  transfers between devices with their start and end apart: 13 -> 13, of which waited for: 9 -> 8; matrix products, arithmetic and copies ran while one was open for 0% -> 0% of each run, Pallas kernels for 6% -> 7%
where the time goes in v7:
time: 32.7 us; the launch traced here: 32.6 us
  starting transfers between devices  19.2 us (59%)
  Pallas kernels  7.09 us (22%)
  waiting for transfers between devices  5.2 us (16%)
  between operations  0.73 us (2%)
  local copies, waits for them, and re-layouts  0.35 us (1%)
    ppermute x13, starting transfers between devices, swap(): return lax.ppermute(value, axis, [(i, i ^ distance) for i in range(size)])  19.2 us
    pallas_call x8, Pallas kernels, call(): pl.pallas_call(kernel, out_shape=out_shape, in_specs=[pl.BlockSpec(memory...  7.09 us
    ppermute x13, waiting for transfers between devices, swap(): return lax.ppermute(value, axis, [(i, i ^ distance) for i in range(size)])  5.2 us
  transfers between devices with their start and end apart: 13, of which 8 were waited for; matrix products, arithmetic and copies ran while one was open for 0% of the time, Pallas kernels for 7%

profile of v7, /device:TPU:0, one launch (start us, length us, event | category | flops | bytes accessed | tf_op | source)
XLA Modules:
  0.0 32.6 jit_solution(10860246117861251207)
XLA Ops:
  0.0 3.3 %shard_map.64 = (bf16[56,640]{1,0:T(8,128)(2,1)S(1)}, bf16[56,640]{1,0:T(8,128)(2,1)S(1)}, bf16[56,640]{1,0:T(8,128)(2,1)S(1)}, bf16[56,640]{1,0:T(8,128)(2,1)S(...) custom-call(s32[1,2]{1,0:T(1,128)} %src_hbm.1, ...), custom_call_target="tpu_custom_call" | custom-call | tf_op jit(solution)/shard_map/pallas_call | solution.py:248
  3.3 5.1 %collective-permute-start = (bf16[56,640]{1,0:T(8,128)(2,1)S(1)}, bf16[56,640]{1,0:T(8,128)(2,1)S(1)}, u32[]{:S(2)}, u32[]{:S(2)}) collective-permute-start(bf16[56,640]{1,0:T(8,128)(2,1)S(1)} %get-tuple-element.19), channel_id=1, source_target_pairs={{0,6},{1,7},{2,4},{3,5},{4,2},{5,3},{6,0},{7,1},{8,14},{9,15},{10,... | collective-permute-start | bytes 215048 | tf_op jit(solution)/shard_map/ppermute | solution.py:259
  8.4 0.6 %collective-permute-start.2 = (bf16[56,640]{1,0:T(8,128)(2,1)S(1)}, bf16[56,640]{1,0:T(8,128)(2,1)S(1)}, u32[]{:S(2)}, u32[]{:S(2)}) collective-permute-start(bf16[56,640]{1,0:T(8,128)(2,1)S(1)} %get-tuple-element.21), channel_id=1, source_target_pairs={{0,2},{1,3},{2,0},{3,1},{4,6},{5,7},{6,4},{7,5},{8,10},{9,11},{10,... | collective-permute-start | bytes 215048 | tf_op jit(solution)/shard_map/ppermute | solution.py:259
  9.1 1.4 %collective-permute-start.3 = (bf16[48,640]{1,0:T(8,128)(2,1)S(1)}, bf16[48,640]{1,0:T(8,128)(2,1)S(1)}, u32[]{:S(2)}, u32[]{:S(2)}) collective-permute-start(bf16[48,640]{1,0:T(8,128)(2,1)S(1)} %get-tuple-element.23), channel_id=1, source_target_pairs={{0,2},{1,3},{2,0},{3,1},{4,6},{5,7},{6,4},{7,5},{8,10},{9,11},{10,... | collective-permute-start | bytes 184328 | tf_op jit(solution)/shard_map/ppermute | solution.py:259
  10.5 2.9 %collective-permute-start.4 = (bf16[48,640]{1,0:T(8,128)(2,1)S(1)}, bf16[48,640]{1,0:T(8,128)(2,1)S(1)}, u32[]{:S(2)}, u32[]{:S(2)}) collective-permute-start(bf16[48,640]{1,0:T(8,128)(2,1)S(1)} %get-tuple-element.24), channel_id=1, source_target_pairs={{0,4},{1,5},{2,6},{3,7},{4,0},{5,1},{6,2},{7,3},{8,12},{9,13},{10,... | collective-permute-start | bytes 184328 | tf_op jit(solution)/shard_map/ppermute | solution.py:259
  13.4 2.0 %collective-permute-start.5 = (bf16[48,640]{1,0:T(8,128)(2,1)S(1)}, bf16[48,640]{1,0:T(8,128)(2,1)S(1)}, u32[]{:S(2)}, u32[]{:S(2)}) collective-permute-start(bf16[48,640]{1,0:T(8,128)(2,1)S(1)} %get-tuple-element.25), channel_id=1, source_target_pairs={{0,6},{1,7},{2,4},{3,5},{4,2},{5,3},{6,0},{7,1},{8,14},{9,15},{10,... | collective-permute-start | bytes 184328 | tf_op jit(solution)/shard_map/ppermute | solution.py:259
  15.4 0.5 %collective-permute-done.1.refs_1_ = bf16[56,640]{1,0:T(8,128)(2,1)S(1)} collective-permute-done((bf16[56,640]{1,0:T(8,128)(2,1)S(1)}, bf16[56,640]{1,0:T(8,128)(2,1)S(1)}, u32[]{:S(2)}, u32[]{:S(2)}) %collective-permute-start.1) | collective-permute-done | bytes 71712 | tf_op jit(solution)/shard_map/ppermute | solution.py:259
  15.9 1.3 %collective-permute-start.6 = (bf16[8,640]{1,0:T(8,128)(2,1)S(1)}, bf16[8,640]{1,0:T(8,128)(2,1)S(1)}, u32[]{:S(2)}, u32[]{:S(2)}) collective-permute-start(bf16[8,640]{1,0:T(8,128)(2,1)S(1)} %shard_map.65.refs_11_), channel_id=1, source_target_pairs={{0,16},{8,24},{16,0},{24,8},{1,17},{9,25},{17,1},{25,9},{2,18},{10... | collective-permute-start | bytes 30728 | tf_op jit(solution)/shard_map/ppermute | solution.py:259
  17.2 1.4 %collective-permute-start.7 = (bf16[8,640]{1,0:T(8,128)(2,1)S(1)}, bf16[8,640]{1,0:T(8,128)(2,1)S(1)}, u32[]{:S(2)}, u32[]{:S(2)}) collective-permute-start(bf16[8,640]{1,0:T(8,128)(2,1)S(1)} %shard_map.65.refs_11_), channel_id=1, source_target_pairs={{0,24},{8,16},{16,8},{24,0},{1,25},{9,17},{17,9},{25,1},{2,26},{10... | collective-permute-start | bytes 30728 | tf_op jit(solution)/shard_map/ppermute | solution.py:259
  18.6 0.8 %collective-permute-start.8 = (bf16[8,640]{1,0:T(8,128)(2,1)S(1)}, bf16[8,640]{1,0:T(8,128)(2,1)S(1)}, u32[]{:S(2)}, u32[]{:S(2)}) collective-permute-start(bf16[8,640]{1,0:T(8,128)(2,1)S(1)} %shard_map.65.refs_11_), channel_id=1, source_target_pairs={{0,8},{8,0},{16,24},{24,16},{1,9},{9,1},{17,25},{25,17},{2,10},{10... | collective-permute-start | bytes 30728 | tf_op jit(solution)/shard_map/ppermute | solution.py:259
  19.4 0.1 collective-permute-done.5.refs_6_
  19.6 2.1 %collective-permute-done.7.refs_9_ = bf16[8,640]{1,0:T(8,128)(2,1)S(1)} collective-permute-done((bf16[8,640]{1,0:T(8,128)(2,1)S(1)}, bf16[8,640]{1,0:T(8,128)(2,1)S(1)}, u32[]{:S(2)}, u32[]{:S(2)}) %collective-permute-start.7) | collective-permute-done | bytes 10272 | tf_op jit(solution)/shard_map/ppermute | solution.py:259
  21.7 0.5 %collective-permute-done.8.refs_10_ = bf16[8,640]{1,0:T(8,128)(2,1)S(1)} collective-permute-done((bf16[8,640]{1,0:T(8,128)(2,1)S(1)}, bf16[8,640]{1,0:T(8,128)(2,1)S(1)}, u32[]{:S(2)}, u32[]{:S(2)}) %collective-permute-start.8) | collective-permute-done | bytes 10272 | tf_op jit(solution)/shard_map/ppermute | solution.py:259
  22.4 1.3 %shard_map.66.half = f32[384,384]{1,0:T(8,128)S(1)} custom-call(bf16[56,640]{1,0:T(8,128)(2,1)S(1)} %collective-permute-done.refs_0_, bf16[56,640]{1,0:T(8,128)(2,1)S(1)} %collective-permute-done.1.refs_1_, bf16[56,640]{1,0:T(8,128)(2,1)S(1)} %collective-permute-done.2.refs_2_, bf16[56,640]{1,0:T(8,128)(2,1)S(1)} %get-tuple-element.22.refs_3_, ...), custom_call_target="tpu_custom_call" | custom-call | tf_op jit(solution)/shard_map/pallas_call | solution.py:248
  23.7 0.3 collective-permute-done.9.other
  23.9 0.6 %shard_map.68 = (bf16[96,384]{1,0:T(8,128)(2,1)S(1)}, bf16[96,384]{1,0:T(8,128)(2,1)S(1)}, bf16[96,384]{1,0:T(8,128)(2,1)S(1)}, f32[192,768]{1,0:T(8,128)S(1)}, f32[32,640]{1,0:T(8,128)S(1)}) custom-call(f32[384,384]{1,0:T(8,128)S(1)} %shard_map.66.half, bf16[224,640]{1,0:T(8,128)(2,1)S(1)} %collective-permute-done.9.other, ...), custom_call_target="tpu_custom_call" | custom-call | tf_op jit(solution)/shard_map/pallas_call | solution.py:248
  24.6 1.6 %collective-permute-start.10 = (bf16[96,384]{1,0:T(8,128)(2,1)S(1)}, bf16[96,384]{1,0:T(8,128)(2,1)S(1)}, u32[]{:S(2)}, u32[]{:S(2)}) collective-permute-start(bf16[96,384]{1,0:T(8,128)(2,1)S(1)} %get-tuple-element.29), channel_id=1, source_target_pairs={{0,24},{8,16},{16,8},{24,0},{1,25},{9,17},{17,9},{25,1},{2,26},{10... | collective-permute-start | bytes 221192 | tf_op jit(solution)/shard_map/ppermute | solution.py:259
  26.2 0.9 %collective-permute-start.11 = (bf16[96,384]{1,0:T(8,128)(2,1)S(1)}, bf16[96,384]{1,0:T(8,128)(2,1)S(1)}, u32[]{:S(2)}, u32[]{:S(2)}) collective-permute-start(bf16[96,384]{1,0:T(8,128)(2,1)S(1)} %get-tuple-element.30), channel_id=1, source_target_pairs={{0,16},{8,24},{16,0},{24,8},{1,17},{9,25},{17,1},{25,9},{2,18},{10... | collective-permute-start | bytes 221192 | tf_op jit(solution)/shard_map/ppermute | solution.py:259
  27.1 1.1 %collective-permute-start.12 = (bf16[96,384]{1,0:T(8,128)(2,1)S(1)}, bf16[96,384]{1,0:T(8,128)(2,1)S(1)}, u32[]{:S(2)}, u32[]{:S(2)}) collective-permute-start(bf16[96,384]{1,0:T(8,128)(2,1)S(1)} %get-tuple-element.28._), channel_id=1, source_target_pairs={{0,8},{8,0},{16,24},{24,16},{1,9},{9,1},{17,25},{25,17},{2,10},{10... | collective-permute-start | bytes 221192 | tf_op jit(solution)/shard_map/ppermute | solution.py:259
  28.8 0.3 shard_map.70.refs_3_
  29.1 0.3 %copy-done = s32[1,3]{1,0:T(1,128)S(1)} copy-done((s32[1,3]{1,0:T(1,128)S(1)}, s32[1,3]{1,0:T(1,128)}, u32[]{:S(2)}) %copy-start) | copy-done | bytes 36
  29.5 0.6 %shard_map.69.wanted_ref = s32[8,128]{1,0:T(8,128)S(1)} custom-call(s32[1,3]{1,0:T(1,128)S(1)} %copy-done, s32[1]{0:T(128)S(6)} %copy.7.live, bf16[96,384]{1,0:T(8,128)(2,1)S(1)} %get-tuple-element.28._), custom_call_target="tpu_custom_call" | custom-call | tf_op jit(solution)/shard_map/pallas_call | solution.py:248
  30.1 1.5 %collective-permute-done.11.refs_1_ = bf16[96,384]{1,0:T(8,128)(2,1)S(1)} collective-permute-done((bf16[96,384]{1,0:T(8,128)(2,1)S(1)}, bf16[96,384]{1,0:T(8,128)(2,1)S(1)}, u32[]{:S(2)}, u32[]{:S(2)}) %collective-permute-start.11) | collective-permute-done | bytes 73760 | tf_op jit(solution)/shard_map/ppermute | solution.py:259
  31.6 1.0 %shard_map.71 = f32[48,3,2,384]{3,2,1,0:T(2,128)} custom-call(s32[8,128]{1,0:T(8,128)S(1)} %shard_map.69.wanted_ref, bf16[96,384]{1,0:T(8,128)(2,1)S(1)} %collective-permute-done.10.refs_0_, bf16[96,384]{1,0:T(8,128)(2,1)S(1)} %collective-permute-done.11.refs_1_, bf16[96,384]{1,0:T(8,128)(2,1)S(1)} %collective-permute-done.12.refs_2_, ...), custom_call_target="tpu_custom_call" | custom-call | tf_op jit(solution)/shard_map/pallas_call | solution.py:248
  (12 shorter events, 0.3 us)
Async XLA Ops:
  3.3 10.1 %collective-permute-start = (bf16[56,640]{1,0:T(8,128)(2,1)S(1)}, bf16[56,640]{1,0:T(8,128)(2,1)S(1)}, u32[]{:S(2)}, u32[]{:S(2)}) collective-permute-start(bf16[56,640]{1,0:T(8,128)(2,1)S(1)} %get-tuple-element.19), channel_id=1, source_target_pairs={{0,6},{1,7},{2,4},{3,5},{4,2},{5,3},{6,0},{7,1},{8,14},{9,15},{10,... | collective-permute-start | bytes 215048 | tf_op jit(solution)/shard_map/ppermute | solution.py:259
  8.4 7.4 %collective-permute-start.1 = (bf16[56,640]{1,0:T(8,128)(2,1)S(1)}, bf16[56,640]{1,0:T(8,128)(2,1)S(1)}, u32[]{:S(2)}, u32[]{:S(2)}) collective-permute-start(bf16[56,640]{1,0:T(8,128)(2,1)S(1)} %get-tuple-element.20), channel_id=1, source_target_pairs={{0,4},{1,5},{2,6},{3,7},{4,0},{5,1},{6,2},{7,3},{8,12},{9,13},{10,... | collective-permute-start | bytes 215048 | tf_op jit(solution)/shard_map/ppermute | solution.py:259
  8.4 7.4 %collective-permute-start.2 = (bf16[56,640]{1,0:T(8,128)(2,1)S(1)}, bf16[56,640]{1,0:T(8,128)(2,1)S(1)}, u32[]{:S(2)}, u32[]{:S(2)}) collective-permute-start(bf16[56,640]{1,0:T(8,128)(2,1)S(1)} %get-tuple-element.21), channel_id=1, source_target_pairs={{0,2},{1,3},{2,0},{3,1},{4,6},{5,7},{6,4},{7,5},{8,10},{9,11},{10,... | collective-permute-start | bytes 215048 | tf_op jit(solution)/shard_map/ppermute | solution.py:259
  9.1 9.5 %collective-permute-start.3 = (bf16[48,640]{1,0:T(8,128)(2,1)S(1)}, bf16[48,640]{1,0:T(8,128)(2,1)S(1)}, u32[]{:S(2)}, u32[]{:S(2)}) collective-permute-start(bf16[48,640]{1,0:T(8,128)(2,1)S(1)} %get-tuple-element.23), channel_id=1, source_target_pairs={{0,2},{1,3},{2,0},{3,1},{4,6},{5,7},{6,4},{7,5},{8,10},{9,11},{10,... | collective-permute-start | bytes 184328 | tf_op jit(solution)/shard_map/ppermute | solution.py:259
  10.5 9.0 %collective-permute-start.4 = (bf16[48,640]{1,0:T(8,128)(2,1)S(1)}, bf16[48,640]{1,0:T(8,128)(2,1)S(1)}, u32[]{:S(2)}, u32[]{:S(2)}) collective-permute-start(bf16[48,640]{1,0:T(8,128)(2,1)S(1)} %get-tuple-element.24), channel_id=1, source_target_pairs={{0,4},{1,5},{2,6},{3,7},{4,0},{5,1},{6,2},{7,3},{8,12},{9,13},{10,... | collective-permute-start | bytes 184328 | tf_op jit(solution)/shard_map/ppermute | solution.py:259
  13.4 6.1 %collective-permute-start.5 = (bf16[48,640]{1,0:T(8,128)(2,1)S(1)}, bf16[48,640]{1,0:T(8,128)(2,1)S(1)}, u32[]{:S(2)}, u32[]{:S(2)}) collective-permute-start(bf16[48,640]{1,0:T(8,128)(2,1)S(1)} %get-tuple-element.25), channel_id=1, source_target_pairs={{0,6},{1,7},{2,4},{3,5},{4,2},{5,3},{6,0},{7,1},{8,14},{9,15},{10,... | collective-permute-start | bytes 184328 | tf_op jit(solution)/shard_map/ppermute | solution.py:259
  15.9 3.7 %collective-permute-start.6 = (bf16[8,640]{1,0:T(8,128)(2,1)S(1)}, bf16[8,640]{1,0:T(8,128)(2,1)S(1)}, u32[]{:S(2)}, u32[]{:S(2)}) collective-permute-start(bf16[8,640]{1,0:T(8,128)(2,1)S(1)} %shard_map.65.refs_11_), channel_id=1, source_target_pairs={{0,16},{8,24},{16,0},{24,8},{1,17},{9,25},{17,1},{25,9},{2,18},{10... | collective-permute-start | bytes 30728 | tf_op jit(solution)/shard_map/ppermute | solution.py:259
  17.2 4.6 %collective-permute-start.7 = (bf16[8,640]{1,0:T(8,128)(2,1)S(1)}, bf16[8,640]{1,0:T(8,128)(2,1)S(1)}, u32[]{:S(2)}, u32[]{:S(2)}) collective-permute-start(bf16[8,640]{1,0:T(8,128)(2,1)S(1)} %shard_map.65.refs_11_), channel_id=1, source_target_pairs={{0,24},{8,16},{16,8},{24,0},{1,25},{9,17},{17,9},{25,1},{2,26},{10... | collective-permute-start | bytes 30728 | tf_op jit(solution)/shard_map/ppermute | solution.py:259
  18.6 3.7 %collective-permute-start.8 = (bf16[8,640]{1,0:T(8,128)(2,1)S(1)}, bf16[8,640]{1,0:T(8,128)(2,1)S(1)}, u32[]{:S(2)}, u32[]{:S(2)}) collective-permute-start(bf16[8,640]{1,0:T(8,128)(2,1)S(1)} %shard_map.65.refs_11_), channel_id=1, source_target_pairs={{0,8},{8,0},{16,24},{24,16},{1,9},{9,1},{17,25},{25,17},{2,10},{10... | collective-permute-start | bytes 30728 | tf_op jit(solution)/shard_map/ppermute | solution.py:259
  22.3 1.6 %collective-permute-start.9 = (bf16[224,640]{1,0:T(8,128)(2,1)S(1)}, bf16[224,640]{1,0:T(8,128)(2,1)S(1)}, u32[]{:S(2)}, u32[]{:S(2)}) collective-permute-start(bf16[224,640]{1,0:T(8,128)(2,1)S(1)} %shard_map.67), channel_id=1, source_target_pairs={{0,1},{1,0},{2,3},{3,2},{4,5},{5,4},{6,7},{7,6},{8,9},{9,8},{10,11... | collective-permute-start | bytes 860168 | tf_op jit(solution)/shard_map/ppermute | solution.py:259
  24.6 5.5 %collective-permute-start.10 = (bf16[96,384]{1,0:T(8,128)(2,1)S(1)}, bf16[96,384]{1,0:T(8,128)(2,1)S(1)}, u32[]{:S(2)}, u32[]{:S(2)}) collective-permute-start(bf16[96,384]{1,0:T(8,128)(2,1)S(1)} %get-tuple-element.29), channel_id=1, source_target_pairs={{0,24},{8,16},{16,8},{24,0},{1,25},{9,17},{17,9},{25,1},{2,26},{10... | collective-permute-start | bytes 221192 | tf_op jit(solution)/shard_map/ppermute | solution.py:259
  26.2 5.4 %collective-permute-start.11 = (bf16[96,384]{1,0:T(8,128)(2,1)S(1)}, bf16[96,384]{1,0:T(8,128)(2,1)S(1)}, u32[]{:S(2)}, u32[]{:S(2)}) collective-permute-start(bf16[96,384]{1,0:T(8,128)(2,1)S(1)} %get-tuple-element.30), channel_id=1, source_target_pairs={{0,16},{8,24},{16,0},{24,8},{1,17},{9,25},{17,1},{25,9},{2,18},{10... | collective-permute-start | bytes 221192 | tf_op jit(solution)/shard_map/ppermute | solution.py:259
  27.1 4.5 %collective-permute-start.12 = (bf16[96,384]{1,0:T(8,128)(2,1)S(1)}, bf16[96,384]{1,0:T(8,128)(2,1)S(1)}, u32[]{:S(2)}, u32[]{:S(2)}) collective-permute-start(bf16[96,384]{1,0:T(8,128)(2,1)S(1)} %get-tuple-element.28._), channel_id=1, source_target_pairs={{0,8},{8,0},{16,24},{24,16},{1,9},{9,1},{17,25},{25,17},{2,10},{10... | collective-permute-start | bytes 221192 | tf_op jit(solution)/shard_map/ppermute | solution.py:259
  28.8 0.7 %copy-start = (s32[1,3]{1,0:T(1,128)S(1)}, s32[1,3]{1,0:T(1,128)}, u32[]{:S(2)}) copy-start(s32[1,3]{1,0:T(1,128)} %partner.1) | copy-start | bytes 40

commit v8 on v7

--- a/solution.py
+++ b/solution.py
@@ -304,7 +304,7 @@
         [vmem] * zs,
         moved[:zs],
     )
-    blocks = list(range(2, chans)) + [1, 0]
+    blocks = list(reversed(range(chans)))
     spectra = [own if e == 0 else swap(own, "chan", chans, e) for e in blocks]
     gathered = call(
         functools.partial(gather_kernel, [n for _, _, n, _ in layout]),

time: 32.7 us -> 32.7 us (level)
  no operation moved by 1% of the time
where the time goes in v8:
time: 32.7 us; the launch traced here: 32.6 us
  starting transfers between devices  19.2 us (59%)
  Pallas kernels  7.1 us (22%)
  waiting for transfers between devices  5.19 us (16%)
  between operations  0.72 us (2%)
  local copies, waits for them, and re-layouts  0.35 us (1%)
    ppermute x13, starting transfers between devices, swap(): return lax.ppermute(value, axis, [(i, i ^ distance) for i in range(size)])  19.2 us
    pallas_call x8, Pallas kernels, call(): pl.pallas_call(kernel, out_shape=out_shape, in_specs=[pl.BlockSpec(memory...  7.1 us
    ppermute x13, waiting for transfers between devices, swap(): return lax.ppermute(value, axis, [(i, i ^ distance) for i in range(size)])  5.19 us
  transfers between devices with their start and end apart: 13, of which 8 were waited for; matrix products, arithmetic and copies ran while one was open for 0% of the time, Pallas kernels for 7%

profile of v8, /device:TPU:0, one launch (start us, length us, event | category | flops | bytes accessed | tf_op | source)
XLA Modules:
  0.0 32.6 jit_solution(10006829469775156838)
XLA Ops:
  0.0 3.3 %shard_map.64 = (bf16[56,640]{1,0:T(8,128)(2,1)S(1)}, bf16[56,640]{1,0:T(8,128)(2,1)S(1)}, bf16[56,640]{1,0:T(8,128)(2,1)S(1)}, bf16[56,640]{1,0:T(8,128)(2,1)S(...) custom-call(s32[1,2]{1,0:T(1,128)} %src_hbm.1, ...), custom_call_target="tpu_custom_call" | custom-call | tf_op jit(solution)/shard_map/pallas_call | solution.py:248
  3.3 5.1 %collective-permute-start = (bf16[56,640]{1,0:T(8,128)(2,1)S(1)}, bf16[56,640]{1,0:T(8,128)(2,1)S(1)}, u32[]{:S(2)}, u32[]{:S(2)}) collective-permute-start(bf16[56,640]{1,0:T(8,128)(2,1)S(1)} %get-tuple-element.19), channel_id=1, source_target_pairs={{0,6},{1,7},{2,4},{3,5},{4,2},{5,3},{6,0},{7,1},{8,14},{9,15},{10,... | collective-permute-start | bytes 215048 | tf_op jit(solution)/shard_map/ppermute | solution.py:259
  8.4 0.6 %collective-permute-start.2 = (bf16[56,640]{1,0:T(8,128)(2,1)S(1)}, bf16[56,640]{1,0:T(8,128)(2,1)S(1)}, u32[]{:S(2)}, u32[]{:S(2)}) collective-permute-start(bf16[56,640]{1,0:T(8,128)(2,1)S(1)} %get-tuple-element.21), channel_id=1, source_target_pairs={{0,2},{1,3},{2,0},{3,1},{4,6},{5,7},{6,4},{7,5},{8,10},{9,11},{10,... | collective-permute-start | bytes 215048 | tf_op jit(solution)/shard_map/ppermute | solution.py:259
  9.1 1.4 %collective-permute-start.3 = (bf16[48,640]{1,0:T(8,128)(2,1)S(1)}, bf16[48,640]{1,0:T(8,128)(2,1)S(1)}, u32[]{:S(2)}, u32[]{:S(2)}) collective-permute-start(bf16[48,640]{1,0:T(8,128)(2,1)S(1)} %get-tuple-element.23), channel_id=1, source_target_pairs={{0,2},{1,3},{2,0},{3,1},{4,6},{5,7},{6,4},{7,5},{8,10},{9,11},{10,... | collective-permute-start | bytes 184328 | tf_op jit(solution)/shard_map/ppermute | solution.py:259
  10.5 2.9 %collective-permute-start.4 = (bf16[48,640]{1,0:T(8,128)(2,1)S(1)}, bf16[48,640]{1,0:T(8,128)(2,1)S(1)}, u32[]{:S(2)}, u32[]{:S(2)}) collective-permute-start(bf16[48,640]{1,0:T(8,128)(2,1)S(1)} %get-tuple-element.24), channel_id=1, source_target_pairs={{0,4},{1,5},{2,6},{3,7},{4,0},{5,1},{6,2},{7,3},{8,12},{9,13},{10,... | collective-permute-start | bytes 184328 | tf_op jit(solution)/shard_map/ppermute | solution.py:259
  13.4 2.0 %collective-permute-start.5 = (bf16[48,640]{1,0:T(8,128)(2,1)S(1)}, bf16[48,640]{1,0:T(8,128)(2,1)S(1)}, u32[]{:S(2)}, u32[]{:S(2)}) collective-permute-start(bf16[48,640]{1,0:T(8,128)(2,1)S(1)} %get-tuple-element.25), channel_id=1, source_target_pairs={{0,6},{1,7},{2,4},{3,5},{4,2},{5,3},{6,0},{7,1},{8,14},{9,15},{10,... | collective-permute-start | bytes 184328 | tf_op jit(solution)/shard_map/ppermute | solution.py:259
  15.4 0.5 %collective-permute-done.1.refs_1_ = bf16[56,640]{1,0:T(8,128)(2,1)S(1)} collective-permute-done((bf16[56,640]{1,0:T(8,128)(2,1)S(1)}, bf16[56,640]{1,0:T(8,128)(2,1)S(1)}, u32[]{:S(2)}, u32[]{:S(2)}) %collective-permute-start.1) | collective-permute-done | bytes 71712 | tf_op jit(solution)/shard_map/ppermute | solution.py:259
  15.9 2.2 %collective-permute-start.6 = (bf16[8,640]{1,0:T(8,128)(2,1)S(1)}, bf16[8,640]{1,0:T(8,128)(2,1)S(1)}, u32[]{:S(2)}, u32[]{:S(2)}) collective-permute-start(bf16[8,640]{1,0:T(8,128)(2,1)S(1)} %shard_map.65.refs_11_), channel_id=1, source_target_pairs={{0,24},{8,16},{16,8},{24,0},{1,25},{9,17},{17,9},{25,1},{2,26},{10... | collective-permute-start | bytes 30728 | tf_op jit(solution)/shard_map/ppermute | solution.py:259
  18.1 0.5 %collective-permute-start.7 = (bf16[8,640]{1,0:T(8,128)(2,1)S(1)}, bf16[8,640]{1,0:T(8,128)(2,1)S(1)}, u32[]{:S(2)}, u32[]{:S(2)}) collective-permute-start(bf16[8,640]{1,0:T(8,128)(2,1)S(1)} %shard_map.65.refs_11_), channel_id=1, source_target_pairs={{0,16},{8,24},{16,0},{24,8},{1,17},{9,25},{17,1},{25,9},{2,18},{10... | collective-permute-start | bytes 30728 | tf_op jit(solution)/shard_map/ppermute | solution.py:259
  18.6 0.8 %collective-permute-start.8 = (bf16[8,640]{1,0:T(8,128)(2,1)S(1)}, bf16[8,640]{1,0:T(8,128)(2,1)S(1)}, u32[]{:S(2)}, u32[]{:S(2)}) collective-permute-start(bf16[8,640]{1,0:T(8,128)(2,1)S(1)} %shard_map.65.refs_11_), channel_id=1, source_target_pairs={{0,8},{8,0},{16,24},{24,16},{1,9},{9,1},{17,25},{25,17},{2,10},{10... | collective-permute-start | bytes 30728 | tf_op jit(solution)/shard_map/ppermute | solution.py:259
  19.5 1.0 %collective-permute-done.6.refs_8_ = bf16[8,640]{1,0:T(8,128)(2,1)S(1)} collective-permute-done((bf16[8,640]{1,0:T(8,128)(2,1)S(1)}, bf16[8,640]{1,0:T(8,128)(2,1)S(1)}, u32[]{:S(2)}, u32[]{:S(2)}) %collective-permute-start.6) | collective-permute-done | bytes 10272 | tf_op jit(solution)/shard_map/ppermute | solution.py:259
  20.5 1.2 %collective-permute-done.7.refs_9_ = bf16[8,640]{1,0:T(8,128)(2,1)S(1)} collective-permute-done((bf16[8,640]{1,0:T(8,128)(2,1)S(1)}, bf16[8,640]{1,0:T(8,128)(2,1)S(1)}, u32[]{:S(2)}, u32[]{:S(2)}) %collective-permute-start.7) | collective-permute-done | bytes 10272 | tf_op jit(solution)/shard_map/ppermute | solution.py:259
  21.8 0.5 %collective-permute-done.8.refs_10_ = bf16[8,640]{1,0:T(8,128)(2,1)S(1)} collective-permute-done((bf16[8,640]{1,0:T(8,128)(2,1)S(1)}, bf16[8,640]{1,0:T(8,128)(2,1)S(1)}, u32[]{:S(2)}, u32[]{:S(2)}) %collective-permute-start.8) | collective-permute-done | bytes 10272 | tf_op jit(solution)/shard_map/ppermute | solution.py:259
  22.4 1.3 %shard_map.66.half = f32[384,384]{1,0:T(8,128)S(1)} custom-call(bf16[56,640]{1,0:T(8,128)(2,1)S(1)} %collective-permute-done.refs_0_, bf16[56,640]{1,0:T(8,128)(2,1)S(1)} %collective-permute-done.1.refs_1_, bf16[56,640]{1,0:T(8,128)(2,1)S(1)} %collective-permute-done.2.refs_2_, bf16[56,640]{1,0:T(8,128)(2,1)S(1)} %get-tuple-element.22.refs_3_, ...), custom_call_target="tpu_custom_call" | custom-call | tf_op jit(solution)/shard_map/pallas_call | solution.py:248
  23.7 0.3 collective-permute-done.9.other
  23.9 0.6 %shard_map.68 = (bf16[96,384]{1,0:T(8,128)(2,1)S(1)}, bf16[96,384]{1,0:T(8,128)(2,1)S(1)}, bf16[96,384]{1,0:T(8,128)(2,1)S(1)}, f32[192,768]{1,0:T(8,128)S(1)}, f32[32,640]{1,0:T(8,128)S(1)}) custom-call(f32[384,384]{1,0:T(8,128)S(1)} %shard_map.66.half, bf16[224,640]{1,0:T(8,128)(2,1)S(1)} %collective-permute-done.9.other, ...), custom_call_target="tpu_custom_call" | custom-call | tf_op jit(solution)/shard_map/pallas_call | solution.py:248
  24.6 1.6 %collective-permute-start.10 = (bf16[96,384]{1,0:T(8,128)(2,1)S(1)}, bf16[96,384]{1,0:T(8,128)(2,1)S(1)}, u32[]{:S(2)}, u32[]{:S(2)}) collective-permute-start(bf16[96,384]{1,0:T(8,128)(2,1)S(1)} %get-tuple-element.29), channel_id=1, source_target_pairs={{0,24},{8,16},{16,8},{24,0},{1,25},{9,17},{17,9},{25,1},{2,26},{10... | collective-permute-start | bytes 221192 | tf_op jit(solution)/shard_map/ppermute | solution.py:259
  26.2 0.8 %collective-permute-start.11 = (bf16[96,384]{1,0:T(8,128)(2,1)S(1)}, bf16[96,384]{1,0:T(8,128)(2,1)S(1)}, u32[]{:S(2)}, u32[]{:S(2)}) collective-permute-start(bf16[96,384]{1,0:T(8,128)(2,1)S(1)} %get-tuple-element.30), channel_id=1, source_target_pairs={{0,16},{8,24},{16,0},{24,8},{1,17},{9,25},{17,1},{25,9},{2,18},{10... | collective-permute-start | bytes 221192 | tf_op jit(solution)/shard_map/ppermute | solution.py:259
  26.9 1.2 %collective-permute-start.12 = (bf16[96,384]{1,0:T(8,128)(2,1)S(1)}, bf16[96,384]{1,0:T(8,128)(2,1)S(1)}, u32[]{:S(2)}, u32[]{:S(2)}) collective-permute-start(bf16[96,384]{1,0:T(8,128)(2,1)S(1)} %get-tuple-element.28._), channel_id=1, source_target_pairs={{0,8},{8,0},{16,24},{24,16},{1,9},{9,1},{17,25},{25,17},{2,10},{10... | collective-permute-start | bytes 221192 | tf_op jit(solution)/shard_map/ppermute | solution.py:259
  28.8 0.3 shard_map.70.refs_3_
  29.1 0.3 %copy-done = s32[1,3]{1,0:T(1,128)S(1)} copy-done((s32[1,3]{1,0:T(1,128)S(1)}, s32[1,3]{1,0:T(1,128)}, u32[]{:S(2)}) %copy-start) | copy-done | bytes 36
  29.5 0.6 %shard_map.69.wanted_ref = s32[8,128]{1,0:T(8,128)S(1)} custom-call(s32[1,3]{1,0:T(1,128)S(1)} %copy-done, s32[1]{0:T(128)S(6)} %copy.7.live, bf16[96,384]{1,0:T(8,128)(2,1)S(1)} %get-tuple-element.28._), custom_call_target="tpu_custom_call" | custom-call | tf_op jit(solution)/shard_map/pallas_call | solution.py:248
  30.1 1.5 %collective-permute-done.11.refs_1_ = bf16[96,384]{1,0:T(8,128)(2,1)S(1)} collective-permute-done((bf16[96,384]{1,0:T(8,128)(2,1)S(1)}, bf16[96,384]{1,0:T(8,128)(2,1)S(1)}, u32[]{:S(2)}, u32[]{:S(2)}) %collective-permute-start.11) | collective-permute-done | bytes 73760 | tf_op jit(solution)/shard_map/ppermute | solution.py:259
  31.6 1.0 %shard_map.71 = f32[48,3,2,384]{3,2,1,0:T(2,128)} custom-call(s32[8,128]{1,0:T(8,128)S(1)} %shard_map.69.wanted_ref, bf16[96,384]{1,0:T(8,128)(2,1)S(1)} %collective-permute-done.10.refs_0_, bf16[96,384]{1,0:T(8,128)(2,1)S(1)} %collective-permute-done.11.refs_1_, bf16[96,384]{1,0:T(8,128)(2,1)S(1)} %collective-permute-done.12.refs_2_, ...), custom_call_target="tpu_custom_call" | custom-call | tf_op jit(solution)/shard_map/pallas_call | solution.py:248
  (12 shorter events, 0.3 us)
Async XLA Ops:
  3.3 10.1 %collective-permute-start = (bf16[56,640]{1,0:T(8,128)(2,1)S(1)}, bf16[56,640]{1,0:T(8,128)(2,1)S(1)}, u32[]{:S(2)}, u32[]{:S(2)}) collective-permute-start(bf16[56,640]{1,0:T(8,128)(2,1)S(1)} %get-tuple-element.19), channel_id=1, source_target_pairs={{0,6},{1,7},{2,4},{3,5},{4,2},{5,3},{6,0},{7,1},{8,14},{9,15},{10,... | collective-permute-start | bytes 215048 | tf_op jit(solution)/shard_map/ppermute | solution.py:259
  8.4 7.4 %collective-permute-start.1 = (bf16[56,640]{1,0:T(8,128)(2,1)S(1)}, bf16[56,640]{1,0:T(8,128)(2,1)S(1)}, u32[]{:S(2)}, u32[]{:S(2)}) collective-permute-start(bf16[56,640]{1,0:T(8,128)(2,1)S(1)} %get-tuple-element.20), channel_id=1, source_target_pairs={{0,4},{1,5},{2,6},{3,7},{4,0},{5,1},{6,2},{7,3},{8,12},{9,13},{10,... | collective-permute-start | bytes 215048 | tf_op jit(solution)/shard_map/ppermute | solution.py:259
  8.4 7.4 %collective-permute-start.2 = (bf16[56,640]{1,0:T(8,128)(2,1)S(1)}, bf16[56,640]{1,0:T(8,128)(2,1)S(1)}, u32[]{:S(2)}, u32[]{:S(2)}) collective-permute-start(bf16[56,640]{1,0:T(8,128)(2,1)S(1)} %get-tuple-element.21), channel_id=1, source_target_pairs={{0,2},{1,3},{2,0},{3,1},{4,6},{5,7},{6,4},{7,5},{8,10},{9,11},{10,... | collective-permute-start | bytes 215048 | tf_op jit(solution)/shard_map/ppermute | solution.py:259
  9.1 9.5 %collective-permute-start.3 = (bf16[48,640]{1,0:T(8,128)(2,1)S(1)}, bf16[48,640]{1,0:T(8,128)(2,1)S(1)}, u32[]{:S(2)}, u32[]{:S(2)}) collective-permute-start(bf16[48,640]{1,0:T(8,128)(2,1)S(1)} %get-tuple-element.23), channel_id=1, source_target_pairs={{0,2},{1,3},{2,0},{3,1},{4,6},{5,7},{6,4},{7,5},{8,10},{9,11},{10,... | collective-permute-start | bytes 184328 | tf_op jit(solution)/shard_map/ppermute | solution.py:259
  10.5 9.0 %collective-permute-start.4 = (bf16[48,640]{1,0:T(8,128)(2,1)S(1)}, bf16[48,640]{1,0:T(8,128)(2,1)S(1)}, u32[]{:S(2)}, u32[]{:S(2)}) collective-permute-start(bf16[48,640]{1,0:T(8,128)(2,1)S(1)} %get-tuple-element.24), channel_id=1, source_target_pairs={{0,4},{1,5},{2,6},{3,7},{4,0},{5,1},{6,2},{7,3},{8,12},{9,13},{10,... | collective-permute-start | bytes 184328 | tf_op jit(solution)/shard_map/ppermute | solution.py:259
  13.4 6.1 %collective-permute-start.5 = (bf16[48,640]{1,0:T(8,128)(2,1)S(1)}, bf16[48,640]{1,0:T(8,128)(2,1)S(1)}, u32[]{:S(2)}, u32[]{:S(2)}) collective-permute-start(bf16[48,640]{1,0:T(8,128)(2,1)S(1)} %get-tuple-element.25), channel_id=1, source_target_pairs={{0,6},{1,7},{2,4},{3,5},{4,2},{5,3},{6,0},{7,1},{8,14},{9,15},{10,... | collective-permute-start | bytes 184328 | tf_op jit(solution)/shard_map/ppermute | solution.py:259
  15.9 4.7 %collective-permute-start.6 = (bf16[8,640]{1,0:T(8,128)(2,1)S(1)}, bf16[8,640]{1,0:T(8,128)(2,1)S(1)}, u32[]{:S(2)}, u32[]{:S(2)}) collective-permute-start(bf16[8,640]{1,0:T(8,128)(2,1)S(1)} %shard_map.65.refs_11_), channel_id=1, source_target_pairs={{0,24},{8,16},{16,8},{24,0},{1,25},{9,17},{17,9},{25,1},{2,26},{10... | collective-permute-start | bytes 30728 | tf_op jit(solution)/shard_map/ppermute | solution.py:259
  18.1 3.7 %collective-permute-start.7 = (bf16[8,640]{1,0:T(8,128)(2,1)S(1)}, bf16[8,640]{1,0:T(8,128)(2,1)S(1)}, u32[]{:S(2)}, u32[]{:S(2)}) collective-permute-start(bf16[8,640]{1,0:T(8,128)(2,1)S(1)} %shard_map.65.refs_11_), channel_id=1, source_target_pairs={{0,16},{8,24},{16,0},{24,8},{1,17},{9,25},{17,1},{25,9},{2,18},{10... | collective-permute-start | bytes 30728 | tf_op jit(solution)/shard_map/ppermute | solution.py:259
  18.6 3.7 %collective-permute-start.8 = (bf16[8,640]{1,0:T(8,128)(2,1)S(1)}, bf16[8,640]{1,0:T(8,128)(2,1)S(1)}, u32[]{:S(2)}, u32[]{:S(2)}) collective-permute-start(bf16[8,640]{1,0:T(8,128)(2,1)S(1)} %shard_map.65.refs_11_), channel_id=1, source_target_pairs={{0,8},{8,0},{16,24},{24,16},{1,9},{9,1},{17,25},{25,17},{2,10},{10... | collective-permute-start | bytes 30728 | tf_op jit(solution)/shard_map/ppermute | solution.py:259
  22.3 1.6 %collective-permute-start.9 = (bf16[224,640]{1,0:T(8,128)(2,1)S(1)}, bf16[224,640]{1,0:T(8,128)(2,1)S(1)}, u32[]{:S(2)}, u32[]{:S(2)}) collective-permute-start(bf16[224,640]{1,0:T(8,128)(2,1)S(1)} %shard_map.67), channel_id=1, source_target_pairs={{0,1},{1,0},{2,3},{3,2},{4,5},{5,4},{6,7},{7,6},{8,9},{9,8},{10,11... | collective-permute-start | bytes 860168 | tf_op jit(solution)/shard_map/ppermute | solution.py:259
  24.6 5.5 %collective-permute-start.10 = (bf16[96,384]{1,0:T(8,128)(2,1)S(1)}, bf16[96,384]{1,0:T(8,128)(2,1)S(1)}, u32[]{:S(2)}, u32[]{:S(2)}) collective-permute-start(bf16[96,384]{1,0:T(8,128)(2,1)S(1)} %get-tuple-element.29), channel_id=1, source_target_pairs={{0,24},{8,16},{16,8},{24,0},{1,25},{9,17},{17,9},{25,1},{2,26},{10... | collective-permute-start | bytes 221192 | tf_op jit(solution)/shard_map/ppermute | solution.py:259
  26.2 5.4 %collective-permute-start.11 = (bf16[96,384]{1,0:T(8,128)(2,1)S(1)}, bf16[96,384]{1,0:T(8,128)(2,1)S(1)}, u32[]{:S(2)}, u32[]{:S(2)}) collective-permute-start(bf16[96,384]{1,0:T(8,128)(2,1)S(1)} %get-tuple-element.30), channel_id=1, source_target_pairs={{0,16},{8,24},{16,0},{24,8},{1,17},{9,25},{17,1},{25,9},{2,18},{10... | collective-permute-start | bytes 221192 | tf_op jit(solution)/shard_map/ppermute | solution.py:259
  26.9 4.6 %collective-permute-start.12 = (bf16[96,384]{1,0:T(8,128)(2,1)S(1)}, bf16[96,384]{1,0:T(8,128)(2,1)S(1)}, u32[]{:S(2)}, u32[]{:S(2)}) collective-permute-start(bf16[96,384]{1,0:T(8,128)(2,1)S(1)} %get-tuple-element.28._), channel_id=1, source_target_pairs={{0,8},{8,0},{16,24},{24,16},{1,9},{9,1},{17,25},{25,17},{2,10},{10... | collective-permute-start | bytes 221192 | tf_op jit(solution)/shard_map/ppermute | solution.py:259
  28.8 0.7 %copy-start = (s32[1,3]{1,0:T(1,128)S(1)}, s32[1,3]{1,0:T(1,128)}, u32[]{:S(2)}) copy-start(s32[1,3]{1,0:T(1,128)} %partner.1) | copy-start | bytes 40

commit v9 on v8

--- a/solution.py
+++ b/solution.py
@@ -20,7 +20,7 @@
 WIDTH = 2 * F
 HALF = L // 2
 SRC_ROWS = 8
-PIECES = 1
+PIECES = 4
 F32 = jnp.float32
 BF16 = jnp.bfloat16
 

time: 32.7 us -> 32.8 us (level)
  no operation moved by 1% of the time
where the time goes in v9:
time: 32.8 us; the launch traced here: 32.6 us
  starting transfers between devices  19.2 us (59%)
  Pallas kernels  7.13 us (22%)
  waiting for transfers between devices  5.2 us (16%)
  between operations  0.73 us (2%)
  local copies, waits for them, and re-layouts  0.35 us (1%)
    ppermute x13, starting transfers between devices, swap(): return lax.ppermute(value, axis, [(i, i ^ distance) for i in range(size)])  19.2 us
    pallas_call x8, Pallas kernels, call(): pl.pallas_call(kernel, out_shape=out_shape, in_specs=[pl.BlockSpec(memory...  7.13 us
    ppermute x13, waiting for transfers between devices, swap(): return lax.ppermute(value, axis, [(i, i ^ distance) for i in range(size)])  5.2 us
  transfers between devices with their start and end apart: 13, of which 8 were waited for; matrix products, arithmetic and copies ran while one was open for 0% of the time, Pallas kernels for 7%

profile of v9, /device:TPU:0, one launch (start us, length us, event | category | flops | bytes accessed | tf_op | source)
XLA Modules:
  0.0 32.6 jit_solution(4315224382612928047)
XLA Ops:
  0.0 3.4 %shard_map.64 = (bf16[56,640]{1,0:T(8,128)(2,1)S(1)}, bf16[56,640]{1,0:T(8,128)(2,1)S(1)}, bf16[56,640]{1,0:T(8,128)(2,1)S(1)}, bf16[56,640]{1,0:T(8,128)(2,1)S(...) custom-call(s32[1,2]{1,0:T(1,128)} %src_hbm.1, ...), custom_call_target="tpu_custom_call" | custom-call | tf_op jit(solution)/shard_map/pallas_call | solution.py:248
  3.4 5.1 %collective-permute-start = (bf16[56,640]{1,0:T(8,128)(2,1)S(1)}, bf16[56,640]{1,0:T(8,128)(2,1)S(1)}, u32[]{:S(2)}, u32[]{:S(2)}) collective-permute-start(bf16[56,640]{1,0:T(8,128)(2,1)S(1)} %get-tuple-element.19), channel_id=1, source_target_pairs={{0,6},{1,7},{2,4},{3,5},{4,2},{5,3},{6,0},{7,1},{8,14},{9,15},{10,... | collective-permute-start | bytes 215048 | tf_op jit(solution)/shard_map/ppermute | solution.py:259
  8.5 0.6 %collective-permute-start.2 = (bf16[56,640]{1,0:T(8,128)(2,1)S(1)}, bf16[56,640]{1,0:T(8,128)(2,1)S(1)}, u32[]{:S(2)}, u32[]{:S(2)}) collective-permute-start(bf16[56,640]{1,0:T(8,128)(2,1)S(1)} %get-tuple-element.21), channel_id=1, source_target_pairs={{0,2},{1,3},{2,0},{3,1},{4,6},{5,7},{6,4},{7,5},{8,10},{9,11},{10,... | collective-permute-start | bytes 215048 | tf_op jit(solution)/shard_map/ppermute | solution.py:259
  9.1 1.4 %collective-permute-start.3 = (bf16[48,640]{1,0:T(8,128)(2,1)S(1)}, bf16[48,640]{1,0:T(8,128)(2,1)S(1)}, u32[]{:S(2)}, u32[]{:S(2)}) collective-permute-start(bf16[48,640]{1,0:T(8,128)(2,1)S(1)} %get-tuple-element.23), channel_id=1, source_target_pairs={{0,2},{1,3},{2,0},{3,1},{4,6},{5,7},{6,4},{7,5},{8,10},{9,11},{10,... | collective-permute-start | bytes 184328 | tf_op jit(solution)/shard_map/ppermute | solution.py:259
  10.5 2.9 %collective-permute-start.4 = (bf16[48,640]{1,0:T(8,128)(2,1)S(1)}, bf16[48,640]{1,0:T(8,128)(2,1)S(1)}, u32[]{:S(2)}, u32[]{:S(2)}) collective-permute-start(bf16[48,640]{1,0:T(8,128)(2,1)S(1)} %get-tuple-element.24), channel_id=1, source_target_pairs={{0,4},{1,5},{2,6},{3,7},{4,0},{5,1},{6,2},{7,3},{8,12},{9,13},{10,... | collective-permute-start | bytes 184328 | tf_op jit(solution)/shard_map/ppermute | solution.py:259
  13.4 2.0 %collective-permute-start.5 = (bf16[48,640]{1,0:T(8,128)(2,1)S(1)}, bf16[48,640]{1,0:T(8,128)(2,1)S(1)}, u32[]{:S(2)}, u32[]{:S(2)}) collective-permute-start(bf16[48,640]{1,0:T(8,128)(2,1)S(1)} %get-tuple-element.25), channel_id=1, source_target_pairs={{0,6},{1,7},{2,4},{3,5},{4,2},{5,3},{6,0},{7,1},{8,14},{9,15},{10,... | collective-permute-start | bytes 184328 | tf_op jit(solution)/shard_map/ppermute | solution.py:259
  15.4 0.5 %collective-permute-done.1.refs_1_ = bf16[56,640]{1,0:T(8,128)(2,1)S(1)} collective-permute-done((bf16[56,640]{1,0:T(8,128)(2,1)S(1)}, bf16[56,640]{1,0:T(8,128)(2,1)S(1)}, u32[]{:S(2)}, u32[]{:S(2)}) %collective-permute-start.1) | collective-permute-done | bytes 71712 | tf_op jit(solution)/shard_map/ppermute | solution.py:259
  15.9 2.2 %collective-permute-start.6 = (bf16[8,640]{1,0:T(8,128)(2,1)S(1)}, bf16[8,640]{1,0:T(8,128)(2,1)S(1)}, u32[]{:S(2)}, u32[]{:S(2)}) collective-permute-start(bf16[8,640]{1,0:T(8,128)(2,1)S(1)} %shard_map.65.refs_11_), channel_id=1, source_target_pairs={{0,24},{8,16},{16,8},{24,0},{1,25},{9,17},{17,9},{25,1},{2,26},{10... | collective-permute-start | bytes 30728 | tf_op jit(solution)/shard_map/ppermute | solution.py:259
  18.1 0.5 %collective-permute-start.7 = (bf16[8,640]{1,0:T(8,128)(2,1)S(1)}, bf16[8,640]{1,0:T(8,128)(2,1)S(1)}, u32[]{:S(2)}, u32[]{:S(2)}) collective-permute-start(bf16[8,640]{1,0:T(8,128)(2,1)S(1)} %shard_map.65.refs_11_), channel_id=1, source_target_pairs={{0,16},{8,24},{16,0},{24,8},{1,17},{9,25},{17,1},{25,9},{2,18},{10... | collective-permute-start | bytes 30728 | tf_op jit(solution)/shard_map/ppermute | solution.py:259
  18.6 0.8 %collective-permute-start.8 = (bf16[8,640]{1,0:T(8,128)(2,1)S(1)}, bf16[8,640]{1,0:T(8,128)(2,1)S(1)}, u32[]{:S(2)}, u32[]{:S(2)}) collective-permute-start(bf16[8,640]{1,0:T(8,128)(2,1)S(1)} %shard_map.65.refs_11_), channel_id=1, source_target_pairs={{0,8},{8,0},{16,24},{24,16},{1,9},{9,1},{17,25},{25,17},{2,10},{10... | collective-permute-start | bytes 30728 | tf_op jit(solution)/shard_map/ppermute | solution.py:259
  19.6 1.0 %collective-permute-done.6.refs_8_ = bf16[8,640]{1,0:T(8,128)(2,1)S(1)} collective-permute-done((bf16[8,640]{1,0:T(8,128)(2,1)S(1)}, bf16[8,640]{1,0:T(8,128)(2,1)S(1)}, u32[]{:S(2)}, u32[]{:S(2)}) %collective-permute-start.6) | collective-permute-done | bytes 10272 | tf_op jit(solution)/shard_map/ppermute | solution.py:259
  20.6 1.2 %collective-permute-done.7.refs_9_ = bf16[8,640]{1,0:T(8,128)(2,1)S(1)} collective-permute-done((bf16[8,640]{1,0:T(8,128)(2,1)S(1)}, bf16[8,640]{1,0:T(8,128)(2,1)S(1)}, u32[]{:S(2)}, u32[]{:S(2)}) %collective-permute-start.7) | collective-permute-done | bytes 10272 | tf_op jit(solution)/shard_map/ppermute | solution.py:259
  21.8 0.5 %collective-permute-done.8.refs_10_ = bf16[8,640]{1,0:T(8,128)(2,1)S(1)} collective-permute-done((bf16[8,640]{1,0:T(8,128)(2,1)S(1)}, bf16[8,640]{1,0:T(8,128)(2,1)S(1)}, u32[]{:S(2)}, u32[]{:S(2)}) %collective-permute-start.8) | collective-permute-done | bytes 10272 | tf_op jit(solution)/shard_map/ppermute | solution.py:259
  22.4 1.3 %shard_map.66.half = f32[384,384]{1,0:T(8,128)S(1)} custom-call(bf16[56,640]{1,0:T(8,128)(2,1)S(1)} %collective-permute-done.refs_0_, bf16[56,640]{1,0:T(8,128)(2,1)S(1)} %collective-permute-done.1.refs_1_, bf16[56,640]{1,0:T(8,128)(2,1)S(1)} %collective-permute-done.2.refs_2_, bf16[56,640]{1,0:T(8,128)(2,1)S(1)} %get-tuple-element.22.refs_3_, ...), custom_call_target="tpu_custom_call" | custom-call | tf_op jit(solution)/shard_map/pallas_call | solution.py:248
  23.7 0.3 collective-permute-done.9.other
  24.0 0.6 %shard_map.68 = (bf16[96,384]{1,0:T(8,128)(2,1)S(1)}, bf16[96,384]{1,0:T(8,128)(2,1)S(1)}, bf16[96,384]{1,0:T(8,128)(2,1)S(1)}, f32[192,768]{1,0:T(8,128)S(1)}, f32[32,640]{1,0:T(8,128)S(1)}) custom-call(f32[384,384]{1,0:T(8,128)S(1)} %shard_map.66.half, bf16[224,640]{1,0:T(8,128)(2,1)S(1)} %collective-permute-done.9.other, ...), custom_call_target="tpu_custom_call" | custom-call | tf_op jit(solution)/shard_map/pallas_call | solution.py:248
  24.6 1.7 %collective-permute-start.10 = (bf16[96,384]{1,0:T(8,128)(2,1)S(1)}, bf16[96,384]{1,0:T(8,128)(2,1)S(1)}, u32[]{:S(2)}, u32[]{:S(2)}) collective-permute-start(bf16[96,384]{1,0:T(8,128)(2,1)S(1)} %get-tuple-element.29), channel_id=1, source_target_pairs={{0,24},{8,16},{16,8},{24,0},{1,25},{9,17},{17,9},{25,1},{2,26},{10... | collective-permute-start | bytes 221192 | tf_op jit(solution)/shard_map/ppermute | solution.py:259
  26.3 0.7 %collective-permute-start.11 = (bf16[96,384]{1,0:T(8,128)(2,1)S(1)}, bf16[96,384]{1,0:T(8,128)(2,1)S(1)}, u32[]{:S(2)}, u32[]{:S(2)}) collective-permute-start(bf16[96,384]{1,0:T(8,128)(2,1)S(1)} %get-tuple-element.30), channel_id=1, source_target_pairs={{0,16},{8,24},{16,0},{24,8},{1,17},{9,25},{17,1},{25,9},{2,18},{10... | collective-permute-start | bytes 221192 | tf_op jit(solution)/shard_map/ppermute | solution.py:259
  27.0 1.2 %collective-permute-start.12 = (bf16[96,384]{1,0:T(8,128)(2,1)S(1)}, bf16[96,384]{1,0:T(8,128)(2,1)S(1)}, u32[]{:S(2)}, u32[]{:S(2)}) collective-permute-start(bf16[96,384]{1,0:T(8,128)(2,1)S(1)} %get-tuple-element.28._), channel_id=1, source_target_pairs={{0,8},{8,0},{16,24},{24,16},{1,9},{9,1},{17,25},{25,17},{2,10},{10... | collective-permute-start | bytes 221192 | tf_op jit(solution)/shard_map/ppermute | solution.py:259
  28.8 0.3 shard_map.70.refs_3_
  29.1 0.3 %copy-done = s32[1,3]{1,0:T(1,128)S(1)} copy-done((s32[1,3]{1,0:T(1,128)S(1)}, s32[1,3]{1,0:T(1,128)}, u32[]{:S(2)}) %copy-start) | copy-done | bytes 36
  29.5 0.6 %shard_map.69.wanted_ref = s32[8,128]{1,0:T(8,128)S(1)} custom-call(s32[1,3]{1,0:T(1,128)S(1)} %copy-done, s32[1]{0:T(128)S(6)} %copy.7.live, bf16[96,384]{1,0:T(8,128)(2,1)S(1)} %get-tuple-element.28._), custom_call_target="tpu_custom_call" | custom-call | tf_op jit(solution)/shard_map/pallas_call | solution.py:248
  30.1 1.5 %collective-permute-done.11.refs_1_ = bf16[96,384]{1,0:T(8,128)(2,1)S(1)} collective-permute-done((bf16[96,384]{1,0:T(8,128)(2,1)S(1)}, bf16[96,384]{1,0:T(8,128)(2,1)S(1)}, u32[]{:S(2)}, u32[]{:S(2)}) %collective-permute-start.11) | collective-permute-done | bytes 73760 | tf_op jit(solution)/shard_map/ppermute | solution.py:259
  31.6 1.0 %shard_map.71 = f32[48,3,2,384]{3,2,1,0:T(2,128)} custom-call(s32[8,128]{1,0:T(8,128)S(1)} %shard_map.69.wanted_ref, bf16[96,384]{1,0:T(8,128)(2,1)S(1)} %collective-permute-done.10.refs_0_, bf16[96,384]{1,0:T(8,128)(2,1)S(1)} %collective-permute-done.11.refs_1_, bf16[96,384]{1,0:T(8,128)(2,1)S(1)} %collective-permute-done.12.refs_2_, ...), custom_call_target="tpu_custom_call" | custom-call | tf_op jit(solution)/shard_map/pallas_call | solution.py:248
  (12 shorter events, 0.3 us)
Async XLA Ops:
  3.4 10.1 %collective-permute-start = (bf16[56,640]{1,0:T(8,128)(2,1)S(1)}, bf16[56,640]{1,0:T(8,128)(2,1)S(1)}, u32[]{:S(2)}, u32[]{:S(2)}) collective-permute-start(bf16[56,640]{1,0:T(8,128)(2,1)S(1)} %get-tuple-element.19), channel_id=1, source_target_pairs={{0,6},{1,7},{2,4},{3,5},{4,2},{5,3},{6,0},{7,1},{8,14},{9,15},{10,... | collective-permute-start | bytes 215048 | tf_op jit(solution)/shard_map/ppermute | solution.py:259
  8.5 7.4 %collective-permute-start.1 = (bf16[56,640]{1,0:T(8,128)(2,1)S(1)}, bf16[56,640]{1,0:T(8,128)(2,1)S(1)}, u32[]{:S(2)}, u32[]{:S(2)}) collective-permute-start(bf16[56,640]{1,0:T(8,128)(2,1)S(1)} %get-tuple-element.20), channel_id=1, source_target_pairs={{0,4},{1,5},{2,6},{3,7},{4,0},{5,1},{6,2},{7,3},{8,12},{9,13},{10,... | collective-permute-start | bytes 215048 | tf_op jit(solution)/shard_map/ppermute | solution.py:259
  8.5 7.4 %collective-permute-start.2 = (bf16[56,640]{1,0:T(8,128)(2,1)S(1)}, bf16[56,640]{1,0:T(8,128)(2,1)S(1)}, u32[]{:S(2)}, u32[]{:S(2)}) collective-permute-start(bf16[56,640]{1,0:T(8,128)(2,1)S(1)} %get-tuple-element.21), channel_id=1, source_target_pairs={{0,2},{1,3},{2,0},{3,1},{4,6},{5,7},{6,4},{7,5},{8,10},{9,11},{10,... | collective-permute-start | bytes 215048 | tf_op jit(solution)/shard_map/ppermute | solution.py:259
  9.1 9.5 %collective-permute-start.3 = (bf16[48,640]{1,0:T(8,128)(2,1)S(1)}, bf16[48,640]{1,0:T(8,128)(2,1)S(1)}, u32[]{:S(2)}, u32[]{:S(2)}) collective-permute-start(bf16[48,640]{1,0:T(8,128)(2,1)S(1)} %get-tuple-element.23), channel_id=1, source_target_pairs={{0,2},{1,3},{2,0},{3,1},{4,6},{5,7},{6,4},{7,5},{8,10},{9,11},{10,... | collective-permute-start | bytes 184328 | tf_op jit(solution)/shard_map/ppermute | solution.py:259
  10.5 9.0 %collective-permute-start.4 = (bf16[48,640]{1,0:T(8,128)(2,1)S(1)}, bf16[48,640]{1,0:T(8,128)(2,1)S(1)}, u32[]{:S(2)}, u32[]{:S(2)}) collective-permute-start(bf16[48,640]{1,0:T(8,128)(2,1)S(1)} %get-tuple-element.24), channel_id=1, source_target_pairs={{0,4},{1,5},{2,6},{3,7},{4,0},{5,1},{6,2},{7,3},{8,12},{9,13},{10,... | collective-permute-start | bytes 184328 | tf_op jit(solution)/shard_map/ppermute | solution.py:259
  13.4 6.1 %collective-permute-start.5 = (bf16[48,640]{1,0:T(8,128)(2,1)S(1)}, bf16[48,640]{1,0:T(8,128)(2,1)S(1)}, u32[]{:S(2)}, u32[]{:S(2)}) collective-permute-start(bf16[48,640]{1,0:T(8,128)(2,1)S(1)} %get-tuple-element.25), channel_id=1, source_target_pairs={{0,6},{1,7},{2,4},{3,5},{4,2},{5,3},{6,0},{7,1},{8,14},{9,15},{10,... | collective-permute-start | bytes 184328 | tf_op jit(solution)/shard_map/ppermute | solution.py:259
  15.9 4.7 %collective-permute-start.6 = (bf16[8,640]{1,0:T(8,128)(2,1)S(1)}, bf16[8,640]{1,0:T(8,128)(2,1)S(1)}, u32[]{:S(2)}, u32[]{:S(2)}) collective-permute-start(bf16[8,640]{1,0:T(8,128)(2,1)S(1)} %shard_map.65.refs_11_), channel_id=1, source_target_pairs={{0,24},{8,16},{16,8},{24,0},{1,25},{9,17},{17,9},{25,1},{2,26},{10... | collective-permute-start | bytes 30728 | tf_op jit(solution)/shard_map/ppermute | solution.py:259
  18.1 3.7 %collective-permute-start.7 = (bf16[8,640]{1,0:T(8,128)(2,1)S(1)}, bf16[8,640]{1,0:T(8,128)(2,1)S(1)}, u32[]{:S(2)}, u32[]{:S(2)}) collective-permute-start(bf16[8,640]{1,0:T(8,128)(2,1)S(1)} %shard_map.65.refs_11_), channel_id=1, source_target_pairs={{0,16},{8,24},{16,0},{24,8},{1,17},{9,25},{17,1},{25,9},{2,18},{10... | collective-permute-start | bytes 30728 | tf_op jit(solution)/shard_map/ppermute | solution.py:259
  18.6 3.7 %collective-permute-start.8 = (bf16[8,640]{1,0:T(8,128)(2,1)S(1)}, bf16[8,640]{1,0:T(8,128)(2,1)S(1)}, u32[]{:S(2)}, u32[]{:S(2)}) collective-permute-start(bf16[8,640]{1,0:T(8,128)(2,1)S(1)} %shard_map.65.refs_11_), channel_id=1, source_target_pairs={{0,8},{8,0},{16,24},{24,16},{1,9},{9,1},{17,25},{25,17},{2,10},{10... | collective-permute-start | bytes 30728 | tf_op jit(solution)/shard_map/ppermute | solution.py:259
  22.3 1.6 %collective-permute-start.9 = (bf16[224,640]{1,0:T(8,128)(2,1)S(1)}, bf16[224,640]{1,0:T(8,128)(2,1)S(1)}, u32[]{:S(2)}, u32[]{:S(2)}) collective-permute-start(bf16[224,640]{1,0:T(8,128)(2,1)S(1)} %shard_map.67), channel_id=1, source_target_pairs={{0,1},{1,0},{2,3},{3,2},{4,5},{5,4},{6,7},{7,6},{8,9},{9,8},{10,11... | collective-permute-start | bytes 860168 | tf_op jit(solution)/shard_map/ppermute | solution.py:259
  24.6 5.5 %collective-permute-start.10 = (bf16[96,384]{1,0:T(8,128)(2,1)S(1)}, bf16[96,384]{1,0:T(8,128)(2,1)S(1)}, u32[]{:S(2)}, u32[]{:S(2)}) collective-permute-start(bf16[96,384]{1,0:T(8,128)(2,1)S(1)} %get-tuple-element.29), channel_id=1, source_target_pairs={{0,24},{8,16},{16,8},{24,0},{1,25},{9,17},{17,9},{25,1},{2,26},{10... | collective-permute-start | bytes 221192 | tf_op jit(solution)/shard_map/ppermute | solution.py:259
  26.3 5.3 %collective-permute-start.11 = (bf16[96,384]{1,0:T(8,128)(2,1)S(1)}, bf16[96,384]{1,0:T(8,128)(2,1)S(1)}, u32[]{:S(2)}, u32[]{:S(2)}) collective-permute-start(bf16[96,384]{1,0:T(8,128)(2,1)S(1)} %get-tuple-element.30), channel_id=1, source_target_pairs={{0,16},{8,24},{16,0},{24,8},{1,17},{9,25},{17,1},{25,9},{2,18},{10... | collective-permute-start | bytes 221192 | tf_op jit(solution)/shard_map/ppermute | solution.py:259
  27.0 4.6 %collective-permute-start.12 = (bf16[96,384]{1,0:T(8,128)(2,1)S(1)}, bf16[96,384]{1,0:T(8,128)(2,1)S(1)}, u32[]{:S(2)}, u32[]{:S(2)}) collective-permute-start(bf16[96,384]{1,0:T(8,128)(2,1)S(1)} %get-tuple-element.28._), channel_id=1, source_target_pairs={{0,8},{8,0},{16,24},{24,16},{1,9},{9,1},{17,25},{25,17},{2,10},{10... | collective-permute-start | bytes 221192 | tf_op jit(solution)/shard_map/ppermute | solution.py:259
  28.8 0.7 %copy-start = (s32[1,3]{1,0:T(1,128)S(1)}, s32[1,3]{1,0:T(1,128)}, u32[]{:S(2)}) copy-start(s32[1,3]{1,0:T(1,128)} %partner.1) | copy-start | bytes 40
